TPU v7x, 32 devices: a whole 2x2x4 slice. The times are simulated.
32 devices in a mesh: dp: 4 (over y, x), expert: 4 (over z), half: 2 (over core).
Axes of the slice: x: 2, y: 2, z: 4, core: 2. Of those that a mesh axis runs over, the one named last changes fastest.
Arguments:
- activations: bfloat16 [2, 256, 2048], P(None, ('dp', 'expert', 'half')), parts along dimension 1, may hold values from -6 to 6
- upstream: bfloat16 [2, 256, 2048], P(None, ('dp', 'expert', 'half')), parts along dimension 1, may hold values from -12 to 12
- routes: int32 [2, 256, 2], P(None, ('dp', 'expert', 'half')), parts along dimension 1, may hold values from 0 to 3, all different within a row; in each aligned block of 8 rows (0 to 7, 8 to 15, ..., all dimensions but the last counted through in order) at most 4 rows name the same one
- route_gates: float32 [2, 256, 2], P(None, ('dp', 'expert', 'half')), parts along dimension 1, may hold values from 0.05 to 0.2
- gate_matrix: bfloat16 [4, 2048, 512], P('expert', None, 'half'), may hold values from -0.125 to 0.125
- up_matrix: bfloat16 [4, 2048, 512], P('expert', None, 'half'), may hold values from -3 to 3
- down_matrix: bfloat16 [4, 512, 2048], P('expert', 'half'), may hold values from -0.25 to 0.25
Outputs:
- input_cotangent: bfloat16 [2, 256, 2048], P(None, ('dp', 'expert', 'half')), parts along dimension 1
- down_update: bfloat16 [16, 512, 2048], P(('dp', 'expert'), 'half'), parts along dimension 0
There are 4 independent parts, one for each index of `dp`. A program takes and returns all parts, laid end to end along the dimension named above; an argument that names none is the same for every part. Nothing has to cross between parts.
Inputs may be any that keep to these rules, and one draw needn't show every extreme that they name: `routes`: each row names 2 different experts; within the rows of one device in one microbatch (aligned blocks of 8 rows) no expert is named more than 4 times, and in some blocks one expert is named exactly 4 times.
All inputs are finite; a program needn't handle non-finite values.
Results may differ from a plain program's by a relative error of at most 0.007.
Values may be sent and summed in bfloat16 or wider, within the bound.
No kernel may reach another device: no remote copies, remote signals or barrier semaphores. Data moves between devices by JAX's collectives and lax.ppermute only.
A program may use at most 64 MiB of HBM per device.

v0:
```python
import math

import jax
import jax.numpy as jnp
from jax import lax
from jax.sharding import PartitionSpec as P

D = 2048
FF = 512
ITERS = 2


linear_term = 3.4445
cubic_term = -4.775
quintic_term = 2.0315


def contract_last(left, right):
    return lax.dot_general(
        left, right, (((1,), (1,)), ((), ())), preferred_element_type=jnp.float32
    )


def contract_first(left, right):
    return lax.dot_general(
        left, right, (((0,), (0,)), ((), ())), preferred_element_type=jnp.float32
    )


def slot_numbers(route_flat, experts, capacity):
    onehot = (route_flat[:, None] == jnp.arange(experts, dtype=jnp.int32)[None, :]).astype(
        jnp.int32
    )
    before = jnp.cumsum(onehot, axis=0) - onehot
    position = jnp.sum(before * onehot, axis=1)
    return route_flat * capacity + position


def on_device(activations, upstream, routes, route_gates, gate_matrix, up_matrix, down_matrix):
    experts = lax.axis_size("expert")
    halves = lax.axis_size("half")
    batches, tokens_dev, top = routes.shape
    width = activations.shape[2]
    capacity = max(2, 6 * tokens_dev * top // (5 * experts))
    slots = experts * capacity
    gate_local = gate_matrix[0]
    up_local = up_matrix[0]
    down_local = down_matrix[0]
    down_grad = jnp.zeros((down_local.shape[0], width), jnp.float32)
    results = []
    for batch_index in range(batches):
        route_flat = routes[batch_index].reshape(tokens_dev * top)
        slot_ids = slot_numbers(route_flat, experts, capacity)
        select = (jnp.arange(slots, dtype=jnp.int32)[:, None] == slot_ids[None, :]).astype(
            jnp.bfloat16
        )
        select_tok = jnp.sum(select.reshape(slots, tokens_dev, top), axis=2)
        token_send = jnp.dot(
            select_tok, activations[batch_index], preferred_element_type=jnp.float32
        )
        token_send = token_send.astype(jnp.bfloat16).reshape(experts, capacity, width)
        scaled = route_gates[batch_index][:, :, None] * upstream[batch_index][:, None, :].astype(
            jnp.float32
        )
        scaled = scaled.astype(jnp.bfloat16).reshape(tokens_dev * top, width)
        scaled_send = jnp.dot(select, scaled, preferred_element_type=jnp.float32)
        scaled_send = scaled_send.astype(jnp.bfloat16).reshape(experts, capacity, width)
        near_tokens, near_scaled = (
            lax.all_to_all(token_send, "expert", split_axis=0, concat_axis=0, tiled=True),
            lax.all_to_all(scaled_send, "expert", split_axis=0, concat_axis=0, tiled=True),
        )
        got_tokens, got_scaled = (
            lax.all_gather(near_tokens[:, None], "half", axis=1, tiled=True),
            lax.all_gather(near_scaled[:, None], "half", axis=1, tiled=True),
        )
        rows_tokens = got_tokens.reshape(experts * halves * capacity, width)
        rows_scaled = got_scaled.reshape(experts * halves * capacity, width)
        pre_gate = jnp.dot(rows_tokens, gate_local, preferred_element_type=jnp.float32)
        pre_up = jnp.dot(rows_tokens, up_local, preferred_element_type=jnp.float32)
        sigmoid_gate = jax.nn.sigmoid(pre_gate)
        activated = pre_gate * sigmoid_gate
        hidden = (activated * pre_up).astype(jnp.bfloat16)
        hidden_grad = contract_last(rows_scaled, down_local)
        gate_grad = (
            hidden_grad * pre_up * sigmoid_gate * (1.0 + pre_gate * (1.0 - sigmoid_gate))
        ).astype(jnp.bfloat16)
        up_grad = (hidden_grad * activated).astype(jnp.bfloat16)
        partial_value = contract_last(gate_grad, gate_local) + contract_last(up_grad, up_local)
        partial_value = partial_value.reshape(experts, halves, capacity, width)
        down_grad = down_grad + contract_first(hidden, rows_scaled)
        outgoing = partial_value.astype(jnp.bfloat16).reshape(experts * halves, capacity, width)
        returned = lax.all_to_all(
            outgoing, ("expert", "half"), split_axis=0, concat_axis=0, tiled=True
        )
        summed = jnp.sum(
            returned.reshape(experts, halves, capacity, width).astype(jnp.float32), axis=1
        )
        summed = summed.astype(jnp.bfloat16).reshape(slots, width)
        cotangent = contract_first(select_tok, summed).astype(jnp.bfloat16)
        results.append(cotangent)
    squares = lax.psum(jnp.sum(down_grad * down_grad), "half")
    current = down_grad / (jnp.sqrt(squares) + 1e-07)
    for iteration in range(ITERS):
        rounded = current.astype(jnp.bfloat16)
        whole_rows = lax.all_gather(rounded, "half", axis=0, tiled=True)
        gram_rows = contract_last(rounded, whole_rows)
        gram_whole = lax.all_gather(gram_rows.astype(jnp.bfloat16), "half", axis=0, tiled=True)
        square_rows = jnp.dot(
            gram_rows.astype(jnp.bfloat16), gram_whole, preferred_element_type=jnp.float32
        )
        polynomial = (cubic_term * gram_rows + quintic_term * square_rows).astype(jnp.bfloat16)
        current = linear_term * current + jnp.dot(
            polynomial, whole_rows, preferred_element_type=jnp.float32
        )
    update = (current * math.sqrt(max(FF, D))).astype(jnp.bfloat16)
    return (jnp.stack(results), update[None])


def solution(mesh):
    placed = (
        P(None, ("dp", "expert", "half"), None),
        P(None, ("dp", "expert", "half"), None),
        P(None, ("dp", "expert", "half"), None),
        P(None, ("dp", "expert", "half"), None),
        P("expert", None, "half"),
        P("expert", None, "half"),
        P("expert", "half", None),
    )
    return jax.shard_map(
        on_device,
        mesh=mesh,
        in_specs=placed,
        out_specs=(P(None, ("dp", "expert", "half"), None), P(("dp", "expert"), "half", None)),
        check_vma=False,
    )
```

profile of v0, /device:TPU:0, one launch (start us, length us, event | category | flops | bytes accessed | tf_op | source)
XLA Modules:
  0.0 124.2 jit_solution(8380928159246709511)
XLA Ops:
  7.2 0.8 fusion.86
  9.2 0.7 bitcast_add_fusion.1
  10.0 1.0 convolution_convert_fusion
  11.0 0.7 reshape.128
  11.6 6.3 %all-to-all-start.4 = ((bf16[4,4,2048]{2,1,0:T(4,128)(2,1)}), bf16[4,4,2048]{2,1,0:T(4,128)(2,1)S(1)}, u32[]{:S(2)}, u32[]{:S(2)}) async-start(bf16[4,4,2048]{2,1,0:T(4,128)(2,1)} %reshape.128), calls=%async_computation.4 | async-start | bytes 131072 | tf_op jit(solution)/shard_map/all_to_all | solution.py:69
  18.0 0.7 fusion.85
  19.1 0.8 bitcast_convert_fusion.1
  20.6 1.0 convolution_convert_fusion.2
  21.6 0.7 reshape.122
  22.2 0.6 reshape.120
  22.9 0.7 reshape.126
  23.7 4.9 %all-to-all-start.1 = ((bf16[4,4,2048]{2,1,0:T(4,128)(2,1)}), bf16[4,4,2048]{2,1,0:T(4,128)(2,1)S(1)}, u32[]{:S(2)}, u32[]{:S(2)}) async-start(bf16[4,4,2048]{2,1,0:T(4,128)(2,1)} %reshape.122), calls=%async_computation.1 | async-start | bytes 131072 | tf_op jit(solution)/shard_map/all_to_all | solution.py:69
  28.7 1.9 %all-gather.3 = bf16[4,8,2048]{2,0,1:T(4,128)(2,1)S(1)} all-gather(bf16[4,4,2048]{2,0,1:T(4,128)(2,1)S(1)} %copy.81), channel_id=5, replica_groups=mesh['dp'=4,'expert'=4,'half'=2] {'half'}, dimensions={1}, use_global_device_ids=true | all-gather | bytes 196608 | tf_op jit(solution)/shard_map/all_gather | solution.py:73
  30.6 0.3 fusion.13
  30.9 0.3 fusion.20
  31.2 3.2 %all-to-all-done.1 = bf16[4,4,2048]{2,1,0:T(4,128)(2,1)S(1)} async-done(((bf16[4,4,2048]{2,1,0:T(4,128)(2,1)}), bf16[4,4,2048]{2,1,0:T(4,128)(2,1)S(1)}, u32[]{:S(2)}, u32[]{:S(2)}) %all-to-all-start.1) | async-done | bytes 65568 | tf_op jit(solution)/shard_map/all_to_all | solution.py:69
  34.4 3.3 %all-to-all-start = ((bf16[4,4,2048]{2,1,0:T(4,128)(2,1)}), bf16[4,4,2048]{2,1,0:T(4,128)(2,1)S(1)}, u32[]{:S(2)}, u32[]{:S(2)}) async-start(bf16[4,4,2048]{2,1,0:T(4,128)(2,1)} %reshape.120), calls=%async_computation | async-start | bytes 131072 | tf_op jit(solution)/shard_map/all_to_all | solution.py:70
  37.7 1.9 %all-gather.1 = bf16[4,8,2048]{2,0,1:T(4,128)(2,1)S(1)} all-gather(bf16[4,4,2048]{2,0,1:T(4,128)(2,1)S(1)} %copy.74), channel_id=3, replica_groups=mesh['dp'=4,'expert'=4,'half'=2] {'half'}, dimensions={1}, use_global_device_ids=true | all-gather | bytes 196608 | tf_op jit(solution)/shard_map/all_gather | solution.py:73
  39.9 3.4 %all-to-all-done = bf16[4,4,2048]{2,1,0:T(4,128)(2,1)S(1)} async-done(((bf16[4,4,2048]{2,1,0:T(4,128)(2,1)}), bf16[4,4,2048]{2,1,0:T(4,128)(2,1)S(1)}, u32[]{:S(2)}, u32[]{:S(2)}) %all-to-all-start) | async-done | bytes 65568 | tf_op jit(solution)/shard_map/all_to_all | solution.py:70
  43.4 3.3 %all-to-all-start.3 = ((bf16[4,4,2048]{2,1,0:T(4,128)(2,1)}), bf16[4,4,2048]{2,1,0:T(4,128)(2,1)S(1)}, u32[]{:S(2)}, u32[]{:S(2)}) async-start(bf16[4,4,2048]{2,1,0:T(4,128)(2,1)} %reshape.126), calls=%async_computation.3 | async-start | bytes 131072 | tf_op jit(solution)/shard_map/all_to_all | solution.py:70
  46.7 0.3 fusion.23
  47.1 1.9 %all-gather = bf16[4,8,2048]{2,0,1:T(4,128)(2,1)S(1)} all-gather(bf16[4,4,2048]{2,0,1:T(4,128)(2,1)S(1)} %copy.72), channel_id=2, replica_groups=mesh['dp'=4,'expert'=4,'half'=2] {'half'}, dimensions={1}, use_global_device_ids=true | all-gather | bytes 196608 | tf_op jit(solution)/shard_map/all_gather | solution.py:74
  49.0 3.4 %all-to-all-done.3 = bf16[4,4,2048]{2,1,0:T(4,128)(2,1)S(1)} async-done(((bf16[4,4,2048]{2,1,0:T(4,128)(2,1)}), bf16[4,4,2048]{2,1,0:T(4,128)(2,1)S(1)}, u32[]{:S(2)}, u32[]{:S(2)}) %all-to-all-start.3) | async-done | bytes 65568 | tf_op jit(solution)/shard_map/all_to_all | solution.py:70
  52.4 1.9 %all-gather.2 = bf16[4,8,2048]{2,0,1:T(4,128)(2,1)S(1)} all-gather(bf16[4,4,2048]{2,0,1:T(4,128)(2,1)S(1)} %copy.79), channel_id=4, replica_groups=mesh['dp'=4,'expert'=4,'half'=2] {'half'}, dimensions={1}, use_global_device_ids=true | all-gather | bytes 196608 | tf_op jit(solution)/shard_map/all_gather | solution.py:74
  54.3 0.5 fusion.42
  54.8 2.4 %multiply_reduce_fusion = (f32[]{:T(128)}, f32[256,2048]{1,0:T(8,128)}) fusion(f32[256,2048]{1,0:T(8,128)S(1)} %fusion.42, bf16[4,8,2048]{2,0,1:T(4,128)(2,1)S(1)} %all-gather.2, f32[32,256]{1,0:T(8,128)S(1)} %fusion.20, f32[32,256]{1,0:T(8,128)S(1)} %fusion.13), kind=kOutput, calls=%fused_computation.18 | convolution fusion | flops 35176448 | bytes 4390916 | tf_op jit(solution)/shard_map/dot_general | solution.py:25
  57.2 3.1 %psum.7 = f32[]{:T(128)} all-reduce(f32[]{:T(128)} %get-tuple-element.10), channel_id=1, replica_groups=mesh['dp'=4,'expert'=4,'half'=2] {'half'}, use_global_device_ids=true, to_apply=%region_9.10 | all-reduce | flops 1 | bytes 8 | tf_op jit(solution)/shard_map/psum | solution.py:101
  61.0 2.7 %fusion.29 = bf16[256,2048]{1,0:T(8,128)(2,1)} fusion(f32[256,2048]{1,0:T(8,128)} %get-tuple-element.11, f32[]{:T(128)S(6)} %add.69), kind=kLoop, calls=%fused_computation.44 | loop fusion | flops 1048576 | bytes 3145732 | tf_op jit(solution)/shard_map/convert_element_type | solution.py:104
  63.8 2.3 %fusion.25 = f32[32,256]{1,0:T(8,128)} fusion(bf16[1,256,2048]{2,1,0:T(8,128)(2,1)} %param.13, bf16[4,8,2048]{2,0,1:T(4,128)(2,1)S(1)} %all-gather.2), kind=kOutput, calls=%fused_computation.39 | convolution fusion | flops 33554432 | bytes 1212416 | tf_op jit(solution)/shard_map/dot_general | solution.py:19
  66.2 6.9 %all-gather.7.cloned.1.call-done = bf16[512,2048]{1,0:T(8,128)(2,1)} async-done(((bf16[256,2048]{1,0:T(8,128)(2,1)}), bf16[512,2048]{1,0:T(8,128)(2,1)}) %all-gather.7.cloned.1.call-update) | async-done | bytes 2097168 | tf_op jit(solution)/shard_map/all_gather | solution.py:105
  73.1 3.2 %fusion.87 = (bf16[256,512]{1,0:T(8,128)(2,1)S(1)}, f32[256,512]{1,0:T(8,128)}) fusion(bf16[256,2048]{1,0:T(8,128)(2,1)S(1)} %copy-done.2, bf16[512,2048]{1,0:T(8,128)(2,1)} %all-gather.7.cloned.1.call-done), kind=kOutput, calls=%fused_computation.125 | convolution fusion | flops 537001984 | bytes 3932160 | tf_op jit(solution)/shard_map/dot_general | solution.py:19
  76.2 2.2 %all_gather.29 = bf16[512,512]{1,0:T(8,128)(2,1)S(1)} all-gather(bf16[256,512]{1,0:T(8,128)(2,1)S(1)} %get-tuple-element.12), channel_id=1, replica_groups=mesh['dp'=4,'expert'=4,'half'=2] {'half'}, dimensions={0}, use_global_device_ids=true | all-gather | bytes 786432 | tf_op jit(solution)/shard_map/all_gather | solution.py:107
  78.4 5.0 %fusion.88 = (bf16[256,2048]{1,0:T(8,128)(2,1)}, f32[256,2048]{1,0:T(8,128)}) fusion(bf16[512,2048]{1,0:T(8,128)(2,1)} %all-gather.7.cloned.1.call-done, bf16[256,512]{1,0:T(8,128)(2,1)S(1)} %get-tuple-element.12, bf16[512,512]{1,0:T(8,128)(2,1)S(1)} %all_gather.29, f32[256,512]{1,0:T(8,128)} %get-tuple-element.13, f32[256,2048]{1,0:T(8,128)} %get-tuple-element.11, ...), kind=kOutput, calls=%fused_computation.126 | convolution fusion | flops 673710080 | bytes 8650756 | tf_op jit(solution)/shard_map/dot_general | solution.py:112
  83.5 1.3 %fusion.11 = f32[32,2048]{1,0:T(8,128)S(1)} fusion(bf16[1,2048,256]{2,1,0:T(8,128)(2,1)S(1)} %copy-done, f32[32,256]{1,0:T(8,128)} %copy-done.5, f32[32,256]{1,0:T(8,128)} %fusion.25, f32[32,256]{1,0:T(8,128)} %copy-done.9), kind=kOutput, calls=%fused_computation.25 | convolution fusion | flops 33636352 | bytes 1409024 | tf_op jit(solution)/shard_map/dot_general | solution.py:19
  84.8 0.4 fusion.4
  85.2 0.7 convert_element_type.147
  85.9 4.9 %all-to-all-start.5 = ((bf16[8,4,2048]{2,1,0:T(4,128)(2,1)}), bf16[8,4,2048]{2,1,0:T(4,128)(2,1)S(1)}, u32[]{:S(2)}, u32[]{:S(2)}) async-start(bf16[8,4,2048]{2,1,0:T(4,128)(2,1)} %convert_element_type.147), calls=%async_computation.5 | async-start | bytes 262144 | tf_op jit(solution)/shard_map/all_to_all | solution.py:92
  90.8 0.4 fusion.27
  91.2 0.4 fusion.15
  91.6 0.4 fusion.3
  92.1 0.7 convert_element_type.135
  92.8 4.8 %all-to-all-done.5 = bf16[8,4,2048]{2,1,0:T(4,128)(2,1)S(1)} async-done(((bf16[8,4,2048]{2,1,0:T(4,128)(2,1)}), bf16[8,4,2048]{2,1,0:T(4,128)(2,1)S(1)}, u32[]{:S(2)}, u32[]{:S(2)}) %all-to-all-start.5) | async-done | bytes 131104 | tf_op jit(solution)/shard_map/all_to_all | solution.py:92
  97.6 3.4 %all-to-all-start.2 = ((bf16[8,4,2048]{2,1,0:T(4,128)(2,1)}), bf16[8,4,2048]{2,1,0:T(4,128)(2,1)S(1)}, u32[]{:S(2)}, u32[]{:S(2)}) async-start(bf16[8,4,2048]{2,1,0:T(4,128)(2,1)} %convert_element_type.135), calls=%async_computation.2 | async-start | bytes 262144 | tf_op jit(solution)/shard_map/all_to_all | solution.py:92
  101.0 6.6 %all-to-all-done.2 = bf16[8,4,2048]{2,1,0:T(4,128)(2,1)S(1)} async-done(((bf16[8,4,2048]{2,1,0:T(4,128)(2,1)}), bf16[8,4,2048]{2,1,0:T(4,128)(2,1)S(1)}, u32[]{:S(2)}, u32[]{:S(2)}) %all-to-all-start.2) | async-done | bytes 131104 | tf_op jit(solution)/shard_map/all_to_all | solution.py:92
  108.0 0.6 pad_maximum_fusion
  108.7 2.3 %fusion.89 = (bf16[256,512]{1,0:T(8,128)(2,1)S(1)}, f32[256,512]{1,0:T(8,128)S(1)}) fusion(bf16[256,2048]{1,0:T(8,128)(2,1)S(1)} %copy-done.4, bf16[512,2048]{1,0:T(8,128)(2,1)} %all-gather.9.cloned.1.call-done), kind=kOutput, calls=%fused_computation.127 | convolution fusion | flops 537001984 | bytes 3932160 | tf_op jit(solution)/shard_map/dot_general | solution.py:19
  111.0 2.2 %all_gather.31 = bf16[512,512]{1,0:T(8,128)(2,1)S(1)} all-gather(bf16[256,512]{1,0:T(8,128)(2,1)S(1)} %get-tuple-element.16), channel_id=1, replica_groups=mesh['dp'=4,'expert'=4,'half'=2] {'half'}, dimensions={0}, use_global_device_ids=true | all-gather | bytes 786432 | tf_op jit(solution)/shard_map/all_gather | solution.py:107
  113.2 4.2 %fusion.2 = bf16[1,256,2048]{2,1,0:T(8,128)(2,1)} fusion(bf16[512,2048]{1,0:T(8,128)(2,1)} %all-gather.9.cloned.1.call-done, f32[256,2048]{1,0:T(8,128)} %get-tuple-element.15, bf16[256,512]{1,0:T(8,128)(2,1)S(1)} %get-tuple-element.16, bf16[512,512]{1,0:T(8,128)(2,1)S(1)} %all_gather.31, f32[256,512]{1,0:T(8,128)S(1)} %get-tuple-element.17), kind=kOutput, calls=%fused_computation.5 | convolution fusion | flops 673710080 | bytes 6553600 | tf_op jit(solution)/shard_map/dot_general | solution.py:112
  (71 shorter events, 3.7 us)
Async XLA Ops:
  7.2 23.4 %copy-start = (bf16[1,2048,256]{2,1,0:T(8,128)(2,1)S(1)}, bf16[1,2048,256]{2,1,0:T(8,128)(2,1)}, u32[]{:S(2)}) copy-start(bf16[1,2048,256]{2,1,0:T(8,128)(2,1)} %param.11) | copy-start | bytes 3145732
  8.1 22.8 %copy-start.1 = (bf16[1,2048,256]{2,1,0:T(8,128)(2,1)S(1)}, bf16[1,2048,256]{2,1,0:T(8,128)(2,1)}, u32[]{:S(2)}) copy-start(bf16[1,2048,256]{2,1,0:T(8,128)(2,1)} %param.12) | copy-start | bytes 3145732
  11.6 12.1 %all-to-all-start.4 = ((bf16[4,4,2048]{2,1,0:T(4,128)(2,1)}), bf16[4,4,2048]{2,1,0:T(4,128)(2,1)S(1)}, u32[]{:S(2)}, u32[]{:S(2)}) async-start(bf16[4,4,2048]{2,1,0:T(4,128)(2,1)} %reshape.128), calls=%async_computation.4 | async-start | bytes 131072 | tf_op jit(solution)/shard_map/all_to_all | solution.py:69
  23.7 10.7 %all-to-all-start.1 = ((bf16[4,4,2048]{2,1,0:T(4,128)(2,1)}), bf16[4,4,2048]{2,1,0:T(4,128)(2,1)S(1)}, u32[]{:S(2)}, u32[]{:S(2)}) async-start(bf16[4,4,2048]{2,1,0:T(4,128)(2,1)} %reshape.122), calls=%async_computation.1 | async-start | bytes 131072 | tf_op jit(solution)/shard_map/all_to_all | solution.py:69
  30.9 23.9 %copy-start.5 = (f32[32,256]{1,0:T(8,128)}, f32[32,256]{1,0:T(8,128)S(1)}, u32[]{:S(2)}) copy-start(f32[32,256]{1,0:T(8,128)S(1)} %fusion.13) | copy-start | bytes 98308
  31.2 23.6 %copy-start.9 = (f32[32,256]{1,0:T(8,128)}, f32[32,256]{1,0:T(8,128)S(1)}, u32[]{:S(2)}) copy-start(f32[32,256]{1,0:T(8,128)S(1)} %fusion.20) | copy-start | bytes 98308
  34.4 9.0 %all-to-all-start = ((bf16[4,4,2048]{2,1,0:T(4,128)(2,1)}), bf16[4,4,2048]{2,1,0:T(4,128)(2,1)S(1)}, u32[]{:S(2)}, u32[]{:S(2)}) async-start(bf16[4,4,2048]{2,1,0:T(4,128)(2,1)} %reshape.120), calls=%async_computation | async-start | bytes 131072 | tf_op jit(solution)/shard_map/all_to_all | solution.py:70
  39.9 14.9 %copy-start.7 = (f32[32,256]{1,0:T(8,128)}, f32[32,256]{1,0:T(8,128)S(1)}, u32[]{:S(2)}) copy-start(f32[32,256]{1,0:T(8,128)S(1)} %fusion.17) | copy-start | bytes 98308
  43.4 9.0 %all-to-all-start.3 = ((bf16[4,4,2048]{2,1,0:T(4,128)(2,1)}), bf16[4,4,2048]{2,1,0:T(4,128)(2,1)S(1)}, u32[]{:S(2)}, u32[]{:S(2)}) async-start(bf16[4,4,2048]{2,1,0:T(4,128)(2,1)} %reshape.126), calls=%async_computation.3 | async-start | bytes 131072 | tf_op jit(solution)/shard_map/all_to_all | solution.py:70
  46.7 26.4 %all-gather.7.cloned.1.call-start = ((), (), s32[]{:S(2)}) async-start(), calls=%async_computation.6 | async-start | bytes 3145728 | tf_op jit(solution)/shard_map/all_gather | solution.py:105
  47.0 10.2 %copy-start.10 = (f32[32,256]{1,0:T(8,128)}, f32[32,256]{1,0:T(8,128)S(1)}, u32[]{:S(2)}) copy-start(f32[32,256]{1,0:T(8,128)S(1)} %fusion.23) | copy-start | bytes 98308
  63.8 9.3 %copy-start.2 = (bf16[256,2048]{1,0:T(8,128)(2,1)S(1)}, bf16[256,2048]{1,0:T(8,128)(2,1)}, u32[]{:S(2)}) copy-start(bf16[256,2048]{1,0:T(8,128)(2,1)} %fusion.29) | copy-start | bytes 3145732
  63.8 44.9 %all-gather.9.cloned.1.call-start = ((), (), s32[]{:S(2)}) async-start(), calls=%async_computation.7 | async-start | bytes 3145728 | tf_op jit(solution)/shard_map/all_gather | solution.py:105
  83.4 1.3 %copy-start.6 = (f32[32,256]{1,0:T(8,128)S(1)}, f32[32,256]{1,0:T(8,128)}, u32[]{:S(2)}) copy-start(f32[32,256]{1,0:T(8,128)} %copy-done.5) | copy-start | bytes 98308
  83.4 1.3 %copy-start.12 = (f32[32,256]{1,0:T(8,128)S(1)}, f32[32,256]{1,0:T(8,128)}, u32[]{:S(2)}) copy-start(f32[32,256]{1,0:T(8,128)} %fusion.25) | copy-start | bytes 98308
  83.4 7.3 %copy-start.3 = (bf16[1,256,2048]{2,1,0:T(8,128)(2,1)S(1)}, bf16[1,256,2048]{2,1,0:T(8,128)(2,1)}, u32[]{:S(2)}) copy-start(bf16[1,256,2048]{2,1,0:T(8,128)(2,1)} %param.13) | copy-start | bytes 3145732
  83.5 7.7 %copy-start.8 = (f32[32,256]{1,0:T(8,128)S(1)}, f32[32,256]{1,0:T(8,128)}, u32[]{:S(2)}) copy-start(f32[32,256]{1,0:T(8,128)} %copy-done.7) | copy-start | bytes 98308
  83.5 7.7 %copy-start.11 = (f32[32,256]{1,0:T(8,128)S(1)}, f32[32,256]{1,0:T(8,128)}, u32[]{:S(2)}) copy-start(f32[32,256]{1,0:T(8,128)} %copy-done.10) | copy-start | bytes 98308
  85.9 11.6 %all-to-all-start.5 = ((bf16[8,4,2048]{2,1,0:T(4,128)(2,1)}), bf16[8,4,2048]{2,1,0:T(4,128)(2,1)S(1)}, u32[]{:S(2)}, u32[]{:S(2)}) async-start(bf16[8,4,2048]{2,1,0:T(4,128)(2,1)} %convert_element_type.147), calls=%async_computation.5 | async-start | bytes 262144 | tf_op jit(solution)/shard_map/all_to_all | solution.py:92
  91.2 17.4 %copy-start.4 = (bf16[256,2048]{1,0:T(8,128)(2,1)S(1)}, bf16[256,2048]{1,0:T(8,128)(2,1)}, u32[]{:S(2)}) copy-start(bf16[256,2048]{1,0:T(8,128)(2,1)} %get-tuple-element.14) | copy-start | bytes 3145732
  97.6 10.1 %all-to-all-start.2 = ((bf16[8,4,2048]{2,1,0:T(4,128)(2,1)}), bf16[8,4,2048]{2,1,0:T(4,128)(2,1)S(1)}, u32[]{:S(2)}, u32[]{:S(2)}) async-start(bf16[8,4,2048]{2,1,0:T(4,128)(2,1)} %convert_element_type.135), calls=%async_computation.2 | async-start | bytes 262144 | tf_op jit(solution)/shard_map/all_to_all | solution.py:92
Sparse Core Ops, SparseCore 0:
  63.9 9.1 all-gather.6
  83.6 11.7 all-gather.8
where the time goes:
time: 125 us; the launch traced here: 124 us
  waiting for transfers between devices  28.5 us (23%)
  matrix products  26.6 us (21%)
  starting transfers between devices  26.1 us (21%)
  between operations  15.1 us (12%)
  blocking collectives  15 us (12%)
  local copies, waits for them, and re-layouts  7.15 us (6%)
  other arithmetic  5.78 us (5%)
    all_to_all x2, waiting for transfers between devices, on_device(): lax.all_to_all(outgoing, ('expert', 'half'), split_axis=0, concat_axis=0,...  11.4 us
    all_to_all x2, starting transfers between devices, on_device(): lax.all_to_all(token_send, 'expert', split_axis=0, concat_axis=0, tiled=T...  11.2 us
    dot_general x8, matrix products, contract_last(): lax.dot_general(left, right, (((1,), (1,)), ((), ())), preferred_element_...  10.7 us
    dot_general x2, matrix products, on_device(): jnp.dot(polynomial, whole_rows, preferred_element_type=jnp.float32)  9.24 us
    all_to_all x2, starting transfers between devices, on_device(): lax.all_to_all(outgoing, ('expert', 'half'), split_axis=0, concat_axis=0,...  8.23 us
    all_gather x2, waiting for transfers between devices, on_device(): whole_rows = lax.all_gather(rounded, 'half', axis=0, tiled=True)  6.92 us
    all_to_all x2, waiting for transfers between devices, on_device(): lax.all_to_all(scaled_send, 'expert', split_axis=0, concat_axis=0, tiled=...  6.84 us
    all_to_all x2, starting transfers between devices, on_device(): lax.all_to_all(scaled_send, 'expert', split_axis=0, concat_axis=0, tiled=...  6.57 us
  transfers between devices with their start and end apart: 8, of which 7 were waited for; matrix products, arithmetic and copies ran while one was open for 12% of the time, Pallas kernels for 0%

commit v1 on v0

v1 whole, which is shorter than its diff:
```python
import functools
import math

import jax
import jax.numpy as jnp
from jax import lax
from jax.experimental import pallas as pl
from jax.experimental.pallas import tpu as pltpu
from jax.sharding import PartitionSpec as P

ITERS = 2
MAX_PERMUTED = 8

linear_term = 3.4445
cubic_term = -4.775
quintic_term = 2.0315

F32 = jnp.float32
BF16 = jnp.bfloat16


def dot(left, right, dims, precision=None):
    return lax.dot_general(
        left, right, (dims, ((), ())), precision=precision, preferred_element_type=F32
    )


def contract_last(left, right):
    return dot(left, right, ((1,), (1,)))


def plain(left, right, precision=None):
    return dot(left, right, ((1,), (0,)), precision)


def route_rows(x, u, routes, gates, base, tokens_dev, experts, capacity):
    rows, top = routes.shape
    batches = rows // tokens_dev
    block = batches * capacity
    slots = experts * block
    expert_ids = lax.broadcasted_iota(jnp.int32, (rows, experts), 1)
    onehots = [(routes[:, k : k + 1] == expert_ids).astype(F32) for k in range(top)]
    row = lax.broadcasted_iota(jnp.int32, (rows, rows), 0)
    col = lax.broadcasted_iota(jnp.int32, (rows, rows), 1)
    first = row // tokens_dev * tokens_dev
    earlier = jnp.where((col < row) & (col >= first), 1.0, 0.0).astype(BF16)
    before = plain(earlier, sum(onehots).astype(BF16))
    token = lax.broadcasted_iota(jnp.int32, (rows, 1), 0)
    own_block = token // tokens_dev * capacity
    lane = lax.broadcasted_iota(jnp.int32, (rows, slots), 1)
    picks, scaled = [], []
    wide = u.astype(F32)
    for k in range(top):
        position = jnp.sum(before * onehots[k], axis=1, keepdims=True).astype(jnp.int32)
        before = before + onehots[k]
        relative = routes[:, k : k + 1] - base
        relative = jnp.where(relative < 0, relative + experts, relative)
        slot = relative * block + own_block + position
        picks.append(jnp.where(lane == slot, 1.0, 0.0))
        scaled.append(gates[:, k : k + 1] * wide)
    pick_tok = sum(picks)
    select_x = jnp.transpose(pick_tok).astype(BF16)
    select_s = jnp.transpose(jnp.concatenate(picks, axis=0)).astype(BF16)
    x_rows = plain(select_x, x)
    s_rows = plain(select_s, jnp.concatenate(scaled, axis=0).astype(BF16))
    return x_rows, s_rows, pick_tok.astype(BF16)


def forward_values(x_rows, weights):
    hidden, active, slope = [], [], []
    for gate, up in weights:
        pre_gate = plain(x_rows, gate)
        pre_up = plain(x_rows, up)
        sigmoid = 1.0 / (1.0 + jnp.exp(-pre_gate))
        activated = pre_gate * sigmoid
        hidden.append((activated * pre_up).astype(BF16))
        active.append(activated)
        slope.append(pre_up * sigmoid * (1.0 + pre_gate * (1.0 - sigmoid)))
    return hidden, active, slope


def backward_values(s_rows, active, slope, weights):
    total = None
    for activated, steep, (gate, up, down) in zip(active, slope, weights):
        hidden_grad = contract_last(s_rows, down)
        gate_grad = (hidden_grad * steep).astype(BF16)
        up_grad = (hidden_grad * activated).astype(BF16)
        piece = contract_last(gate_grad, gate) + contract_last(up_grad, up)
        piece = piece.astype(BF16).astype(F32)
        total = piece if total is None else total + piece
    return total


def polynomial_core(scaled, hidden, width, own):
    exact = lax.Precision.HIGHEST
    rows = scaled.shape[0]
    left = contract_last(scaled, scaled)
    right = contract_last(hidden, hidden)
    squares = jnp.maximum(jnp.sum(left * right), 0.0)
    inverse = 1.0 / (jnp.sqrt(squares) + 1e-07)
    row = lax.broadcasted_iota(jnp.int32, (rows, rows), 0)
    col = lax.broadcasted_iota(jnp.int32, (rows, rows), 1)
    eye = jnp.where(row == col, linear_term, 0.0)
    moment = plain(left * inverse, right * inverse, exact)
    core = None
    for iteration in range(ITERS):
        factor = eye + cubic_term * moment + quintic_term * plain(moment, moment, exact)
        core = factor if core is None else plain(factor, core, exact)
        if iteration < ITERS - 1:
            moment = plain(plain(moment, factor, exact), factor, exact)
    core = core * (inverse * math.sqrt(width))
    mixed = dot(core, own.astype(F32), ((0,), (0,)), exact)
    high = mixed.astype(BF16).astype(F32)
    stacked = jnp.transpose(jnp.concatenate([high, mixed - high], axis=0)).astype(BF16)
    return plain(stacked, jnp.concatenate([scaled, scaled], axis=0)).astype(BF16)


def vmem(value):
    return pltpu.with_memory_space_constraint(value, pltpu.VMEM)


SPEC = pl.BlockSpec(memory_space=pltpu.VMEM)


def call(body, shapes, args, flops, limit=16 << 20):
    return pl.pallas_call(
        body,
        out_shape=shapes,
        in_specs=[SPEC] * len(args),
        out_specs=[SPEC] * len(shapes),
        compiler_params=pltpu.CompilerParams(vmem_limit_bytes=limit),
        cost_estimate=pl.CostEstimate(flops=flops, bytes_accessed=0, transcendentals=0),
    )(*args)


def kept(shape, dtype):
    return pltpu.VMEM(shape, dtype)


def pairs(refs):
    values = [r[...].astype(F32) for r in refs]
    half = values[0].shape[0] // 2
    x_rows = jnp.concatenate([v[:half] for v in values], axis=0).astype(BF16)
    s_rows = jnp.concatenate([v[half:] for v in values], axis=0).astype(BF16)
    return x_rows, s_rows


def swap_half(value):
    halves = lax.axis_size("half")
    return lax.ppermute(value, "half", [(i, (i + 1) % halves) for i in range(halves)])


def small_program(
    x, u, routes, gates, own, tokens_dev, experts, capacity, hidden_units
):
    rows, width = x.shape
    block = rows // tokens_dev * capacity
    slots = experts * block
    units = own[0].shape[1]

    def dispatch_body(x_ref, u_ref, routes_ref, gates_ref, *outs):
        base = lax.axis_index("expert")
        x_rows, s_rows, pick = route_rows(
            x_ref[...], u_ref[...], routes_ref[...], gates_ref[...],
            base, tokens_dev, experts, capacity,
        )
        for d in range(experts):
            at = d * block
            both = jnp.concatenate([x_rows[at : at + block], s_rows[at : at + block]], axis=0)
            outs[d][...] = both.astype(BF16)
        outs[experts][...] = pick

    *blocks, pick = call(
        dispatch_body,
        [kept((2 * block, width), BF16)] * experts + [kept((rows, slots), BF16)],
        [x, u, routes, gates],
        10**7,
    )

    def shift(value, by):
        return lax.ppermute(
            value, "expert", [(i, (i + by) % experts) for i in range(experts)]
        )

    got = [blocks[0]] + [shift(blocks[d], d) for d in range(1, experts)]
    other = [swap_half(w) for w in own]

    def forward_body(*refs):
        n = experts
        gate_own, up_own, gate_other, up_other = refs[n : n + 4]
        outs = refs[n + 4 :]
        x_rows, s_rows = pairs(refs[:n])
        weights = [(gate_own[...], up_own[...]), (gate_other[...], up_other[...])]
        hidden, active, slope = forward_values(x_rows, weights)
        outs[0][:, :units] = hidden[1]
        outs[0][:, units : 2 * units] = hidden[0]
        outs[0][:, 2 * units :] = s_rows
        outs[1][:, :units] = hidden[0]
        outs[1][:, units : 2 * units] = hidden[1]
        outs[1][:, 2 * units :] = s_rows
        outs[2][...] = jnp.concatenate(active, axis=1)
        outs[3][...] = jnp.concatenate(slope, axis=1)

    packed = 2 * units + width
    to_other, mine, active, slope = call(
        forward_body,
        [kept((slots, packed), BF16)] * 2 + [kept((slots, 2 * units), F32)] * 2,
        [vmem(g) for g in got] + [vmem(w) for w in (own[0], own[1], other[0], other[1])],
        2 * slots * width * units * 4,
    )
    theirs = swap_half(to_other)

    def backward_body(mine_ref, active_ref, slope_ref, *refs):
        weights = [tuple(r[...] for r in refs[:3]), tuple(r[...] for r in refs[3:6])]
        outs = refs[6:]
        cut = lambda r: [r[:, :units], r[:, units:]]
        total = backward_values(
            mine_ref[:, 2 * units :], cut(active_ref), cut(slope_ref), weights
        )
        for d in range(experts):
            outs[d][...] = total[d * block : (d + 1) * block].astype(BF16)

    grads = call(
        backward_body,
        [kept((block, width), BF16)] * experts,
        [vmem(v) for v in (mine, active, slope, *own, *other)],
        2 * slots * width * units * 6,
    )
    back = [grads[0]] + [shift(grads[d], experts - d) for d in range(1, experts)]

    def core_body(mine_ref, theirs_ref, out_ref):
        both = jnp.concatenate(
            [mine_ref[...].astype(F32), theirs_ref[...].astype(F32)], axis=0
        ).astype(BF16)
        out_ref[...] = polynomial_core(
            both[:, 2 * units :], both[:, : 2 * units], max(hidden_units, width), both[:, :units]
        )

    (update,) = call(
        core_body,
        [jax.ShapeDtypeStruct((units, width), BF16)],
        [vmem(mine), vmem(theirs)],
        2 * 4 * slots * width * units * 2,
    )

    def combine_body(pick_ref, *refs):
        rows_back = jnp.concatenate([r[...].astype(F32) for r in refs[:-1]], axis=0)
        refs[-1][...] = plain(pick_ref[...], rows_back.astype(BF16)).astype(BF16)

    (cotangent,) = call(
        combine_body,
        [jax.ShapeDtypeStruct((rows, width), BF16)],
        [vmem(pick)] + [vmem(b) for b in back],
        10**6,
    )
    return cotangent, update


def large_program(
    x, u, routes, gates, own, tokens_dev, experts, capacity, hidden_units
):
    rows, width = x.shape
    block = rows // tokens_dev * capacity
    slots = experts * block
    units = own[0].shape[1]
    x_rows, s_rows, pick = route_rows(
        x, u, routes, gates, 0, tokens_dev, experts, capacity
    )
    other = [swap_half(w) for w in own]
    sent = jnp.stack([x_rows.astype(BF16), s_rows.astype(BF16)])
    sent = sent.reshape(2, experts, block, width)
    got = lax.all_to_all(sent, "expert", split_axis=1, concat_axis=1, tiled=True)
    x_rows = got[0].reshape(slots, width)
    s_rows = got[1].reshape(slots, width)
    hidden, active, slope = forward_values(x_rows, [own[:2], other[:2]])
    theirs = swap_half(jnp.concatenate([hidden[1], hidden[0], s_rows], axis=1))
    mine = jnp.concatenate([hidden[0], hidden[1], s_rows], axis=1)
    total = backward_values(s_rows, active, slope, [own, other])
    total = total.astype(BF16).reshape(experts, block, width)
    back = lax.all_to_all(total, "expert", split_axis=0, concat_axis=0, tiled=True)
    cotangent = plain(pick, back.reshape(slots, width)).astype(BF16)
    both = jnp.concatenate([mine, theirs], axis=0)
    update = polynomial_core(
        both[:, 2 * units :], both[:, : 2 * units], max(hidden_units, width), both[:, :units]
    )
    return cotangent, update


def on_device(activations, upstream, routes, route_gates, gate_matrix, up_matrix, down_matrix):
    experts = lax.axis_size("expert")
    halves = lax.axis_size("half")
    batches, tokens_dev, top = routes.shape
    width = activations.shape[2]
    capacity = max(2, 6 * tokens_dev * top // (5 * experts))
    rows = batches * tokens_dev
    own = (gate_matrix[0], up_matrix[0], down_matrix[0])
    hidden_units = down_matrix.shape[1] * halves
    program = small_program if experts <= MAX_PERMUTED else large_program
    cotangent, update = program(
        activations.reshape(rows, width),
        upstream.reshape(rows, width),
        routes.reshape(rows, top),
        route_gates.reshape(rows, top),
        own, tokens_dev, experts, capacity, hidden_units,
    )
    return cotangent.reshape(batches, tokens_dev, width), update[None]


def solution(mesh):
    tokens = P(None, ("dp", "expert", "half"), None)
    return jax.shard_map(
        on_device,
        mesh=mesh,
        in_specs=(tokens,) * 4
        + (P("expert", None, "half"), P("expert", None, "half"), P("expert", "half", None)),
        out_specs=(tokens, P(("dp", "expert"), "half", None)),
        check_vma=False,
    )
```

time: 125 us -> 37.3 us (0.30)
  matrix products: 26.6 us -> 0 us
  waiting for transfers between devices: 28.5 us -> 8.95 us
  blocking collectives: 15 us -> 0 us
  between operations: 15.1 us -> 0.7 us
  starting transfers between devices: 26.1 us -> 14 us
  Pallas kernels: 0 us -> 7.86 us
  other arithmetic: 5.78 us -> 0 us
  local copies, waits for them, and re-layouts: 7.15 us -> 5.39 us
    dot_general x22 -> x0, matrix products: 26.6 us -> none  [the longest x8 10.7 us: contract_last(): lax.dot_general(left, right, (((1,), (1,)), ((), ())), preferred_element_...]
    all_to_all x6 -> x0, starting transfers between devices: 26 us -> none  [the longest x2 11.2 us: on_device(): lax.all_to_all(token_send, 'expert', split_axis=0, concat_axis=0, tiled=T...]
    all_to_all x6 -> x0, waiting for transfers between devices: 21.6 us -> none  [the longest x2 11.4 us: on_device(): lax.all_to_all(outgoing, ('expert', 'half'), split_axis=0, concat_axis=0,...]
    ppermute x0 -> x10, starting transfers between devices: none -> 14 us  [the longest x6 12.9 us: shift(): lax.ppermute(value, 'expert', [(i, (i + by) % experts) for i in range(exp...]
    all_gather x6 -> x0, blocking collectives: 12 us -> none  [the longest x2 4.35 us: on_device(): lax.all_gather(gram_rows.astype(jnp.bfloat16), 'half', axis=0, tiled=True)]
    ppermute x0 -> x10, waiting for transfers between devices: none -> 8.95 us  [the longest x6 8.94 us: shift(): lax.ppermute(value, 'expert', [(i, (i + by) % experts) for i in range(exp...]
    pallas_call x0 -> x5, Pallas kernels: none -> 7.86 us  [call(): pl.pallas_call(body, out_shape=shapes, in_specs=[SPEC] * len(args), out_s...]
    all_gather x2 -> x0, waiting for transfers between devices: 6.92 us -> none  [on_device(): whole_rows = lax.all_gather(rounded, 'half', axis=0, tiled=True)]
  transfers between devices with their start and end apart: 8 -> 10, of which waited for: 7 -> 6; matrix products, arithmetic and copies ran while one was open for 12% -> 0% of each run, Pallas kernels for 0% -> 13%
where the time goes in v1:
time: 37.3 us; the launch traced here: 36.9 us
  starting transfers between devices  14 us (38%)
  waiting for transfers between devices  8.95 us (24%)
  Pallas kernels  7.86 us (21%)
  local copies, waits for them, and re-layouts  5.39 us (14%)
  between operations  0.7 us (2%)
    ppermute x6, starting transfers between devices, shift(): lax.ppermute(value, 'expert', [(i, (i + by) % experts) for i in range(exp...  12.9 us
    ppermute x6, waiting for transfers between devices, shift(): lax.ppermute(value, 'expert', [(i, (i + by) % experts) for i in range(exp...  8.94 us
    pallas_call x5, Pallas kernels, call(): pl.pallas_call(body, out_shape=shapes, in_specs=[SPEC] * len(args), out_s...  7.86 us
    unnamed x18, local copies, waits for them, and re-layouts  5.21 us
    ppermute x4, starting transfers between devices, swap_half(): lax.ppermute(value, 'half', [(i, (i + 1) % halves) for i in range(halves)])  1.1 us
  transfers between devices with their start and end apart: 10, of which 6 were waited for; matrix products, arithmetic and copies ran while one was open for 0% of the time, Pallas kernels for 13%

profile of v1, /device:TPU:0, one launch (start us, length us, event | category | flops | bytes accessed | tf_op | source)
XLA Modules:
  0.0 36.9 jit_solution(15501979905235257966)
XLA Ops:
  0.6 0.0 copy-start.7
  0.6 0.5 %collective-permute-start.3 = (bf16[2048,256]{1,0:T(8,128)(2,1)}, bf16[2048,256]{1,0:T(8,128)(2,1)S(1)}, u32[]{:S(2)}, u32[]{:S(2)}) collective-permute-start(bf16[2048,256]{1,0:T(8,128)(2,1)} %bitcast.9), channel_id=1, source_target_pairs={{0,1},{1,0},{2,3},{3,2},{4,5},{5,4},{6,7},{7,6},{8,9},{9,8},{10,11... | collective-permute-start | bytes 3145736 | tf_op jit(solution)/shard_map/ppermute | solution.py:150
  1.2 0.1 collective-permute-start.4
  1.2 0.0 copy-start.8
  1.2 0.4 %collective-permute-start.5 = (bf16[256,2048]{1,0:T(8,128)(2,1)}, bf16[256,2048]{1,0:T(8,128)(2,1)S(1)}, u32[]{:S(2)}, u32[]{:S(2)}) collective-permute-start(bf16[256,2048]{1,0:T(8,128)(2,1)} %bitcast.15), channel_id=1, source_target_pairs={{0,1},{1,0},{2,3},{3,2},{4,5},{5,4},{6,7},{7,6},{8,9},{9,8},{10,11... | collective-permute-start | bytes 3145736 | tf_op jit(solution)/shard_map/ppermute | solution.py:150
  1.7 0.0 copy-done.7
  1.7 0.1 copy.13
  1.8 0.2 copy-done.8
  1.9 0.1 copy.14
  2.0 0.0 copy-start.5
  2.0 0.8 %copy-done.5 = bf16[2,8,2048]{2,1,0:T(8,128)(2,1)S(1)} copy-done((bf16[2,8,2048]{2,1,0:T(8,128)(2,1)S(1)}, bf16[2,8,2048]{2,1,0:T(8,128)(2,1)}, u32[]{:S(2)}) %copy-start.5) | copy-done | bytes 65560
  2.8 0.0 copy-start.6
  2.9 0.8 %copy-done.6 = bf16[2,8,2048]{2,1,0:T(8,128)(2,1)S(1)} copy-done((bf16[2,8,2048]{2,1,0:T(8,128)(2,1)S(1)}, bf16[2,8,2048]{2,1,0:T(8,128)(2,1)}, u32[]{:S(2)}) %copy-start.6) | copy-done | bytes 65560
  3.7 0.6 %shard_map.86 = (bf16[16,2048]{1,0:T(8,128)(2,1)S(1)}, bf16[16,2048]{1,0:T(8,128)(2,1)S(1)}, bf16[16,2048]{1,0:T(8,128)(2,1)S(1)}, bf16[16,2048]{1,0:T(8,128)(2,1)S(1)}, bf16[16,32]{1,0:T(8,128)(2,1)S(1)}) custom-call(bf16[16,2048]{1,0:T(8,128)(2,1)S(1)} %bitcast.17, bf16[16,2048]{1,0:T(8,128)(2,1)S(1)} %bitcast.18, s32[16,2]{1,0:T(8,128)S(1)} %bitcast.19, ...), custom_call_target="tpu_custom_call" | custom-call | flops 10000000 | tf_op jit(solution)/shard_map/pallas_call | solution.py:126
  4.3 3.1 %collective-permute-start = (bf16[16,2048]{1,0:T(8,128)(2,1)S(1)}, bf16[16,2048]{1,0:T(8,128)(2,1)S(1)}, u32[]{:S(2)}, u32[]{:S(2)}) collective-permute-start(bf16[16,2048]{1,0:T(8,128)(2,1)S(1)} %get-tuple-element.17), channel_id=1, source_target_pairs={{0,2},{2,4},{4,6},{6,0},{1,3},{3,5},{5,7},{7,1},{8,10},{10,12},{12... | collective-permute-start | bytes 196616 | tf_op jit(solution)/shard_map/ppermute | solution.py:181
  7.4 2.6 %collective-permute-start.1 = (bf16[16,2048]{1,0:T(8,128)(2,1)S(1)}, bf16[16,2048]{1,0:T(8,128)(2,1)S(1)}, u32[]{:S(2)}, u32[]{:S(2)}) collective-permute-start(bf16[16,2048]{1,0:T(8,128)(2,1)S(1)} %get-tuple-element.18), channel_id=1, source_target_pairs={{0,4},{2,6},{4,0},{6,2},{1,5},{3,7},{5,1},{7,3},{8,12},{10,14},{12... | collective-permute-start | bytes 196616 | tf_op jit(solution)/shard_map/ppermute | solution.py:181
  9.9 2.0 %collective-permute-done.refs_1_ = bf16[16,2048]{1,0:T(8,128)(2,1)S(1)} collective-permute-done((bf16[16,2048]{1,0:T(8,128)(2,1)S(1)}, bf16[16,2048]{1,0:T(8,128)(2,1)S(1)}, u32[]{:S(2)}, u32[]{:S(2)}) %collective-permute-start) | collective-permute-done | bytes 65568 | tf_op jit(solution)/shard_map/ppermute | solution.py:181
  11.9 2.4 %collective-permute-start.2 = (bf16[16,2048]{1,0:T(8,128)(2,1)S(1)}, bf16[16,2048]{1,0:T(8,128)(2,1)S(1)}, u32[]{:S(2)}, u32[]{:S(2)}) collective-permute-start(bf16[16,2048]{1,0:T(8,128)(2,1)S(1)} %get-tuple-element.19), channel_id=1, source_target_pairs={{0,6},{2,0},{4,2},{6,4},{1,7},{3,1},{5,3},{7,5},{8,14},{10,8},{12,... | collective-permute-start | bytes 196616 | tf_op jit(solution)/shard_map/ppermute | solution.py:181
  14.4 0.3 collective-permute-done.1.refs_2_
  14.6 1.6 %collective-permute-done.2.refs_3_ = bf16[16,2048]{1,0:T(8,128)(2,1)S(1)} collective-permute-done((bf16[16,2048]{1,0:T(8,128)(2,1)S(1)}, bf16[16,2048]{1,0:T(8,128)(2,1)S(1)}, u32[]{:S(2)}, u32[]{:S(2)}) %collective-permute-start.2) | collective-permute-done | bytes 65568 | tf_op jit(solution)/shard_map/ppermute | solution.py:181
  16.3 0.0 collective-permute-done.3.refs_6_.refs_3_
  16.3 0.0 collective-permute-done.4.refs_7_.refs_4_
  16.3 0.0 copy-start
  16.3 1.2 %copy-done = bf16[1,2048,256]{2,1,0:T(8,128)(2,1)S(1)} copy-done((bf16[1,2048,256]{2,1,0:T(8,128)(2,1)S(1)}, bf16[1,2048,256]{2,1,0:T(8,128)(2,1)}, u32[]{:S(2)}) %copy-start) | copy-done | bytes 1048600
  17.5 0.0 copy-start.2
  17.5 1.2 %copy-done.2 = bf16[1,2048,256]{2,1,0:T(8,128)(2,1)S(1)} copy-done((bf16[1,2048,256]{2,1,0:T(8,128)(2,1)S(1)}, bf16[1,2048,256]{2,1,0:T(8,128)(2,1)}, u32[]{:S(2)}) %copy-start.2) | copy-done | bytes 1048600
  18.7 0.0 copy-start.1
  18.7 0.0 copy-start.3
  18.7 0.0 copy-start.4
  18.7 0.8 %shard_map.87 = (bf16[32,2560]{1,0:T(8,128)(2,1)S(1)}, bf16[32,2560]{1,0:T(8,128)(2,1)S(1)}, f32[32,512]{1,0:T(8,128)S(1)}, f32[32,512]{1,0:T(8,128)S(1)}) custom-call(bf16[16,2048]{1,0:T(8,128)(2,1)S(1)} %get-tuple-element.16.refs_0_, bf16[16,2048]{1,0:T(8,128)(2,1)S(1)} %collective-permute-done.refs_1_, ...), custom_call_target="tpu_custom_call" | custom-call | flops 134217728 | tf_op jit(solution)/shard_map/pallas_call | solution.py:126
  19.6 0.1 collective-permute-start.9
  19.6 0.0 collective-permute-done.5.refs_5_
  19.7 0.3 copy-done.1
  19.9 0.3 copy-done.3
  20.3 0.3 copy-done.4
  20.6 2.4 %shard_map.88 = (bf16[8,2048]{1,0:T(8,128)(2,1)S(1)}, bf16[8,2048]{1,0:T(8,128)(2,1)S(1)}, bf16[8,2048]{1,0:T(8,128)(2,1)S(1)}, bf16[8,2048]{1,0:T(8,128)(2,1)S(1)}) custom-call(bf16[32,2560]{1,0:T(8,128)(2,1)S(1)} %get-tuple-element.20.mine_ref, f32[32,512]{1,0:T(8,128)S(1)} %get-tuple-element.21.active_ref, f32[32,512]{1,0:T(8,128)S(1)} %get-tuple-element.22.slope_ref, ...), custom_call_target="tpu_custom_call" | custom-call | flops 201326592 | tf_op jit(solution)/shard_map/pallas_call | solution.py:126
  23.0 4.2 %collective-permute-start.6 = (bf16[8,2048]{1,0:T(8,128)(2,1)S(1)}, bf16[8,2048]{1,0:T(8,128)(2,1)S(1)}, u32[]{:S(2)}, u32[]{:S(2)}) collective-permute-start(bf16[8,2048]{1,0:T(8,128)(2,1)S(1)} %get-tuple-element.24), channel_id=1, source_target_pairs={{0,6},{2,0},{4,2},{6,4},{1,7},{3,1},{5,3},{7,5},{8,14},{10,8},{12,... | collective-permute-start | bytes 98312 | tf_op jit(solution)/shard_map/ppermute | solution.py:181
  27.2 0.0 collective-permute-start.7
  27.2 0.6 %collective-permute-start.8 = (bf16[8,2048]{1,0:T(8,128)(2,1)S(1)}, bf16[8,2048]{1,0:T(8,128)(2,1)S(1)}, u32[]{:S(2)}, u32[]{:S(2)}) collective-permute-start(bf16[8,2048]{1,0:T(8,128)(2,1)S(1)} %get-tuple-element.26), channel_id=1, source_target_pairs={{0,2},{2,4},{4,6},{6,0},{1,3},{3,5},{5,7},{7,1},{8,10},{10,12},{12... | collective-permute-start | bytes 98312 | tf_op jit(solution)/shard_map/ppermute | solution.py:181
  27.8 1.0 %collective-permute-done.6.refs_1_ = bf16[8,2048]{1,0:T(8,128)(2,1)S(1)} collective-permute-done((bf16[8,2048]{1,0:T(8,128)(2,1)S(1)}, bf16[8,2048]{1,0:T(8,128)(2,1)S(1)}, u32[]{:S(2)}, u32[]{:S(2)}) %collective-permute-start.6) | collective-permute-done | bytes 32800 | tf_op jit(solution)/shard_map/ppermute | solution.py:181
  28.8 3.2 %collective-permute-done.7.refs_2_ = bf16[8,2048]{1,0:T(8,128)(2,1)S(1)} collective-permute-done((bf16[8,2048]{1,0:T(8,128)(2,1)S(1)}, bf16[8,2048]{1,0:T(8,128)(2,1)S(1)}, u32[]{:S(2)}, u32[]{:S(2)}) %collective-permute-start.7) | collective-permute-done | bytes 32800 | tf_op jit(solution)/shard_map/ppermute | solution.py:181
  32.0 0.9 %collective-permute-done.8.refs_3_ = bf16[8,2048]{1,0:T(8,128)(2,1)S(1)} collective-permute-done((bf16[8,2048]{1,0:T(8,128)(2,1)S(1)}, bf16[8,2048]{1,0:T(8,128)(2,1)S(1)}, u32[]{:S(2)}, u32[]{:S(2)}) %collective-permute-start.8) | collective-permute-done | bytes 32800 | tf_op jit(solution)/shard_map/ppermute | solution.py:181
  32.9 0.8 %shard_map.89 = bf16[16,2048]{1,0:T(8,128)(2,1)} custom-call(bf16[16,32]{1,0:T(8,128)(2,1)S(1)} %get-tuple-element.15.pick_ref, bf16[8,2048]{1,0:T(8,128)(2,1)S(1)} %get-tuple-element.23.refs_0_, bf16[8,2048]{1,0:T(8,128)(2,1)S(1)} %collective-permute-done.6.refs_1_, bf16[8,2048]{1,0:T(8,128)(2,1)S(1)} %collective-permute-done.7.refs_2_, ...), custom_call_target="tpu_custom_call" | custom-call | flops 1000000 | tf_op jit(solution)/shard_map/pallas_call | solution.py:126
  33.7 0.0 collective-permute-done.9.theirs_ref
  33.7 3.3 %shard_map.90 = bf16[256,2048]{1,0:T(8,128)(2,1)} custom-call(bf16[32,2560]{1,0:T(8,128)(2,1)S(1)} %get-tuple-element.20.mine_ref, bf16[32,2560]{1,0:T(8,128)(2,1)S(1)} %collective-permute-done.9.theirs_ref), custom_call_target="tpu_custom_call" | custom-call | flops 268435456 | tf_op jit(solution)/shard_map/pallas_call | solution.py:126
Async XLA Ops:
  0.6 1.0 %copy-start.7 = (s32[2,8,2]{1,2,0:T(2,128)S(1)}, s32[2,8,2]{1,2,0:T(2,128)}, u32[]{:S(2)}) copy-start(s32[2,8,2]{1,2,0:T(2,128)} %param.9) | copy-start | bytes 388
  0.6 15.6 %collective-permute-start.3 = (bf16[2048,256]{1,0:T(8,128)(2,1)}, bf16[2048,256]{1,0:T(8,128)(2,1)S(1)}, u32[]{:S(2)}, u32[]{:S(2)}) collective-permute-start(bf16[2048,256]{1,0:T(8,128)(2,1)} %bitcast.9), channel_id=1, source_target_pairs={{0,1},{1,0},{2,3},{3,2},{4,5},{5,4},{6,7},{7,6},{8,9},{9,8},{10,11... | collective-permute-start | bytes 3145736 | tf_op jit(solution)/shard_map/ppermute | solution.py:150
  1.2 15.1 %collective-permute-start.4 = (bf16[2048,256]{1,0:T(8,128)(2,1)}, bf16[2048,256]{1,0:T(8,128)(2,1)S(1)}, u32[]{:S(2)}, u32[]{:S(2)}) collective-permute-start(bf16[2048,256]{1,0:T(8,128)(2,1)} %bitcast.12), channel_id=1, source_target_pairs={{0,1},{1,0},{2,3},{3,2},{4,5},{5,4},{6,7},{7,6},{8,9},{9,8},{10,11... | collective-permute-start | bytes 3145736 | tf_op jit(solution)/shard_map/ppermute | solution.py:150
  1.2 0.7 %copy-start.8 = (f32[2,8,2]{1,2,0:T(2,128)S(1)}, f32[2,8,2]{1,2,0:T(2,128)}, u32[]{:S(2)}) copy-start(f32[2,8,2]{1,2,0:T(2,128)} %param.10) | copy-start | bytes 388
  1.2 18.4 %collective-permute-start.5 = (bf16[256,2048]{1,0:T(8,128)(2,1)}, bf16[256,2048]{1,0:T(8,128)(2,1)S(1)}, u32[]{:S(2)}, u32[]{:S(2)}) collective-permute-start(bf16[256,2048]{1,0:T(8,128)(2,1)} %bitcast.15), channel_id=1, source_target_pairs={{0,1},{1,0},{2,3},{3,2},{4,5},{5,4},{6,7},{7,6},{8,9},{9,8},{10,11... | collective-permute-start | bytes 3145736 | tf_op jit(solution)/shard_map/ppermute | solution.py:150
  2.0 0.8 %copy-start.5 = (bf16[2,8,2048]{2,1,0:T(8,128)(2,1)S(1)}, bf16[2,8,2048]{2,1,0:T(8,128)(2,1)}, u32[]{:S(2)}) copy-start(bf16[2,8,2048]{2,1,0:T(8,128)(2,1)} %param.7) | copy-start | bytes 196612
  2.8 0.8 %copy-start.6 = (bf16[2,8,2048]{2,1,0:T(8,128)(2,1)S(1)}, bf16[2,8,2048]{2,1,0:T(8,128)(2,1)}, u32[]{:S(2)}) copy-start(bf16[2,8,2048]{2,1,0:T(8,128)(2,1)} %param.8) | copy-start | bytes 196612
  4.3 7.6 %collective-permute-start = (bf16[16,2048]{1,0:T(8,128)(2,1)S(1)}, bf16[16,2048]{1,0:T(8,128)(2,1)S(1)}, u32[]{:S(2)}, u32[]{:S(2)}) collective-permute-start(bf16[16,2048]{1,0:T(8,128)(2,1)S(1)} %get-tuple-element.17), channel_id=1, source_target_pairs={{0,2},{2,4},{4,6},{6,0},{1,3},{3,5},{5,7},{7,1},{8,10},{10,12},{12... | collective-permute-start | bytes 196616 | tf_op jit(solution)/shard_map/ppermute | solution.py:181
  7.4 7.3 %collective-permute-start.1 = (bf16[16,2048]{1,0:T(8,128)(2,1)S(1)}, bf16[16,2048]{1,0:T(8,128)(2,1)S(1)}, u32[]{:S(2)}, u32[]{:S(2)}) collective-permute-start(bf16[16,2048]{1,0:T(8,128)(2,1)S(1)} %get-tuple-element.18), channel_id=1, source_target_pairs={{0,4},{2,6},{4,0},{6,2},{1,5},{3,7},{5,1},{7,3},{8,12},{10,14},{12... | collective-permute-start | bytes 196616 | tf_op jit(solution)/shard_map/ppermute | solution.py:181
  11.9 4.3 %collective-permute-start.2 = (bf16[16,2048]{1,0:T(8,128)(2,1)S(1)}, bf16[16,2048]{1,0:T(8,128)(2,1)S(1)}, u32[]{:S(2)}, u32[]{:S(2)}) collective-permute-start(bf16[16,2048]{1,0:T(8,128)(2,1)S(1)} %get-tuple-element.19), channel_id=1, source_target_pairs={{0,6},{2,0},{4,2},{6,4},{1,7},{3,1},{5,3},{7,5},{8,14},{10,8},{12,... | collective-permute-start | bytes 196616 | tf_op jit(solution)/shard_map/ppermute | solution.py:181
  16.3 1.2 %copy-start = (bf16[1,2048,256]{2,1,0:T(8,128)(2,1)S(1)}, bf16[1,2048,256]{2,1,0:T(8,128)(2,1)}, u32[]{:S(2)}) copy-start(bf16[1,2048,256]{2,1,0:T(8,128)(2,1)} %param.11) | copy-start | bytes 3145732
  17.5 1.2 %copy-start.2 = (bf16[1,2048,256]{2,1,0:T(8,128)(2,1)S(1)}, bf16[1,2048,256]{2,1,0:T(8,128)(2,1)}, u32[]{:S(2)}) copy-start(bf16[1,2048,256]{2,1,0:T(8,128)(2,1)} %param.12) | copy-start | bytes 3145732
  18.7 1.2 %copy-start.1 = (bf16[1,2048,256]{2,1,0:T(8,128)(2,1)S(1)}, bf16[1,2048,256]{2,1,0:T(8,128)(2,1)}, u32[]{:S(2)}) copy-start(bf16[1,2048,256]{2,1,0:T(8,128)(2,1)} %param.11) | copy-start | bytes 3145732
  18.7 1.5 %copy-start.3 = (bf16[1,2048,256]{2,1,0:T(8,128)(2,1)S(1)}, bf16[1,2048,256]{2,1,0:T(8,128)(2,1)}, u32[]{:S(2)}) copy-start(bf16[1,2048,256]{2,1,0:T(8,128)(2,1)} %param.12) | copy-start | bytes 3145732
  18.7 1.9 %copy-start.4 = (bf16[1,256,2048]{2,1,0:T(8,128)(2,1)S(1)}, bf16[1,256,2048]{2,1,0:T(8,128)(2,1)}, u32[]{:S(2)}) copy-start(bf16[1,256,2048]{2,1,0:T(8,128)(2,1)} %param.13) | copy-start | bytes 3145732
  19.6 14.1 %collective-permute-start.9 = (bf16[32,2560]{1,0:T(8,128)(2,1)S(1)}, bf16[32,2560]{1,0:T(8,128)(2,1)S(1)}, u32[]{:S(2)}, u32[]{:S(2)}) collective-permute-start(bf16[32,2560]{1,0:T(8,128)(2,1)S(1)} %get-tuple-element.27), channel_id=1, source_target_pairs={{0,1},{1,0},{2,3},{3,2},{4,5},{5,4},{6,7},{7,6},{8,9},{9,8},{10,11... | collective-permute-start | bytes 491528 | tf_op jit(solution)/shard_map/ppermute | solution.py:150
  23.0 5.8 %collective-permute-start.6 = (bf16[8,2048]{1,0:T(8,128)(2,1)S(1)}, bf16[8,2048]{1,0:T(8,128)(2,1)S(1)}, u32[]{:S(2)}, u32[]{:S(2)}) collective-permute-start(bf16[8,2048]{1,0:T(8,128)(2,1)S(1)} %get-tuple-element.24), channel_id=1, source_target_pairs={{0,6},{2,0},{4,2},{6,4},{1,7},{3,1},{5,3},{7,5},{8,14},{10,8},{12,... | collective-permute-start | bytes 98312 | tf_op jit(solution)/shard_map/ppermute | solution.py:181
  27.2 4.8 %collective-permute-start.7 = (bf16[8,2048]{1,0:T(8,128)(2,1)S(1)}, bf16[8,2048]{1,0:T(8,128)(2,1)S(1)}, u32[]{:S(2)}, u32[]{:S(2)}) collective-permute-start(bf16[8,2048]{1,0:T(8,128)(2,1)S(1)} %get-tuple-element.25), channel_id=1, source_target_pairs={{0,4},{2,6},{4,0},{6,2},{1,5},{3,7},{5,1},{7,3},{8,12},{10,14},{12... | collective-permute-start | bytes 98312 | tf_op jit(solution)/shard_map/ppermute | solution.py:181
  27.2 5.7 %collective-permute-start.8 = (bf16[8,2048]{1,0:T(8,128)(2,1)S(1)}, bf16[8,2048]{1,0:T(8,128)(2,1)S(1)}, u32[]{:S(2)}, u32[]{:S(2)}) collective-permute-start(bf16[8,2048]{1,0:T(8,128)(2,1)S(1)} %get-tuple-element.26), channel_id=1, source_target_pairs={{0,2},{2,4},{4,6},{6,0},{1,3},{3,5},{5,7},{7,1},{8,10},{10,12},{12... | collective-permute-start | bytes 98312 | tf_op jit(solution)/shard_map/ppermute | solution.py:181

commit v2 on v1

v2 whole, which is shorter than its diff:
```python
import functools
import math

import jax
import jax.numpy as jnp
from jax import lax
from jax.experimental import pallas as pl
from jax.experimental.pallas import tpu as pltpu
from jax.sharding import PartitionSpec as P

ITERS = 2
MAX_PERMUTED = 8

linear_term = 3.4445
cubic_term = -4.775
quintic_term = 2.0315

F32 = jnp.float32
BF16 = jnp.bfloat16


def dot(left, right, dims, precision=None):
    return lax.dot_general(
        left, right, (dims, ((), ())), precision=precision, preferred_element_type=F32
    )


def contract_last(left, right):
    return dot(left, right, ((1,), (1,)))


def plain(left, right, precision=None):
    return dot(left, right, ((1,), (0,)), precision)


def route_slots(routes, base, experts, block, capacity):
    tokens_dev = routes[0].shape[1]
    expert_ids = lax.broadcasted_iota(jnp.int32, (experts, tokens_dev), 0)
    row = lax.broadcasted_iota(jnp.int32, (tokens_dev, tokens_dev), 0)
    col = lax.broadcasted_iota(jnp.int32, (tokens_dev, tokens_dev), 1)
    earlier = jnp.where(row < col, 1.0, 0.0).astype(BF16)
    found = []
    for batch, named in enumerate(routes):
        top = named.shape[0]
        onehots = [jnp.where(named[k : k + 1] == expert_ids, 1.0, 0.0) for k in range(top)]
        before = plain(sum(onehots).astype(BF16), earlier)
        slots = []
        for k in range(top):
            position = jnp.sum(before * onehots[k], axis=0, keepdims=True).astype(jnp.int32)
            before = before + onehots[k]
            relative = named[k : k + 1] - base
            relative = jnp.where(relative < 0, relative + experts, relative)
            slots.append((relative, batch * capacity + position))
        found.append(slots)
    return found


def route_rows(data, routes, gates, base, experts, capacity):
    batches, top = len(routes), routes[0].shape[0]
    block = batches * capacity
    found = route_slots(routes, base, experts, block, capacity)
    joined = lambda rows: jnp.concatenate(rows, axis=1)
    tokens = data.shape[0] // 2
    row = lax.broadcasted_iota(jnp.int32, (2 * experts * block, tokens), 0)
    slot = lax.broadcasted_iota(jnp.int32, (experts * block, tokens), 0)
    in_x = row[:, :1] % (2 * block) < block
    pick_x, pick_u, pick_tok, gate = 0.0, 0.0, 0.0, jnp.where(in_x, 1.0, 0.0)
    for k in range(top):
        relative = joined([found[m][k][0] for m in range(batches)])
        within = joined([found[m][k][1] for m in range(batches)])
        gates_k = joined([gates[m][k : k + 1] for m in range(batches)])
        at = relative * (2 * block) + within
        here = row == at + block
        pick_x = pick_x + jnp.where(row == at, 1.0, 0.0)
        pick_u = pick_u + jnp.where(here, 1.0, 0.0)
        pick_tok = pick_tok + jnp.where(slot == relative * block + within, 1.0, 0.0)
        gate = gate + jnp.sum(jnp.where(here, gates_k, 0.0), axis=1, keepdims=True)
    picks = joined([pick_x, pick_u]).astype(BF16)
    return plain(picks, data) * gate, pick_tok


def forward_values(x_rows, weights):
    hidden, active, slope = [], [], []
    for gate, up in weights:
        pre_gate = plain(x_rows, gate)
        pre_up = plain(x_rows, up)
        sigmoid = 1.0 / (1.0 + jnp.exp(-pre_gate))
        activated = pre_gate * sigmoid
        hidden.append((activated * pre_up).astype(BF16))
        active.append(activated)
        slope.append(pre_up * sigmoid * (1.0 + pre_gate * (1.0 - sigmoid)))
    return hidden, active, slope


def backward_values(s_rows, active, slope, weights):
    total = None
    for activated, steep, (gate, up, down) in zip(active, slope, weights):
        hidden_grad = contract_last(s_rows, down)
        gate_grad = (hidden_grad * steep).astype(BF16)
        up_grad = (hidden_grad * activated).astype(BF16)
        piece = contract_last(gate_grad, gate) + contract_last(up_grad, up)
        piece = piece.astype(BF16).astype(F32)
        total = piece if total is None else total + piece
    return total


def polynomial_core(scaled, hidden, width, own):
    exact = lax.Precision.HIGHEST
    rows = scaled.shape[0]
    left = contract_last(scaled, scaled)
    right = contract_last(hidden, hidden)
    squares = jnp.maximum(jnp.sum(left * right), 0.0)
    inverse = 1.0 / (jnp.sqrt(squares) + 1e-07)
    row = lax.broadcasted_iota(jnp.int32, (rows, rows), 0)
    col = lax.broadcasted_iota(jnp.int32, (rows, rows), 1)
    eye = jnp.where(row == col, linear_term, 0.0)
    moment = plain(left * inverse, right * inverse, exact)
    core = None
    for iteration in range(ITERS):
        factor = eye + cubic_term * moment + quintic_term * plain(moment, moment, exact)
        core = factor if core is None else plain(factor, core, exact)
        if iteration < ITERS - 1:
            moment = plain(plain(moment, factor, exact), factor, exact)
    core = core * (inverse * math.sqrt(width))
    mixed = dot(core, own.astype(F32), ((0,), (0,)), exact)
    high = mixed.astype(BF16).astype(F32)
    stacked = jnp.transpose(jnp.concatenate([high, mixed - high], axis=0)).astype(BF16)
    return plain(stacked, jnp.concatenate([scaled, scaled], axis=0)).astype(BF16)


def vmem(value):
    return pltpu.with_memory_space_constraint(value, pltpu.VMEM)


def hbm(value):
    return pltpu.with_memory_space_constraint(value, pltpu.HBM)


IN_VMEM = pl.BlockSpec(memory_space=pltpu.VMEM)
IN_HBM = pl.BlockSpec(memory_space=pltpu.HBM)


def call(body, shapes, args, flops, specs=None, scratch=(), limit=16 << 20):
    return pl.pallas_call(
        body,
        out_shape=shapes,
        in_specs=specs or [IN_VMEM] * len(args),
        out_specs=[IN_VMEM] * len(shapes),
        scratch_shapes=scratch,
        compiler_params=pltpu.CompilerParams(vmem_limit_bytes=limit),
        cost_estimate=pl.CostEstimate(flops=flops, bytes_accessed=0, transcendentals=0),
    )(*args)


def kept(shape, dtype):
    return pltpu.VMEM(shape, dtype)


def pairs(refs):
    values = [r[...].astype(F32) for r in refs]
    half = values[0].shape[0] // 2
    x_rows = jnp.concatenate([v[:half] for v in values], axis=0).astype(BF16)
    s_rows = jnp.concatenate([v[half:] for v in values], axis=0).astype(BF16)
    return x_rows, s_rows


def swap_half(value):
    halves = lax.axis_size("half")
    return lax.ppermute(value, "half", [(i, (i + 1) % halves) for i in range(halves)])


def small_program(activations, upstream, routes, gates, own, experts, capacity, hidden_units):
    batches, top, tokens_dev = routes.shape
    width = activations.shape[1]
    rows = batches * tokens_dev
    block = batches * capacity
    slots = experts * block
    units = own[0].shape[1]

    def dispatch_body(x_hbm, u_hbm, routes_hbm, gates_hbm, *refs):
        *outs, pick_ref, data, routes_ref, gates_ref, sems = refs
        copies = [
            pltpu.make_async_copy(routes_hbm, routes_ref, sems.at[0]),
            pltpu.make_async_copy(gates_hbm, gates_ref, sems.at[1]),
            pltpu.make_async_copy(x_hbm, data.at[:rows], sems.at[2]),
            pltpu.make_async_copy(u_hbm, data.at[rows:], sems.at[3]),
        ]
        for copy in copies:
            copy.start()
        for copy in copies:
            copy.wait()
        sent, pick = route_rows(
            data[...],
            [routes_ref[m] for m in range(batches)],
            [gates_ref[m] for m in range(batches)],
            lax.axis_index("expert"), experts, capacity,
        )
        for d in range(experts):
            outs[d][...] = sent[2 * d * block : 2 * (d + 1) * block].astype(BF16)
        pick_ref[...] = pick

    *blocks, pick = call(
        dispatch_body,
        [kept((2 * block, width), BF16)] * experts + [kept((slots, rows), F32)],
        [hbm(v) for v in (activations, upstream, routes, gates)],
        10**7,
        specs=[IN_HBM] * 4,
        scratch=[
            pltpu.VMEM((2 * rows, width), BF16),
            pltpu.VMEM((batches, top, tokens_dev), jnp.int32),
            pltpu.VMEM((batches, top, tokens_dev), F32),
            pltpu.SemaphoreType.DMA((4,)),
        ],
    )

    def shift(value, by):
        return lax.ppermute(
            value, "expert", [(i, (i + by) % experts) for i in range(experts)]
        )

    held, blocks = lax.optimization_barrier((own, blocks))
    got = [blocks[0]] + [shift(blocks[d], d) for d in range(1, experts)]
    other = [swap_half(w) for w in held]

    def fetch_body(pick_ref, *refs):
        ins, outs, sems = refs[:3], refs[3:6], refs[7]
        copies = [pltpu.make_async_copy(ins[i], outs[i], sems.at[i]) for i in range(3)]
        for copy in copies:
            copy.start()
        refs[6][...] = jnp.transpose(pick_ref[...]).astype(BF16)
        for copy in copies:
            copy.wait()

    *near, pick = call(
        fetch_body,
        [kept(w.shape, BF16) for w in own] + [kept((rows, slots), BF16)],
        [vmem(pick)] + [hbm(w) for w in held],
        10**9,
        specs=[IN_VMEM] + [IN_HBM] * 3,
        scratch=[pltpu.SemaphoreType.DMA((3,))],
    )

    def expert_body(*refs):
        weights = [tuple(r[...] for r in refs[experts + 3 * i :][:3]) for i in range(2)]
        to_other, mine, *outs = refs[experts + 6 :]
        x_rows, s_rows = pairs(refs[:experts])
        hidden, active, slope = forward_values(x_rows, [w[:2] for w in weights])
        to_other[:, :units] = hidden[1]
        to_other[:, units : 2 * units] = hidden[0]
        to_other[:, 2 * units :] = s_rows
        mine[:, :units] = hidden[0]
        mine[:, units : 2 * units] = hidden[1]
        mine[:, 2 * units :] = s_rows
        total = backward_values(s_rows, active, slope, weights)
        for d in range(experts):
            outs[d][...] = total[d * block : (d + 1) * block].astype(BF16)

    to_other, mine, *grads = call(
        expert_body,
        [kept((slots, 2 * units + width), BF16)] * 2 + [kept((block, width), BF16)] * experts,
        [vmem(v) for v in (*got, *near, *other)],
        2 * slots * width * units * 10,
    )
    back = [grads[0]] + [shift(grads[d], experts - d) for d in range(1, experts)]
    theirs = swap_half(to_other)

    def core_body(mine_ref, theirs_ref, out_ref):
        both = jnp.concatenate(
            [mine_ref[...].astype(F32), theirs_ref[...].astype(F32)], axis=0
        ).astype(BF16)
        out_ref[...] = polynomial_core(
            both[:, 2 * units :], both[:, : 2 * units], max(hidden_units, width), both[:, :units]
        )

    (update,) = call(
        core_body,
        [jax.ShapeDtypeStruct((units, width), BF16)],
        [vmem(mine), vmem(theirs)],
        2 * 4 * slots * width * units * 2,
    )
    update, back = lax.optimization_barrier((update, back))

    def combine_body(pick_ref, *refs):
        rows_back = jnp.concatenate([r[...].astype(F32) for r in refs[:-1]], axis=0)
        refs[-1][...] = plain(pick_ref[...], rows_back.astype(BF16)).astype(BF16)

    (cotangent,) = call(
        combine_body,
        [jax.ShapeDtypeStruct((rows, width), BF16)],
        [vmem(pick)] + [vmem(b) for b in back],
        10**6,
    )
    return cotangent, update


def large_program(activations, upstream, routes, gates, own, experts, capacity, hidden_units):
    batches, top, tokens_dev = routes.shape
    width = activations.shape[1]
    block = batches * capacity
    slots = experts * block
    units = own[0].shape[1]
    sent, pick = route_rows(
        jnp.concatenate([activations, upstream], axis=0), routes, gates, 0, experts, capacity
    )
    other = [swap_half(w) for w in own]
    sent = sent.astype(BF16).reshape(experts, 2 * block, width)
    got = lax.all_to_all(sent, "expert", split_axis=0, concat_axis=0, tiled=True)
    x_rows = got[:, :block].reshape(slots, width)
    s_rows = got[:, block:].reshape(slots, width)
    hidden, active, slope = forward_values(x_rows, [own[:2], other[:2]])
    theirs = swap_half(jnp.concatenate([hidden[1], hidden[0], s_rows], axis=1))
    mine = jnp.concatenate([hidden[0], hidden[1], s_rows], axis=1)
    total = backward_values(s_rows, active, slope, [own, other])
    total = total.astype(BF16).reshape(experts, block, width)
    back = lax.all_to_all(total, "expert", split_axis=0, concat_axis=0, tiled=True)
    cotangent = dot(pick.astype(BF16), back.reshape(slots, width), ((0,), (0,))).astype(BF16)
    both = jnp.concatenate([mine, theirs], axis=0)
    update = polynomial_core(
        both[:, 2 * units :], both[:, : 2 * units], max(hidden_units, width), both[:, :units]
    )
    return cotangent, update


def on_device(activations, upstream, routes, route_gates, gate_matrix, up_matrix, down_matrix):
    experts = lax.axis_size("expert")
    halves = lax.axis_size("half")
    batches, tokens_dev, top = routes.shape
    width = activations.shape[2]
    capacity = max(2, 6 * tokens_dev * top // (5 * experts))
    rows = batches * tokens_dev
    own = (gate_matrix[0], up_matrix[0], down_matrix[0])
    hidden_units = down_matrix.shape[1] * halves
    program = small_program if experts <= MAX_PERMUTED else large_program
    cotangent, update = program(
        activations.reshape(rows, width),
        upstream.reshape(rows, width),
        jnp.swapaxes(routes, 1, 2),
        jnp.swapaxes(route_gates, 1, 2),
        own, experts, capacity, hidden_units,
    )
    return cotangent.reshape(batches, tokens_dev, width), update[None]


def solution(mesh):
    tokens = P(None, ("dp", "expert", "half"), None)
    return jax.shard_map(
        on_device,
        mesh=mesh,
        in_specs=(tokens,) * 4
        + (P("expert", None, "half"), P("expert", None, "half"), P("expert", "half", None)),
        out_specs=(tokens, P(("dp", "expert"), "half", None)),
        check_vma=False,
    )
```

time: 37.3 us -> 29.1 us (0.78)
  local copies, waits for them, and re-layouts: 5.39 us -> 0 us
  waiting for transfers between devices: 8.95 us -> 4.07 us
  Pallas kernels: 7.86 us -> 10.4 us
    unnamed x18 -> x0, local copies, waits for them, and re-layouts: 5.21 us -> none
    ppermute x6, waiting for transfers between devices: 8.94 us -> 4.06 us  [shift(): lax.ppermute(value, 'expert', [(i, (i + by) % experts) for i in range(exp...]
    pallas_call x5, Pallas kernels: 7.86 us -> 10.4 us  [call(): pl.pallas_call(body, out_shape=shapes, in_specs=specs or [IN_VMEM] * len(...]
  transfers between devices with their start and end apart: 10 -> 10, of which waited for: 6 -> 3; matrix products, arithmetic and copies ran while one was open for 0% -> 0% of each run, Pallas kernels for 13% -> 18%
where the time goes in v2:
time: 29.1 us; the launch traced here: 28.9 us
  starting transfers between devices  13.7 us (47%)
  Pallas kernels  10.4 us (36%)
  waiting for transfers between devices  4.07 us (14%)
  between operations  0.71 us (2%)
    ppermute x6, starting transfers between devices, shift(): lax.ppermute(value, 'expert', [(i, (i + by) % experts) for i in range(exp...  12.6 us
    pallas_call x5, Pallas kernels, call(): pl.pallas_call(body, out_shape=shapes, in_specs=specs or [IN_VMEM] * len(...  10.4 us
    ppermute x6, waiting for transfers between devices, shift(): lax.ppermute(value, 'expert', [(i, (i + by) % experts) for i in range(exp...  4.06 us
    ppermute x4, starting transfers between devices, swap_half(): lax.ppermute(value, 'half', [(i, (i + 1) % halves) for i in range(halves)])  1.1 us
  transfers between devices with their start and end apart: 10, of which 3 were waited for; matrix products, arithmetic and copies ran while one was open for 0% of the time, Pallas kernels for 18%

profile of v2, /device:TPU:0, one launch (start us, length us, event | category | flops | bytes accessed | tf_op | source)
XLA Modules:
  0.0 28.9 jit_solution(9348340762801391531)
XLA Ops:
  0.6 1.4 %shard_map.86 = (bf16[16,2048]{1,0:T(8,128)(2,1)S(1)}, bf16[16,2048]{1,0:T(8,128)(2,1)S(1)}, bf16[16,2048]{1,0:T(8,128)(2,1)S(1)}, bf16[16,2048]{1,0:T(8,128)(2,1)S(1)}, f32[32,16]{1,0:T(8,128)S(1)}) custom-call(bf16[16,2048]{1,0:T(8,128)(2,1)} %bitcast.11, bf16[16,2048]{1,0:T(8,128)(2,1)} %bitcast.12, s32[2,2,8]{2,1,0:T(2,128)} %bitcast.13, f32[2,2,8]{2,1,0:T(2,128)} %bitcast.14), custom_call_target="tpu_custom_call" | custom-call | flops 10000000 | tf_op jit(solution)/shard_map/pallas_call | solution.py:144
  2.1 0.5 %collective-permute-start.3 = (bf16[2048,256]{1,0:T(8,128)(2,1)}, bf16[2048,256]{1,0:T(8,128)(2,1)S(1)}, u32[]{:S(2)}, u32[]{:S(2)}) collective-permute-start(bf16[2048,256]{1,0:T(8,128)(2,1)} %bitcast.15), channel_id=1, source_target_pairs={{0,1},{1,0},{2,3},{3,2},{4,5},{5,4},{6,7},{7,6},{8,9},{9,8},{10,11... | collective-permute-start | bytes 3145736 | tf_op jit(solution)/shard_map/ppermute | solution.py:169
  2.6 0.1 collective-permute-start.4
  2.7 0.4 %collective-permute-start.5 = (bf16[256,2048]{1,0:T(8,128)(2,1)}, bf16[256,2048]{1,0:T(8,128)(2,1)S(1)}, u32[]{:S(2)}, u32[]{:S(2)}) collective-permute-start(bf16[256,2048]{1,0:T(8,128)(2,1)} %bitcast.19), channel_id=1, source_target_pairs={{0,1},{1,0},{2,3},{3,2},{4,5},{5,4},{6,7},{7,6},{8,9},{9,8},{10,11... | collective-permute-start | bytes 3145736 | tf_op jit(solution)/shard_map/ppermute | solution.py:169
  3.1 2.7 %collective-permute-start = (bf16[16,2048]{1,0:T(8,128)(2,1)S(1)}, bf16[16,2048]{1,0:T(8,128)(2,1)S(1)}, u32[]{:S(2)}, u32[]{:S(2)}) collective-permute-start(bf16[16,2048]{1,0:T(8,128)(2,1)S(1)} %get-tuple-element.39), channel_id=1, source_target_pairs={{0,2},{2,4},{4,6},{6,0},{1,3},{3,5},{5,7},{7,1},{8,10},{10,12},{12... | collective-permute-start | bytes 196616 | tf_op jit(solution)/shard_map/ppermute | solution.py:217
  5.7 2.6 %collective-permute-start.1 = (bf16[16,2048]{1,0:T(8,128)(2,1)S(1)}, bf16[16,2048]{1,0:T(8,128)(2,1)S(1)}, u32[]{:S(2)}, u32[]{:S(2)}) collective-permute-start(bf16[16,2048]{1,0:T(8,128)(2,1)S(1)} %get-tuple-element.40), channel_id=1, source_target_pairs={{0,4},{2,6},{4,0},{6,2},{1,5},{3,7},{5,1},{7,3},{8,12},{10,14},{12... | collective-permute-start | bytes 196616 | tf_op jit(solution)/shard_map/ppermute | solution.py:217
  8.3 2.2 %collective-permute-done.refs_1_ = bf16[16,2048]{1,0:T(8,128)(2,1)S(1)} collective-permute-done((bf16[16,2048]{1,0:T(8,128)(2,1)S(1)}, bf16[16,2048]{1,0:T(8,128)(2,1)S(1)}, u32[]{:S(2)}, u32[]{:S(2)}) %collective-permute-start) | collective-permute-done | bytes 65568 | tf_op jit(solution)/shard_map/ppermute | solution.py:217
  10.6 2.5 %collective-permute-start.2 = (bf16[16,2048]{1,0:T(8,128)(2,1)S(1)}, bf16[16,2048]{1,0:T(8,128)(2,1)S(1)}, u32[]{:S(2)}, u32[]{:S(2)}) collective-permute-start(bf16[16,2048]{1,0:T(8,128)(2,1)S(1)} %get-tuple-element.41), channel_id=1, source_target_pairs={{0,6},{2,0},{4,2},{6,4},{1,7},{3,1},{5,3},{7,5},{8,14},{10,8},{12,... | collective-permute-start | bytes 196616 | tf_op jit(solution)/shard_map/ppermute | solution.py:217
  13.1 1.9 %shard_map.87 = (bf16[2048,256]{1,0:T(8,128)(2,1)S(1)}, bf16[2048,256]{1,0:T(8,128)(2,1)S(1)}, bf16[256,2048]{1,0:T(8,128)(2,1)S(1)}, bf16[16,32]{1,0:T(8,128)(2,1)S(1)}) custom-call(f32[32,16]{1,0:T(8,128)S(1)} %get-tuple-element.29.pick_ref, bf16[2048,256]{1,0:T(8,128)(2,1)} %bitcast.16, bf16[2048,256]{1,0:T(8,128)(2,1)} %bitcast.18, ...), custom_call_target="tpu_custom_call" | custom-call | flops 1000000000 | tf_op jit(solution)/shard_map/pallas_call | solution.py:144
  15.0 0.0 collective-permute-done.1.refs_2_
  15.0 0.0 collective-permute-done.2.refs_3_
  15.0 0.0 collective-permute-done.3.refs_7_
  15.0 0.0 collective-permute-done.4.refs_8_
  15.0 0.0 collective-permute-done.5.refs_9_
  15.0 3.1 %shard_map.88 = (bf16[32,2560]{1,0:T(8,128)(2,1)S(1)}, bf16[32,2560]{1,0:T(8,128)(2,1)S(1)}, bf16[8,2048]{1,0:T(8,128)(2,1)S(1)}, bf16[8,2048]{1,0:T(8,128)(2,1)...) custom-call(bf16[16,2048]{1,0:T(8,128)(2,1)S(1)} %get-tuple-element.38.refs_0_, ...), custom_call_target="tpu_custom_call" | custom-call | flops 335544320 | tf_op jit(solution)/shard_map/pallas_call | solution.py:144
  18.2 0.1 collective-permute-start.6
  18.2 4.2 %collective-permute-start.7 = (bf16[8,2048]{1,0:T(8,128)(2,1)S(1)}, bf16[8,2048]{1,0:T(8,128)(2,1)S(1)}, u32[]{:S(2)}, u32[]{:S(2)}) collective-permute-start(bf16[8,2048]{1,0:T(8,128)(2,1)S(1)} %get-tuple-element.48), channel_id=1, source_target_pairs={{0,6},{2,0},{4,2},{6,4},{1,7},{3,1},{5,3},{7,5},{8,14},{10,8},{12,... | collective-permute-start | bytes 98312 | tf_op jit(solution)/shard_map/ppermute | solution.py:217
  22.4 0.0 collective-permute-start.8
  22.4 0.7 %collective-permute-start.9 = (bf16[8,2048]{1,0:T(8,128)(2,1)S(1)}, bf16[8,2048]{1,0:T(8,128)(2,1)S(1)}, u32[]{:S(2)}, u32[]{:S(2)}) collective-permute-start(bf16[8,2048]{1,0:T(8,128)(2,1)S(1)} %get-tuple-element.50), channel_id=1, source_target_pairs={{0,2},{2,4},{4,6},{6,0},{1,3},{3,5},{5,7},{7,1},{8,10},{10,12},{12... | collective-permute-start | bytes 98312 | tf_op jit(solution)/shard_map/ppermute | solution.py:217
  23.1 0.0 collective-permute-done.6.theirs_ref
  23.1 3.3 %shard_map.89 = bf16[256,2048]{1,0:T(8,128)(2,1)} custom-call(bf16[32,2560]{1,0:T(8,128)(2,1)S(1)} %get-tuple-element.45.mine_ref, bf16[32,2560]{1,0:T(8,128)(2,1)S(1)} %collective-permute-done.6.theirs_ref), custom_call_target="tpu_custom_call" | custom-call | flops 268435456 | tf_op jit(solution)/shard_map/pallas_call | solution.py:144
  26.3 0.0 collective-permute-done.7.refs_1_
  26.3 1.2 %collective-permute-done.8.refs_2_ = bf16[8,2048]{1,0:T(8,128)(2,1)S(1)} collective-permute-done((bf16[8,2048]{1,0:T(8,128)(2,1)S(1)}, bf16[8,2048]{1,0:T(8,128)(2,1)S(1)}, u32[]{:S(2)}, u32[]{:S(2)}) %collective-permute-start.8) | collective-permute-done | bytes 32800 | tf_op jit(solution)/shard_map/ppermute | solution.py:217
  27.6 0.6 %collective-permute-done.9.refs_3_ = bf16[8,2048]{1,0:T(8,128)(2,1)S(1)} collective-permute-done((bf16[8,2048]{1,0:T(8,128)(2,1)S(1)}, bf16[8,2048]{1,0:T(8,128)(2,1)S(1)}, u32[]{:S(2)}, u32[]{:S(2)}) %collective-permute-start.9) | collective-permute-done | bytes 32800 | tf_op jit(solution)/shard_map/ppermute | solution.py:217
  28.1 0.8 %shard_map.90 = bf16[16,2048]{1,0:T(8,128)(2,1)} custom-call(bf16[16,32]{1,0:T(8,128)(2,1)S(1)} %get-tuple-element.37.pick_ref, bf16[8,2048]{1,0:T(8,128)(2,1)S(1)} %get-tuple-element.51.refs_0_, bf16[8,2048]{1,0:T(8,128)(2,1)S(1)} %collective-permute-done.7.refs_1_, bf16[8,2048]{1,0:T(8,128)(2,1)S(1)} %collective-permute-done.8.refs_2_, ...), custom_call_target="tpu_custom_call" | custom-call | flops 1000000 | tf_op jit(solution)/shard_map/pallas_call | solution.py:144
Async XLA Ops:
  2.1 13.0 %collective-permute-start.3 = (bf16[2048,256]{1,0:T(8,128)(2,1)}, bf16[2048,256]{1,0:T(8,128)(2,1)S(1)}, u32[]{:S(2)}, u32[]{:S(2)}) collective-permute-start(bf16[2048,256]{1,0:T(8,128)(2,1)} %bitcast.15), channel_id=1, source_target_pairs={{0,1},{1,0},{2,3},{3,2},{4,5},{5,4},{6,7},{7,6},{8,9},{9,8},{10,11... | collective-permute-start | bytes 3145736 | tf_op jit(solution)/shard_map/ppermute | solution.py:169
  2.6 12.5 %collective-permute-start.4 = (bf16[2048,256]{1,0:T(8,128)(2,1)}, bf16[2048,256]{1,0:T(8,128)(2,1)S(1)}, u32[]{:S(2)}, u32[]{:S(2)}) collective-permute-start(bf16[2048,256]{1,0:T(8,128)(2,1)} %bitcast.17), channel_id=1, source_target_pairs={{0,1},{1,0},{2,3},{3,2},{4,5},{5,4},{6,7},{7,6},{8,9},{9,8},{10,11... | collective-permute-start | bytes 3145736 | tf_op jit(solution)/shard_map/ppermute | solution.py:169
  2.7 12.4 %collective-permute-start.5 = (bf16[256,2048]{1,0:T(8,128)(2,1)}, bf16[256,2048]{1,0:T(8,128)(2,1)S(1)}, u32[]{:S(2)}, u32[]{:S(2)}) collective-permute-start(bf16[256,2048]{1,0:T(8,128)(2,1)} %bitcast.19), channel_id=1, source_target_pairs={{0,1},{1,0},{2,3},{3,2},{4,5},{5,4},{6,7},{7,6},{8,9},{9,8},{10,11... | collective-permute-start | bytes 3145736 | tf_op jit(solution)/shard_map/ppermute | solution.py:169
  3.1 7.5 %collective-permute-start = (bf16[16,2048]{1,0:T(8,128)(2,1)S(1)}, bf16[16,2048]{1,0:T(8,128)(2,1)S(1)}, u32[]{:S(2)}, u32[]{:S(2)}) collective-permute-start(bf16[16,2048]{1,0:T(8,128)(2,1)S(1)} %get-tuple-element.39), channel_id=1, source_target_pairs={{0,2},{2,4},{4,6},{6,0},{1,3},{3,5},{5,7},{7,1},{8,10},{10,12},{12... | collective-permute-start | bytes 196616 | tf_op jit(solution)/shard_map/ppermute | solution.py:217
  5.7 9.3 %collective-permute-start.1 = (bf16[16,2048]{1,0:T(8,128)(2,1)S(1)}, bf16[16,2048]{1,0:T(8,128)(2,1)S(1)}, u32[]{:S(2)}, u32[]{:S(2)}) collective-permute-start(bf16[16,2048]{1,0:T(8,128)(2,1)S(1)} %get-tuple-element.40), channel_id=1, source_target_pairs={{0,4},{2,6},{4,0},{6,2},{1,5},{3,7},{5,1},{7,3},{8,12},{10,14},{12... | collective-permute-start | bytes 196616 | tf_op jit(solution)/shard_map/ppermute | solution.py:217
  10.6 4.4 %collective-permute-start.2 = (bf16[16,2048]{1,0:T(8,128)(2,1)S(1)}, bf16[16,2048]{1,0:T(8,128)(2,1)S(1)}, u32[]{:S(2)}, u32[]{:S(2)}) collective-permute-start(bf16[16,2048]{1,0:T(8,128)(2,1)S(1)} %get-tuple-element.41), channel_id=1, source_target_pairs={{0,6},{2,0},{4,2},{6,4},{1,7},{3,1},{5,3},{7,5},{8,14},{10,8},{12,... | collective-permute-start | bytes 196616 | tf_op jit(solution)/shard_map/ppermute | solution.py:217
  18.2 4.9 %collective-permute-start.6 = (bf16[32,2560]{1,0:T(8,128)(2,1)S(1)}, bf16[32,2560]{1,0:T(8,128)(2,1)S(1)}, u32[]{:S(2)}, u32[]{:S(2)}) collective-permute-start(bf16[32,2560]{1,0:T(8,128)(2,1)S(1)} %get-tuple-element.46), channel_id=1, source_target_pairs={{0,1},{1,0},{2,3},{3,2},{4,5},{5,4},{6,7},{7,6},{8,9},{9,8},{10,11... | collective-permute-start | bytes 491528 | tf_op jit(solution)/shard_map/ppermute | solution.py:169
  18.2 8.1 %collective-permute-start.7 = (bf16[8,2048]{1,0:T(8,128)(2,1)S(1)}, bf16[8,2048]{1,0:T(8,128)(2,1)S(1)}, u32[]{:S(2)}, u32[]{:S(2)}) collective-permute-start(bf16[8,2048]{1,0:T(8,128)(2,1)S(1)} %get-tuple-element.48), channel_id=1, source_target_pairs={{0,6},{2,0},{4,2},{6,4},{1,7},{3,1},{5,3},{7,5},{8,14},{10,8},{12,... | collective-permute-start | bytes 98312 | tf_op jit(solution)/shard_map/ppermute | solution.py:217
  22.4 5.2 %collective-permute-start.8 = (bf16[8,2048]{1,0:T(8,128)(2,1)S(1)}, bf16[8,2048]{1,0:T(8,128)(2,1)S(1)}, u32[]{:S(2)}, u32[]{:S(2)}) collective-permute-start(bf16[8,2048]{1,0:T(8,128)(2,1)S(1)} %get-tuple-element.49), channel_id=1, source_target_pairs={{0,4},{2,6},{4,0},{6,2},{1,5},{3,7},{5,1},{7,3},{8,12},{10,14},{12... | collective-permute-start | bytes 98312 | tf_op jit(solution)/shard_map/ppermute | solution.py:217
  22.4 5.7 %collective-permute-start.9 = (bf16[8,2048]{1,0:T(8,128)(2,1)S(1)}, bf16[8,2048]{1,0:T(8,128)(2,1)S(1)}, u32[]{:S(2)}, u32[]{:S(2)}) collective-permute-start(bf16[8,2048]{1,0:T(8,128)(2,1)S(1)} %get-tuple-element.50), channel_id=1, source_target_pairs={{0,2},{2,4},{4,6},{6,0},{1,3},{3,5},{5,7},{7,1},{8,10},{10,12},{12... | collective-permute-start | bytes 98312 | tf_op jit(solution)/shard_map/ppermute | solution.py:217

commit v3 on v2

--- a/solution.py
+++ b/solution.py
@@ -81,7 +81,7 @@
 
 def forward_values(x_rows, weights):
     hidden, active, slope = [], [], []
-    for gate, up in weights:
+    for gate, up, _ in weights:
         pre_gate = plain(x_rows, gate)
         pre_up = plain(x_rows, up)
         sigmoid = 1.0 / (1.0 + jnp.exp(-pre_gate))
@@ -95,7 +95,11 @@
 def backward_values(s_rows, active, slope, weights):
     total = None
     for activated, steep, (gate, up, down) in zip(active, slope, weights):
-        hidden_grad = contract_last(s_rows, down)
+        wide = s_rows.shape[1] // len(down)
+        hidden_grad = sum(
+            contract_last(s_rows[:, c * wide : (c + 1) * wide], block)
+            for c, block in enumerate(down)
+        )
         gate_grad = (hidden_grad * steep).astype(BF16)
         up_grad = (hidden_grad * activated).astype(BF16)
         piece = contract_last(gate_grad, gate) + contract_last(up_grad, up)
@@ -177,6 +181,8 @@
     slots = experts * block
     units = own[0].shape[1]
 
+    far = [swap_half(w) for w in own]
+
     def dispatch_body(x_hbm, u_hbm, routes_hbm, gates_hbm, *refs):
         *outs, pick_ref, data, routes_ref, gates_ref, sems = refs
         copies = [
@@ -218,9 +224,8 @@
             value, "expert", [(i, (i + by) % experts) for i in range(experts)]
         )
 
-    held, blocks = lax.optimization_barrier((own, blocks))
+    blocks[-1], far[0] = lax.optimization_barrier((blocks[-1], far[0]))
     got = [blocks[0]] + [shift(blocks[d], d) for d in range(1, experts)]
-    other = [swap_half(w) for w in held]
 
     def fetch_body(pick_ref, *refs):
         ins, outs, sems = refs[:3], refs[3:6], refs[7]
@@ -234,17 +239,18 @@
     *near, pick = call(
         fetch_body,
         [kept(w.shape, BF16) for w in own] + [kept((rows, slots), BF16)],
-        [vmem(pick)] + [hbm(w) for w in held],
+        [vmem(pick)] + [hbm(w) for w in own],
         10**9,
         specs=[IN_VMEM] + [IN_HBM] * 3,
         scratch=[pltpu.SemaphoreType.DMA((3,))],
     )
 
     def expert_body(*refs):
-        weights = [tuple(r[...] for r in refs[experts + 3 * i :][:3]) for i in range(2)]
+        held = [r[...] for r in refs[experts : experts + 6]]
+        weights = [(*held[:2], [held[2]]), (*held[3:5], [held[5]])]
         to_other, mine, *outs = refs[experts + 6 :]
         x_rows, s_rows = pairs(refs[:experts])
-        hidden, active, slope = forward_values(x_rows, [w[:2] for w in weights])
+        hidden, active, slope = forward_values(x_rows, weights)
         to_other[:, :units] = hidden[1]
         to_other[:, units : 2 * units] = hidden[0]
         to_other[:, 2 * units :] = s_rows
@@ -258,7 +264,7 @@
     to_other, mine, *grads = call(
         expert_body,
         [kept((slots, 2 * units + width), BF16)] * 2 + [kept((block, width), BF16)] * experts,
-        [vmem(v) for v in (*got, *near, *other)],
+        [vmem(v) for v in (*got, *near, *far)],
         2 * slots * width * units * 10,
     )
     back = [grads[0]] + [shift(grads[d], experts - d) for d in range(1, experts)]
@@ -302,15 +308,15 @@
     sent, pick = route_rows(
         jnp.concatenate([activations, upstream], axis=0), routes, gates, 0, experts, capacity
     )
-    other = [swap_half(w) for w in own]
+    weights = [(*w[:2], [w[2]]) for w in (own, [swap_half(w) for w in own])]
     sent = sent.astype(BF16).reshape(experts, 2 * block, width)
     got = lax.all_to_all(sent, "expert", split_axis=0, concat_axis=0, tiled=True)
     x_rows = got[:, :block].reshape(slots, width)
     s_rows = got[:, block:].reshape(slots, width)
-    hidden, active, slope = forward_values(x_rows, [own[:2], other[:2]])
+    hidden, active, slope = forward_values(x_rows, weights)
     theirs = swap_half(jnp.concatenate([hidden[1], hidden[0], s_rows], axis=1))
     mine = jnp.concatenate([hidden[0], hidden[1], s_rows], axis=1)
-    total = backward_values(s_rows, active, slope, [own, other])
+    total = backward_values(s_rows, active, slope, weights)
     total = total.astype(BF16).reshape(experts, block, width)
     back = lax.all_to_all(total, "expert", split_axis=0, concat_axis=0, tiled=True)
     cotangent = dot(pick.astype(BF16), back.reshape(slots, width), ((0,), (0,))).astype(BF16)

time: 29.1 us -> 26.6 us (0.914)
  starting transfers between devices: 13.7 us -> 11.2 us
    ppermute x6, starting transfers between devices: 12.6 us -> 10.1 us  [shift(): lax.ppermute(value, 'expert', [(i, (i + by) % experts) for i in range(exp...]
  transfers between devices with their start and end apart: 10 -> 10, of which waited for: 3 -> 4; matrix products, arithmetic and copies ran while one was open for 0% -> 0% of each run, Pallas kernels for 18% -> 25%
where the time goes in v3:
time: 26.6 us; the launch traced here: 26.5 us
  starting transfers between devices  11.2 us (42%)
  Pallas kernels  10.4 us (39%)
  waiting for transfers between devices  4.21 us (16%)
  between operations  0.68 us (3%)
    pallas_call x5, Pallas kernels, call(): pl.pallas_call(body, out_shape=shapes, in_specs=specs or [IN_VMEM] * len(...  10.4 us
    ppermute x6, starting transfers between devices, shift(): lax.ppermute(value, 'expert', [(i, (i + by) % experts) for i in range(exp...  10.1 us
    ppermute x6, waiting for transfers between devices, shift(): lax.ppermute(value, 'expert', [(i, (i + by) % experts) for i in range(exp...  4.2 us
    ppermute x4, starting transfers between devices, swap_half(): lax.ppermute(value, 'half', [(i, (i + 1) % halves) for i in range(halves)])  1.1 us
  transfers between devices with their start and end apart: 10, of which 4 were waited for; matrix products, arithmetic and copies ran while one was open for 0% of the time, Pallas kernels for 25%

profile of v3, /device:TPU:0, one launch (start us, length us, event | category | flops | bytes accessed | tf_op | source)
XLA Modules:
  0.0 26.5 jit_solution(17344680873438976652)
XLA Ops:
  0.6 0.5 %collective-permute-start.2 = (bf16[2048,256]{1,0:T(8,128)(2,1)}, bf16[2048,256]{1,0:T(8,128)(2,1)S(1)}, u32[]{:S(2)}, u32[]{:S(2)}) collective-permute-start(bf16[2048,256]{1,0:T(8,128)(2,1)} %bitcast.15), channel_id=1, source_target_pairs={{0,1},{1,0},{2,3},{3,2},{4,5},{5,4},{6,7},{7,6},{8,9},{9,8},{10,11... | collective-permute-start | bytes 3145736 | tf_op jit(solution)/shard_map/ppermute | solution.py:173
  1.1 0.1 collective-permute-start.4
  1.2 0.4 %collective-permute-start.5 = (bf16[256,2048]{1,0:T(8,128)(2,1)}, bf16[256,2048]{1,0:T(8,128)(2,1)S(1)}, u32[]{:S(2)}, u32[]{:S(2)}) collective-permute-start(bf16[256,2048]{1,0:T(8,128)(2,1)} %bitcast.19), channel_id=1, source_target_pairs={{0,1},{1,0},{2,3},{3,2},{4,5},{5,4},{6,7},{7,6},{8,9},{9,8},{10,11... | collective-permute-start | bytes 3145736 | tf_op jit(solution)/shard_map/ppermute | solution.py:173
  1.7 1.4 %shard_map.86 = (bf16[16,2048]{1,0:T(8,128)(2,1)S(1)}, bf16[16,2048]{1,0:T(8,128)(2,1)S(1)}, bf16[16,2048]{1,0:T(8,128)(2,1)S(1)}, bf16[16,2048]{1,0:T(8,128)(2,1)S(1)}, f32[32,16]{1,0:T(8,128)S(1)}) custom-call(bf16[16,2048]{1,0:T(8,128)(2,1)} %bitcast.11, bf16[16,2048]{1,0:T(8,128)(2,1)} %bitcast.12, s32[2,2,8]{2,1,0:T(2,128)} %bitcast.13, f32[2,2,8]{2,1,0:T(2,128)} %bitcast.14), custom_call_target="tpu_custom_call" | custom-call | flops 10000000 | tf_op jit(solution)/shard_map/pallas_call | solution.py:148
  3.1 2.7 %collective-permute-start = (bf16[16,2048]{1,0:T(8,128)(2,1)S(1)}, bf16[16,2048]{1,0:T(8,128)(2,1)S(1)}, u32[]{:S(2)}, u32[]{:S(2)}) collective-permute-start(bf16[16,2048]{1,0:T(8,128)(2,1)S(1)} %get-tuple-element.27), channel_id=1, source_target_pairs={{0,2},{2,4},{4,6},{6,0},{1,3},{3,5},{5,7},{7,1},{8,10},{10,12},{12... | collective-permute-start | bytes 196616 | tf_op jit(solution)/shard_map/ppermute | solution.py:223
  5.8 2.6 %collective-permute-start.1 = (bf16[16,2048]{1,0:T(8,128)(2,1)S(1)}, bf16[16,2048]{1,0:T(8,128)(2,1)S(1)}, u32[]{:S(2)}, u32[]{:S(2)}) collective-permute-start(bf16[16,2048]{1,0:T(8,128)(2,1)S(1)} %get-tuple-element.28), channel_id=1, source_target_pairs={{0,4},{2,6},{4,0},{6,2},{1,5},{3,7},{5,1},{7,3},{8,12},{10,14},{12... | collective-permute-start | bytes 196616 | tf_op jit(solution)/shard_map/ppermute | solution.py:223
  8.4 0.0 collective-permute-done.2.refs_7_
  8.4 1.3 %collective-permute-start.3 = (bf16[16,2048]{1,0:T(8,128)(2,1)S(1)}, bf16[16,2048]{1,0:T(8,128)(2,1)S(1)}, u32[]{:S(2)}, u32[]{:S(2)}) collective-permute-start(bf16[16,2048]{1,0:T(8,128)(2,1)S(1)} %get-tuple-element.30), channel_id=1, source_target_pairs={{0,6},{2,0},{4,2},{6,4},{1,7},{3,1},{5,3},{7,5},{8,14},{10,8},{12,... | collective-permute-start | bytes 196616 | tf_op jit(solution)/shard_map/ppermute | solution.py:223
  9.7 1.9 %shard_map.87 = (bf16[2048,256]{1,0:T(8,128)(2,1)S(1)}, bf16[2048,256]{1,0:T(8,128)(2,1)S(1)}, bf16[256,2048]{1,0:T(8,128)(2,1)S(1)}, bf16[16,32]{1,0:T(8,128)(2,1)S(1)}) custom-call(f32[32,16]{1,0:T(8,128)S(1)} %get-tuple-element.24.pick_ref, bf16[2048,256]{1,0:T(8,128)(2,1)} %bitcast.16, bf16[2048,256]{1,0:T(8,128)(2,1)} %bitcast.18, ...), custom_call_target="tpu_custom_call" | custom-call | flops 1000000000 | tf_op jit(solution)/shard_map/pallas_call | solution.py:148
  11.6 0.0 collective-permute-done.refs_1_
  11.6 1.8 %collective-permute-done.1.refs_2_ = bf16[16,2048]{1,0:T(8,128)(2,1)S(1)} collective-permute-done((bf16[16,2048]{1,0:T(8,128)(2,1)S(1)}, bf16[16,2048]{1,0:T(8,128)(2,1)S(1)}, u32[]{:S(2)}, u32[]{:S(2)}) %collective-permute-start.1) | collective-permute-done | bytes 65568 | tf_op jit(solution)/shard_map/ppermute | solution.py:223
  13.4 0.0 collective-permute-done.4.refs_8_
  13.4 0.0 collective-permute-done.5.refs_9_
  13.4 0.2 collective-permute-done.3.refs_3_
  13.7 3.1 %shard_map.88 = (bf16[32,2560]{1,0:T(8,128)(2,1)S(1)}, bf16[32,2560]{1,0:T(8,128)(2,1)S(1)}, bf16[8,2048]{1,0:T(8,128)(2,1)S(1)}, bf16[8,2048]{1,0:T(8,128)(2,1)...) custom-call(bf16[16,2048]{1,0:T(8,128)(2,1)S(1)} %get-tuple-element.26.refs_0_, ...), custom_call_target="tpu_custom_call" | custom-call | flops 335544320 | tf_op jit(solution)/shard_map/pallas_call | solution.py:148
  16.8 0.1 collective-permute-start.6
  16.8 2.8 %collective-permute-start.7 = (bf16[8,2048]{1,0:T(8,128)(2,1)S(1)}, bf16[8,2048]{1,0:T(8,128)(2,1)S(1)}, u32[]{:S(2)}, u32[]{:S(2)}) collective-permute-start(bf16[8,2048]{1,0:T(8,128)(2,1)S(1)} %get-tuple-element.38), channel_id=1, source_target_pairs={{0,6},{2,0},{4,2},{6,4},{1,7},{3,1},{5,3},{7,5},{8,14},{10,8},{12,... | collective-permute-start | bytes 98312 | tf_op jit(solution)/shard_map/ppermute | solution.py:223
  19.6 0.4 %collective-permute-start.8 = (bf16[8,2048]{1,0:T(8,128)(2,1)S(1)}, bf16[8,2048]{1,0:T(8,128)(2,1)S(1)}, u32[]{:S(2)}, u32[]{:S(2)}) collective-permute-start(bf16[8,2048]{1,0:T(8,128)(2,1)S(1)} %get-tuple-element.39), channel_id=1, source_target_pairs={{0,4},{2,6},{4,0},{6,2},{1,5},{3,7},{5,1},{7,3},{8,12},{10,14},{12... | collective-permute-start | bytes 98312 | tf_op jit(solution)/shard_map/ppermute | solution.py:223
  20.0 0.3 %collective-permute-start.9 = (bf16[8,2048]{1,0:T(8,128)(2,1)S(1)}, bf16[8,2048]{1,0:T(8,128)(2,1)S(1)}, u32[]{:S(2)}, u32[]{:S(2)}) collective-permute-start(bf16[8,2048]{1,0:T(8,128)(2,1)S(1)} %get-tuple-element.40), channel_id=1, source_target_pairs={{0,2},{2,4},{4,6},{6,0},{1,3},{3,5},{5,7},{7,1},{8,10},{10,12},{12... | collective-permute-start | bytes 98312 | tf_op jit(solution)/shard_map/ppermute | solution.py:223
  20.3 0.0 collective-permute-done.6.theirs_ref
  20.3 3.3 %shard_map.89 = bf16[256,2048]{1,0:T(8,128)(2,1)} custom-call(bf16[32,2560]{1,0:T(8,128)(2,1)S(1)} %get-tuple-element.35.mine_ref, bf16[32,2560]{1,0:T(8,128)(2,1)S(1)} %collective-permute-done.6.theirs_ref), custom_call_target="tpu_custom_call" | custom-call | flops 268435456 | tf_op jit(solution)/shard_map/pallas_call | solution.py:148
  23.5 0.0 collective-permute-done.7.refs_1_
  23.5 1.2 %collective-permute-done.8.refs_2_ = bf16[8,2048]{1,0:T(8,128)(2,1)S(1)} collective-permute-done((bf16[8,2048]{1,0:T(8,128)(2,1)S(1)}, bf16[8,2048]{1,0:T(8,128)(2,1)S(1)}, u32[]{:S(2)}, u32[]{:S(2)}) %collective-permute-start.8) | collective-permute-done | bytes 32800 | tf_op jit(solution)/shard_map/ppermute | solution.py:223
  24.8 0.9 %collective-permute-done.9.refs_3_ = bf16[8,2048]{1,0:T(8,128)(2,1)S(1)} collective-permute-done((bf16[8,2048]{1,0:T(8,128)(2,1)S(1)}, bf16[8,2048]{1,0:T(8,128)(2,1)S(1)}, u32[]{:S(2)}, u32[]{:S(2)}) %collective-permute-start.9) | collective-permute-done | bytes 32800 | tf_op jit(solution)/shard_map/ppermute | solution.py:223
  25.7 0.8 %shard_map.90 = bf16[16,2048]{1,0:T(8,128)(2,1)} custom-call(bf16[16,32]{1,0:T(8,128)(2,1)S(1)} %get-tuple-element.25.pick_ref, bf16[8,2048]{1,0:T(8,128)(2,1)S(1)} %get-tuple-element.41.refs_0_, bf16[8,2048]{1,0:T(8,128)(2,1)S(1)} %collective-permute-done.7.refs_1_, bf16[8,2048]{1,0:T(8,128)(2,1)S(1)} %collective-permute-done.8.refs_2_, ...), custom_call_target="tpu_custom_call" | custom-call | flops 1000000 | tf_op jit(solution)/shard_map/pallas_call | solution.py:148
Async XLA Ops:
  0.6 7.7 %collective-permute-start.2 = (bf16[2048,256]{1,0:T(8,128)(2,1)}, bf16[2048,256]{1,0:T(8,128)(2,1)S(1)}, u32[]{:S(2)}, u32[]{:S(2)}) collective-permute-start(bf16[2048,256]{1,0:T(8,128)(2,1)} %bitcast.15), channel_id=1, source_target_pairs={{0,1},{1,0},{2,3},{3,2},{4,5},{5,4},{6,7},{7,6},{8,9},{9,8},{10,11... | collective-permute-start | bytes 3145736 | tf_op jit(solution)/shard_map/ppermute | solution.py:173
  1.1 12.3 %collective-permute-start.4 = (bf16[2048,256]{1,0:T(8,128)(2,1)}, bf16[2048,256]{1,0:T(8,128)(2,1)S(1)}, u32[]{:S(2)}, u32[]{:S(2)}) collective-permute-start(bf16[2048,256]{1,0:T(8,128)(2,1)} %bitcast.17), channel_id=1, source_target_pairs={{0,1},{1,0},{2,3},{3,2},{4,5},{5,4},{6,7},{7,6},{8,9},{9,8},{10,11... | collective-permute-start | bytes 3145736 | tf_op jit(solution)/shard_map/ppermute | solution.py:173
  1.2 12.2 %collective-permute-start.5 = (bf16[256,2048]{1,0:T(8,128)(2,1)}, bf16[256,2048]{1,0:T(8,128)(2,1)S(1)}, u32[]{:S(2)}, u32[]{:S(2)}) collective-permute-start(bf16[256,2048]{1,0:T(8,128)(2,1)} %bitcast.19), channel_id=1, source_target_pairs={{0,1},{1,0},{2,3},{3,2},{4,5},{5,4},{6,7},{7,6},{8,9},{9,8},{10,11... | collective-permute-start | bytes 3145736 | tf_op jit(solution)/shard_map/ppermute | solution.py:173
  3.1 8.5 %collective-permute-start = (bf16[16,2048]{1,0:T(8,128)(2,1)S(1)}, bf16[16,2048]{1,0:T(8,128)(2,1)S(1)}, u32[]{:S(2)}, u32[]{:S(2)}) collective-permute-start(bf16[16,2048]{1,0:T(8,128)(2,1)S(1)} %get-tuple-element.27), channel_id=1, source_target_pairs={{0,2},{2,4},{4,6},{6,0},{1,3},{3,5},{5,7},{7,1},{8,10},{10,12},{12... | collective-permute-start | bytes 196616 | tf_op jit(solution)/shard_map/ppermute | solution.py:223
  5.8 7.6 %collective-permute-start.1 = (bf16[16,2048]{1,0:T(8,128)(2,1)S(1)}, bf16[16,2048]{1,0:T(8,128)(2,1)S(1)}, u32[]{:S(2)}, u32[]{:S(2)}) collective-permute-start(bf16[16,2048]{1,0:T(8,128)(2,1)S(1)} %get-tuple-element.28), channel_id=1, source_target_pairs={{0,4},{2,6},{4,0},{6,2},{1,5},{3,7},{5,1},{7,3},{8,12},{10,14},{12... | collective-permute-start | bytes 196616 | tf_op jit(solution)/shard_map/ppermute | solution.py:223
  8.4 5.3 %collective-permute-start.3 = (bf16[16,2048]{1,0:T(8,128)(2,1)S(1)}, bf16[16,2048]{1,0:T(8,128)(2,1)S(1)}, u32[]{:S(2)}, u32[]{:S(2)}) collective-permute-start(bf16[16,2048]{1,0:T(8,128)(2,1)S(1)} %get-tuple-element.30), channel_id=1, source_target_pairs={{0,6},{2,0},{4,2},{6,4},{1,7},{3,1},{5,3},{7,5},{8,14},{10,8},{12,... | collective-permute-start | bytes 196616 | tf_op jit(solution)/shard_map/ppermute | solution.py:223
  16.8 3.5 %collective-permute-start.6 = (bf16[32,2560]{1,0:T(8,128)(2,1)S(1)}, bf16[32,2560]{1,0:T(8,128)(2,1)S(1)}, u32[]{:S(2)}, u32[]{:S(2)}) collective-permute-start(bf16[32,2560]{1,0:T(8,128)(2,1)S(1)} %get-tuple-element.36), channel_id=1, source_target_pairs={{0,1},{1,0},{2,3},{3,2},{4,5},{5,4},{6,7},{7,6},{8,9},{9,8},{10,11... | collective-permute-start | bytes 491528 | tf_op jit(solution)/shard_map/ppermute | solution.py:173
  16.8 6.7 %collective-permute-start.7 = (bf16[8,2048]{1,0:T(8,128)(2,1)S(1)}, bf16[8,2048]{1,0:T(8,128)(2,1)S(1)}, u32[]{:S(2)}, u32[]{:S(2)}) collective-permute-start(bf16[8,2048]{1,0:T(8,128)(2,1)S(1)} %get-tuple-element.38), channel_id=1, source_target_pairs={{0,6},{2,0},{4,2},{6,4},{1,7},{3,1},{5,3},{7,5},{8,14},{10,8},{12,... | collective-permute-start | bytes 98312 | tf_op jit(solution)/shard_map/ppermute | solution.py:223
  19.6 5.2 %collective-permute-start.8 = (bf16[8,2048]{1,0:T(8,128)(2,1)S(1)}, bf16[8,2048]{1,0:T(8,128)(2,1)S(1)}, u32[]{:S(2)}, u32[]{:S(2)}) collective-permute-start(bf16[8,2048]{1,0:T(8,128)(2,1)S(1)} %get-tuple-element.39), channel_id=1, source_target_pairs={{0,4},{2,6},{4,0},{6,2},{1,5},{3,7},{5,1},{7,3},{8,12},{10,14},{12... | collective-permute-start | bytes 98312 | tf_op jit(solution)/shard_map/ppermute | solution.py:223
  20.0 5.7 %collective-permute-start.9 = (bf16[8,2048]{1,0:T(8,128)(2,1)S(1)}, bf16[8,2048]{1,0:T(8,128)(2,1)S(1)}, u32[]{:S(2)}, u32[]{:S(2)}) collective-permute-start(bf16[8,2048]{1,0:T(8,128)(2,1)S(1)} %get-tuple-element.40), channel_id=1, source_target_pairs={{0,2},{2,4},{4,6},{6,0},{1,3},{3,5},{5,7},{7,1},{8,10},{10,12},{12... | collective-permute-start | bytes 98312 | tf_op jit(solution)/shard_map/ppermute | solution.py:223

commit v4 on v3

--- a/solution.py
+++ b/solution.py
@@ -10,6 +10,7 @@
 
 ITERS = 2
 MAX_PERMUTED = 8
+CHUNKS = 4
 
 linear_term = 3.4445
 cubic_term = -4.775
@@ -81,7 +82,7 @@
 
 def forward_values(x_rows, weights):
     hidden, active, slope = [], [], []
-    for gate, up, _ in weights:
+    for gate, up, *_ in weights:
         pre_gate = plain(x_rows, gate)
         pre_up = plain(x_rows, up)
         sigmoid = 1.0 / (1.0 + jnp.exp(-pre_gate))
@@ -94,23 +95,40 @@
 
 def backward_values(s_rows, active, slope, weights):
     total = None
-    for activated, steep, (gate, up, down) in zip(active, slope, weights):
-        wide = s_rows.shape[1] // len(down)
-        hidden_grad = sum(
-            contract_last(s_rows[:, c * wide : (c + 1) * wide], block)
-            for c, block in enumerate(down)
-        )
+    for activated, steep, (_, _, gate_turned, up_turned, down_turned) in zip(
+        active, slope, weights
+    ):
+        hidden_grad = plain(s_rows, down_turned)
         gate_grad = (hidden_grad * steep).astype(BF16)
         up_grad = (hidden_grad * activated).astype(BF16)
-        piece = contract_last(gate_grad, gate) + contract_last(up_grad, up)
+        piece = plain(gate_grad, gate_turned) + plain(up_grad, up_turned)
         piece = piece.astype(BF16).astype(F32)
         total = piece if total is None else total + piece
     return total
 
 
-def polynomial_core(scaled, hidden, width, own):
-    exact = lax.Precision.HIGHEST
+def parts_of(value, count):
+    parts = []
+    for _ in range(count):
+        part = value.astype(BF16)
+        parts.append(part)
+        value = value - part.astype(F32)
+    return parts
+
+
+def product(left, right, count):
+    terms = [
+        plain(l, r)
+        for i, l in enumerate(left)
+        for j, r in enumerate(right)
+        if i + j < count
+    ]
+    return sum(terms[1:], terms[0])
+
+
+def polynomial_core(scaled, hidden, units, width):
     rows = scaled.shape[0]
+    own = jnp.transpose(hidden[:, :units].astype(F32)).astype(BF16)
     left = contract_last(scaled, scaled)
     right = contract_last(hidden, hidden)
     squares = jnp.maximum(jnp.sum(left * right), 0.0)
@@ -118,18 +136,23 @@
     row = lax.broadcasted_iota(jnp.int32, (rows, rows), 0)
     col = lax.broadcasted_iota(jnp.int32, (rows, rows), 1)
     eye = jnp.where(row == col, linear_term, 0.0)
-    moment = plain(left * inverse, right * inverse, exact)
-    core = None
+    moment = product(parts_of(left * inverse, 3), parts_of(right * inverse, 3), 3)
+    mixed = [own]
     for iteration in range(ITERS):
-        factor = eye + cubic_term * moment + quintic_term * plain(moment, moment, exact)
-        core = factor if core is None else plain(factor, core, exact)
-        if iteration < ITERS - 1:
-            moment = plain(plain(moment, factor, exact), factor, exact)
-    core = core * (inverse * math.sqrt(width))
-    mixed = dot(core, own.astype(F32), ((0,), (0,)), exact)
-    high = mixed.astype(BF16).astype(F32)
-    stacked = jnp.transpose(jnp.concatenate([high, mixed - high], axis=0)).astype(BF16)
-    return plain(stacked, jnp.concatenate([scaled, scaled], axis=0)).astype(BF16)
+        halves = parts_of(moment, 2)
+        if iteration == ITERS - 1:
+            once = product(mixed, halves, 2)
+            twice = product(parts_of(once, 2), halves, 2)
+            mixed = linear_term * sum(m.astype(F32) for m in mixed)
+            mixed = mixed + cubic_term * once + quintic_term * twice
+        else:
+            factor = eye + cubic_term * moment + quintic_term * product(halves, halves, 2)
+            factor = parts_of(factor, 2)
+            mixed = parts_of(product(mixed, factor, 2), 2)
+            moment = product(parts_of(product(halves, factor, 2), 2), factor, 2)
+    high, low = parts_of(mixed * (inverse * math.sqrt(width)), 2)
+    both = jnp.concatenate([high.astype(F32), low.astype(F32)], axis=1).astype(BF16)
+    return both, jnp.concatenate([scaled, scaled], axis=0)
 
 
 def vmem(value):
@@ -227,28 +250,39 @@
     blocks[-1], far[0] = lax.optimization_barrier((blocks[-1], far[0]))
     got = [blocks[0]] + [shift(blocks[d], d) for d in range(1, experts)]
 
-    def fetch_body(pick_ref, *refs):
-        ins, outs, sems = refs[:3], refs[3:6], refs[7]
-        copies = [pltpu.make_async_copy(ins[i], outs[i], sems.at[i]) for i in range(3)]
+    turned_shapes = [
+        kept((units, width), BF16), kept((units, width), BF16), kept((width, units), BF16)
+    ]
+
+    def prepare_body(pick_ref, *refs):
+        ins, far_refs, (gate, up), near_turned, far_turned, pick_out, down, sems = (
+            refs[:3], refs[3:6], refs[6:8], refs[8:11], refs[11:14], *refs[14:]
+        )
+        held = (gate, up, down)
+        copies = [pltpu.make_async_copy(ins[i], held[i], sems.at[i]) for i in range(3)]
         for copy in copies:
             copy.start()
-        refs[6][...] = jnp.transpose(pick_ref[...]).astype(BF16)
-        for copy in copies:
+        pick_out[...] = jnp.transpose(pick_ref[...]).astype(BF16)
+        for source, to in zip(far_refs, far_turned):
+            to[...] = jnp.transpose(source[...])
+        for copy, source, to in zip(copies, held, near_turned):
             copy.wait()
-
-    *near, pick = call(
-        fetch_body,
-        [kept(w.shape, BF16) for w in own] + [kept((rows, slots), BF16)],
-        [vmem(pick)] + [hbm(w) for w in own],
+            to[...] = jnp.transpose(source[...])
+
+    gate, up, *turned, pick = call(
+        prepare_body,
+        [kept(w.shape, BF16) for w in own[:2]] + turned_shapes * 2 + [kept((rows, slots), BF16)],
+        [vmem(pick)] + [hbm(w) for w in own] + [vmem(w) for w in far],
         10**9,
-        specs=[IN_VMEM] + [IN_HBM] * 3,
-        scratch=[pltpu.SemaphoreType.DMA((3,))],
-    )
+        specs=[IN_VMEM] + [IN_HBM] * 3 + [IN_VMEM] * 3,
+        scratch=[pltpu.VMEM(own[2].shape, BF16), pltpu.SemaphoreType.DMA((3,))],
+    )
+    near, far = [gate, up, *turned[:3]], [*far[:2], *turned[3:]]
 
     def expert_body(*refs):
-        held = [r[...] for r in refs[experts : experts + 6]]
-        weights = [(*held[:2], [held[2]]), (*held[3:5], [held[5]])]
-        to_other, mine, *outs = refs[experts + 6 :]
+        held = [r[...] for r in refs[experts : experts + 10]]
+        weights = [held[:5], held[5:]]
+        to_other, mine, *outs = refs[experts + 10 :]
         x_rows, s_rows = pairs(refs[:experts])
         hidden, active, slope = forward_values(x_rows, weights)
         to_other[:, :units] = hidden[1]
@@ -270,20 +304,37 @@
     back = [grads[0]] + [shift(grads[d], experts - d) for d in range(1, experts)]
     theirs = swap_half(to_other)
 
-    def core_body(mine_ref, theirs_ref, out_ref):
+    chunk = width // CHUNKS
+
+    def core_body(mine_ref, theirs_ref, out_hbm, out_ref, sems):
         both = jnp.concatenate(
             [mine_ref[...].astype(F32), theirs_ref[...].astype(F32)], axis=0
         ).astype(BF16)
-        out_ref[...] = polynomial_core(
-            both[:, 2 * units :], both[:, : 2 * units], max(hidden_units, width), both[:, :units]
+        mixed, rows_twice = polynomial_core(
+            both[:, 2 * units :], both[:, : 2 * units], units, max(hidden_units, width)
         )
-
-    (update,) = call(
+        copies = []
+        for i in range(CHUNKS):
+            cut = slice(i * chunk, (i + 1) * chunk)
+            out_ref[:, cut] = plain(mixed, rows_twice[:, cut]).astype(BF16)
+            copies.append(
+                pltpu.make_async_copy(out_ref.at[:, cut], out_hbm.at[:, cut], sems.at[i])
+            )
+            copies[-1].start()
+        for copy in copies:
+            copy.wait()
+
+    update = pl.pallas_call(
         core_body,
-        [jax.ShapeDtypeStruct((units, width), BF16)],
-        [vmem(mine), vmem(theirs)],
-        2 * 4 * slots * width * units * 2,
-    )
+        out_shape=jax.ShapeDtypeStruct((units, width), BF16),
+        in_specs=[IN_VMEM] * 2,
+        out_specs=IN_HBM,
+        scratch_shapes=[pltpu.VMEM((units, width), BF16), pltpu.SemaphoreType.DMA((CHUNKS,))],
+        compiler_params=pltpu.CompilerParams(vmem_limit_bytes=16 << 20),
+        cost_estimate=pl.CostEstimate(
+            flops=2 * 4 * slots * width * units * 2, bytes_accessed=0, transcendentals=0
+        ),
+    )(vmem(mine), vmem(theirs))
     update, back = lax.optimization_barrier((update, back))
 
     def combine_body(pick_ref, *refs):
@@ -308,7 +359,7 @@
     sent, pick = route_rows(
         jnp.concatenate([activations, upstream], axis=0), routes, gates, 0, experts, capacity
     )
-    weights = [(*w[:2], [w[2]]) for w in (own, [swap_half(w) for w in own])]
+    weights = [(*w[:2], *(m.T for m in w)) for w in (own, [swap_half(w) for w in own])]
     sent = sent.astype(BF16).reshape(experts, 2 * block, width)
     got = lax.all_to_all(sent, "expert", split_axis=0, concat_axis=0, tiled=True)
     x_rows = got[:, :block].reshape(slots, width)
@@ -321,10 +372,10 @@
     back = lax.all_to_all(total, "expert", split_axis=0, concat_axis=0, tiled=True)
     cotangent = dot(pick.astype(BF16), back.reshape(slots, width), ((0,), (0,))).astype(BF16)
     both = jnp.concatenate([mine, theirs], axis=0)
-    update = polynomial_core(
-        both[:, 2 * units :], both[:, : 2 * units], max(hidden_units, width), both[:, :units]
-    )
-    return cotangent, update
+    mixed, rows_twice = polynomial_core(
+        both[:, 2 * units :], both[:, : 2 * units], units, max(hidden_units, width)
+    )
+    return cotangent, plain(mixed, rows_twice).astype(BF16)
 
 
 def on_device(activations, upstream, routes, route_gates, gate_matrix, up_matrix, down_matrix):

time: 26.6 us -> 25.6 us (0.962)
  Pallas kernels: 10.4 us -> 9.57 us
    pallas_call x5 -> x4, Pallas kernels: 10.4 us -> 6.82 us  [call(): pl.pallas_call(body, out_shape=shapes, in_specs=specs or [IN_VMEM] * len(...]
    pallas_call x0 -> x1, Pallas kernels: none -> 2.75 us  [small_program(): pl.pallas_call(core_body, out_shape=jax.ShapeDtypeStruct((units, width),...]
  transfers between devices with their start and end apart: 10 -> 10, of which waited for: 4 -> 4; matrix products, arithmetic and copies ran while one was open for 0% -> 0% of each run, Pallas kernels for 25% -> 26%
where the time goes in v4:
time: 25.6 us; the launch traced here: 25.4 us
  starting transfers between devices  11.1 us (43%)
  Pallas kernels  9.57 us (37%)
  waiting for transfers between devices  4.03 us (16%)
  between operations  0.69 us (3%)
    ppermute x6, starting transfers between devices, shift(): lax.ppermute(value, 'expert', [(i, (i + by) % experts) for i in range(exp...  10 us
    pallas_call x4, Pallas kernels, call(): pl.pallas_call(body, out_shape=shapes, in_specs=specs or [IN_VMEM] * len(...  6.82 us
    ppermute x6, waiting for transfers between devices, shift(): lax.ppermute(value, 'expert', [(i, (i + by) % experts) for i in range(exp...  4.02 us
    pallas_call x1, Pallas kernels, small_program(): pl.pallas_call(core_body, out_shape=jax.ShapeDtypeStruct((units, width),...  2.75 us
    ppermute x4, starting transfers between devices, swap_half(): lax.ppermute(value, 'half', [(i, (i + 1) % halves) for i in range(halves)])  1.1 us
  transfers between devices with their start and end apart: 10, of which 4 were waited for; matrix products, arithmetic and copies ran while one was open for 0% of the time, Pallas kernels for 26%

profile of v4, /device:TPU:0, one launch (start us, length us, event | category | flops | bytes accessed | tf_op | source)
XLA Modules:
  0.0 25.4 jit_solution(17191688884043312562)
XLA Ops:
  0.6 0.5 %collective-permute-start = (bf16[2048,256]{1,0:T(8,128)(2,1)}, bf16[2048,256]{1,0:T(8,128)(2,1)S(1)}, u32[]{:S(2)}, u32[]{:S(2)}) collective-permute-start(bf16[2048,256]{1,0:T(8,128)(2,1)} %bitcast.10), channel_id=1, source_target_pairs={{0,1},{1,0},{2,3},{3,2},{4,5},{5,4},{6,7},{7,6},{8,9},{9,8},{10,11... | collective-permute-start | bytes 3145736 | tf_op jit(solution)/shard_map/ppermute | solution.py:196
  1.1 0.1 collective-permute-start.1
  1.2 0.4 %collective-permute-start.2 = (bf16[256,2048]{1,0:T(8,128)(2,1)}, bf16[256,2048]{1,0:T(8,128)(2,1)S(1)}, u32[]{:S(2)}, u32[]{:S(2)}) collective-permute-start(bf16[256,2048]{1,0:T(8,128)(2,1)} %bitcast.14), channel_id=1, source_target_pairs={{0,1},{1,0},{2,3},{3,2},{4,5},{5,4},{6,7},{7,6},{8,9},{9,8},{10,11... | collective-permute-start | bytes 3145736 | tf_op jit(solution)/shard_map/ppermute | solution.py:196
  1.7 1.4 %shard_map.86 = (bf16[16,2048]{1,0:T(8,128)(2,1)S(1)}, bf16[16,2048]{1,0:T(8,128)(2,1)S(1)}, bf16[16,2048]{1,0:T(8,128)(2,1)S(1)}, bf16[16,2048]{1,0:T(8,128)(2,1)S(1)}, f32[32,16]{1,0:T(8,128)S(1)}) custom-call(bf16[16,2048]{1,0:T(8,128)(2,1)} %bitcast.17, bf16[16,2048]{1,0:T(8,128)(2,1)} %bitcast.18, s32[2,2,8]{2,1,0:T(2,128)} %bitcast.19, f32[2,2,8]{2,1,0:T(2,128)} %bitcast.20), custom_call_target="tpu_custom_call" | custom-call | flops 10000000 | tf_op jit(solution)/shard_map/pallas_call | solution.py:171
  3.1 2.7 %collective-permute-start.3 = (bf16[16,2048]{1,0:T(8,128)(2,1)S(1)}, bf16[16,2048]{1,0:T(8,128)(2,1)S(1)}, u32[]{:S(2)}, u32[]{:S(2)}) collective-permute-start(bf16[16,2048]{1,0:T(8,128)(2,1)S(1)} %get-tuple-element.34), channel_id=1, source_target_pairs={{0,2},{2,4},{4,6},{6,0},{1,3},{3,5},{5,7},{7,1},{8,10},{10,12},{12... | collective-permute-start | bytes 196616 | tf_op jit(solution)/shard_map/ppermute | solution.py:246
  5.8 2.6 %collective-permute-start.4 = (bf16[16,2048]{1,0:T(8,128)(2,1)S(1)}, bf16[16,2048]{1,0:T(8,128)(2,1)S(1)}, u32[]{:S(2)}, u32[]{:S(2)}) collective-permute-start(bf16[16,2048]{1,0:T(8,128)(2,1)S(1)} %get-tuple-element.35), channel_id=1, source_target_pairs={{0,4},{2,6},{4,0},{6,2},{1,5},{3,7},{5,1},{7,3},{8,12},{10,14},{12... | collective-permute-start | bytes 196616 | tf_op jit(solution)/shard_map/ppermute | solution.py:246
  8.4 0.0 collective-permute-done.refs_3_.refs_9_
  8.4 1.3 %collective-permute-start.5 = (bf16[16,2048]{1,0:T(8,128)(2,1)S(1)}, bf16[16,2048]{1,0:T(8,128)(2,1)S(1)}, u32[]{:S(2)}, u32[]{:S(2)}) collective-permute-start(bf16[16,2048]{1,0:T(8,128)(2,1)S(1)} %get-tuple-element.36), channel_id=1, source_target_pairs={{0,6},{2,0},{4,2},{6,4},{1,7},{3,1},{5,3},{7,5},{8,14},{10,8},{12,... | collective-permute-start | bytes 196616 | tf_op jit(solution)/shard_map/ppermute | solution.py:246
  9.7 0.0 collective-permute-done.1.refs_4_.refs_10_
  9.7 0.0 collective-permute-done.2.refs_5_
  9.7 2.6 %shard_map.87 = (bf16[2048,256]{1,0:T(8,128)(2,1)S(1)}, bf16[2048,256]{1,0:T(8,128)(2,1)S(1)}, bf16[256,2048]{1,0:T(8,128)(2,1)S(1)}, bf16[256,2048]{1,0:T(8,128...) custom-call(f32[32,16]{1,0:T(8,128)S(1)} %get-tuple-element.29.pick_, ...), custom_call_target="tpu_custom_call" | custom-call | flops 1000000000 | tf_op jit(solution)/shard_map/pallas_call | solution.py:171
  12.3 0.0 collective-permute-done.3.refs_1_
  12.3 1.1 %collective-permute-done.4.refs_2_ = bf16[16,2048]{1,0:T(8,128)(2,1)S(1)} collective-permute-done((bf16[16,2048]{1,0:T(8,128)(2,1)S(1)}, bf16[16,2048]{1,0:T(8,128)(2,1)S(1)}, u32[]{:S(2)}, u32[]{:S(2)}) %collective-permute-start.4) | collective-permute-done | bytes 65568 | tf_op jit(solution)/shard_map/ppermute | solution.py:246
  13.4 0.2 collective-permute-done.5.refs_3_
  13.7 2.1 %shard_map.88 = (bf16[32,2560]{1,0:T(8,128)(2,1)S(1)}, bf16[32,2560]{1,0:T(8,128)(2,1)S(1)}, bf16[8,2048]{1,0:T(8,128)(2,1)S(1)}, bf16[8,2048]{1,0:T(8,128)(2,1)...) custom-call(bf16[16,2048]{1,0:T(8,128)(2,1)S(1)} %get-tuple-element.33.refs_0_, ...), custom_call_target="tpu_custom_call" | custom-call | flops 335544320 | tf_op jit(solution)/shard_map/pallas_call | solution.py:171
  15.7 0.1 collective-permute-start.6
  15.8 2.7 %collective-permute-start.7 = (bf16[8,2048]{1,0:T(8,128)(2,1)S(1)}, bf16[8,2048]{1,0:T(8,128)(2,1)S(1)}, u32[]{:S(2)}, u32[]{:S(2)}) collective-permute-start(bf16[8,2048]{1,0:T(8,128)(2,1)S(1)} %get-tuple-element.48), channel_id=1, source_target_pairs={{0,6},{2,0},{4,2},{6,4},{1,7},{3,1},{5,3},{7,5},{8,14},{10,8},{12,... | collective-permute-start | bytes 98312 | tf_op jit(solution)/shard_map/ppermute | solution.py:246
  18.6 0.4 %collective-permute-start.8 = (bf16[8,2048]{1,0:T(8,128)(2,1)S(1)}, bf16[8,2048]{1,0:T(8,128)(2,1)S(1)}, u32[]{:S(2)}, u32[]{:S(2)}) collective-permute-start(bf16[8,2048]{1,0:T(8,128)(2,1)S(1)} %get-tuple-element.49), channel_id=1, source_target_pairs={{0,4},{2,6},{4,0},{6,2},{1,5},{3,7},{5,1},{7,3},{8,12},{10,14},{12... | collective-permute-start | bytes 98312 | tf_op jit(solution)/shard_map/ppermute | solution.py:246
  19.0 0.3 %collective-permute-start.9 = (bf16[8,2048]{1,0:T(8,128)(2,1)S(1)}, bf16[8,2048]{1,0:T(8,128)(2,1)S(1)}, u32[]{:S(2)}, u32[]{:S(2)}) collective-permute-start(bf16[8,2048]{1,0:T(8,128)(2,1)S(1)} %get-tuple-element.50), channel_id=1, source_target_pairs={{0,2},{2,4},{4,6},{6,0},{1,3},{3,5},{5,7},{7,1},{8,10},{10,12},{12... | collective-permute-start | bytes 98312 | tf_op jit(solution)/shard_map/ppermute | solution.py:246
  19.2 0.0 collective-permute-done.6.theirs_ref
  19.2 2.8 %shard_map.89 = bf16[256,2048]{1,0:T(8,128)(2,1)} custom-call(bf16[32,2560]{1,0:T(8,128)(2,1)S(1)} %get-tuple-element.45.mine_ref, bf16[32,2560]{1,0:T(8,128)(2,1)S(1)} %collective-permute-done.6.theirs_ref), custom_call_target="tpu_custom_call" | custom-call | flops 268435456 | tf_op jit(solution)/shard_map/pallas_call | solution.py:327
  22.0 0.0 collective-permute-done.7.refs_1_
  22.0 1.7 %collective-permute-done.8.refs_2_ = bf16[8,2048]{1,0:T(8,128)(2,1)S(1)} collective-permute-done((bf16[8,2048]{1,0:T(8,128)(2,1)S(1)}, bf16[8,2048]{1,0:T(8,128)(2,1)S(1)}, u32[]{:S(2)}, u32[]{:S(2)}) %collective-permute-start.8) | collective-permute-done | bytes 32800 | tf_op jit(solution)/shard_map/ppermute | solution.py:246
  23.7 0.9 %collective-permute-done.9.refs_3_ = bf16[8,2048]{1,0:T(8,128)(2,1)S(1)} collective-permute-done((bf16[8,2048]{1,0:T(8,128)(2,1)S(1)}, bf16[8,2048]{1,0:T(8,128)(2,1)S(1)}, u32[]{:S(2)}, u32[]{:S(2)}) %collective-permute-start.9) | collective-permute-done | bytes 32800 | tf_op jit(solution)/shard_map/ppermute | solution.py:246
  24.7 0.8 %shard_map.90 = bf16[16,2048]{1,0:T(8,128)(2,1)} custom-call(bf16[16,32]{1,0:T(8,128)(2,1)S(1)} %get-tuple-element.32.pick_ref, bf16[8,2048]{1,0:T(8,128)(2,1)S(1)} %get-tuple-element.51.refs_0_, bf16[8,2048]{1,0:T(8,128)(2,1)S(1)} %collective-permute-done.7.refs_1_, bf16[8,2048]{1,0:T(8,128)(2,1)S(1)} %collective-permute-done.8.refs_2_, ...), custom_call_target="tpu_custom_call" | custom-call | flops 1000000 | tf_op jit(solution)/shard_map/pallas_call | solution.py:171
Async XLA Ops:
  0.6 7.7 %collective-permute-start = (bf16[2048,256]{1,0:T(8,128)(2,1)}, bf16[2048,256]{1,0:T(8,128)(2,1)S(1)}, u32[]{:S(2)}, u32[]{:S(2)}) collective-permute-start(bf16[2048,256]{1,0:T(8,128)(2,1)} %bitcast.10), channel_id=1, source_target_pairs={{0,1},{1,0},{2,3},{3,2},{4,5},{5,4},{6,7},{7,6},{8,9},{9,8},{10,11... | collective-permute-start | bytes 3145736 | tf_op jit(solution)/shard_map/ppermute | solution.py:196
  1.1 8.6 %collective-permute-start.1 = (bf16[2048,256]{1,0:T(8,128)(2,1)}, bf16[2048,256]{1,0:T(8,128)(2,1)S(1)}, u32[]{:S(2)}, u32[]{:S(2)}) collective-permute-start(bf16[2048,256]{1,0:T(8,128)(2,1)} %bitcast.12), channel_id=1, source_target_pairs={{0,1},{1,0},{2,3},{3,2},{4,5},{5,4},{6,7},{7,6},{8,9},{9,8},{10,11... | collective-permute-start | bytes 3145736 | tf_op jit(solution)/shard_map/ppermute | solution.py:196
  1.2 8.5 %collective-permute-start.2 = (bf16[256,2048]{1,0:T(8,128)(2,1)}, bf16[256,2048]{1,0:T(8,128)(2,1)S(1)}, u32[]{:S(2)}, u32[]{:S(2)}) collective-permute-start(bf16[256,2048]{1,0:T(8,128)(2,1)} %bitcast.14), channel_id=1, source_target_pairs={{0,1},{1,0},{2,3},{3,2},{4,5},{5,4},{6,7},{7,6},{8,9},{9,8},{10,11... | collective-permute-start | bytes 3145736 | tf_op jit(solution)/shard_map/ppermute | solution.py:196
  3.1 9.2 %collective-permute-start.3 = (bf16[16,2048]{1,0:T(8,128)(2,1)S(1)}, bf16[16,2048]{1,0:T(8,128)(2,1)S(1)}, u32[]{:S(2)}, u32[]{:S(2)}) collective-permute-start(bf16[16,2048]{1,0:T(8,128)(2,1)S(1)} %get-tuple-element.34), channel_id=1, source_target_pairs={{0,2},{2,4},{4,6},{6,0},{1,3},{3,5},{5,7},{7,1},{8,10},{10,12},{12... | collective-permute-start | bytes 196616 | tf_op jit(solution)/shard_map/ppermute | solution.py:246
  5.8 7.6 %collective-permute-start.4 = (bf16[16,2048]{1,0:T(8,128)(2,1)S(1)}, bf16[16,2048]{1,0:T(8,128)(2,1)S(1)}, u32[]{:S(2)}, u32[]{:S(2)}) collective-permute-start(bf16[16,2048]{1,0:T(8,128)(2,1)S(1)} %get-tuple-element.35), channel_id=1, source_target_pairs={{0,4},{2,6},{4,0},{6,2},{1,5},{3,7},{5,1},{7,3},{8,12},{10,14},{12... | collective-permute-start | bytes 196616 | tf_op jit(solution)/shard_map/ppermute | solution.py:246
  8.4 5.3 %collective-permute-start.5 = (bf16[16,2048]{1,0:T(8,128)(2,1)S(1)}, bf16[16,2048]{1,0:T(8,128)(2,1)S(1)}, u32[]{:S(2)}, u32[]{:S(2)}) collective-permute-start(bf16[16,2048]{1,0:T(8,128)(2,1)S(1)} %get-tuple-element.36), channel_id=1, source_target_pairs={{0,6},{2,0},{4,2},{6,4},{1,7},{3,1},{5,3},{7,5},{8,14},{10,8},{12,... | collective-permute-start | bytes 196616 | tf_op jit(solution)/shard_map/ppermute | solution.py:246
  15.7 3.5 %collective-permute-start.6 = (bf16[32,2560]{1,0:T(8,128)(2,1)S(1)}, bf16[32,2560]{1,0:T(8,128)(2,1)S(1)}, u32[]{:S(2)}, u32[]{:S(2)}) collective-permute-start(bf16[32,2560]{1,0:T(8,128)(2,1)S(1)} %get-tuple-element.46), channel_id=1, source_target_pairs={{0,1},{1,0},{2,3},{3,2},{4,5},{5,4},{6,7},{7,6},{8,9},{9,8},{10,11... | collective-permute-start | bytes 491528 | tf_op jit(solution)/shard_map/ppermute | solution.py:196
  15.8 6.2 %collective-permute-start.7 = (bf16[8,2048]{1,0:T(8,128)(2,1)S(1)}, bf16[8,2048]{1,0:T(8,128)(2,1)S(1)}, u32[]{:S(2)}, u32[]{:S(2)}) collective-permute-start(bf16[8,2048]{1,0:T(8,128)(2,1)S(1)} %get-tuple-element.48), channel_id=1, source_target_pairs={{0,6},{2,0},{4,2},{6,4},{1,7},{3,1},{5,3},{7,5},{8,14},{10,8},{12,... | collective-permute-start | bytes 98312 | tf_op jit(solution)/shard_map/ppermute | solution.py:246
  18.6 5.2 %collective-permute-start.8 = (bf16[8,2048]{1,0:T(8,128)(2,1)S(1)}, bf16[8,2048]{1,0:T(8,128)(2,1)S(1)}, u32[]{:S(2)}, u32[]{:S(2)}) collective-permute-start(bf16[8,2048]{1,0:T(8,128)(2,1)S(1)} %get-tuple-element.49), channel_id=1, source_target_pairs={{0,4},{2,6},{4,0},{6,2},{1,5},{3,7},{5,1},{7,3},{8,12},{10,14},{12... | collective-permute-start | bytes 98312 | tf_op jit(solution)/shard_map/ppermute | solution.py:246
  19.0 5.7 %collective-permute-start.9 = (bf16[8,2048]{1,0:T(8,128)(2,1)S(1)}, bf16[8,2048]{1,0:T(8,128)(2,1)S(1)}, u32[]{:S(2)}, u32[]{:S(2)}) collective-permute-start(bf16[8,2048]{1,0:T(8,128)(2,1)S(1)} %get-tuple-element.50), channel_id=1, source_target_pairs={{0,2},{2,4},{4,6},{6,0},{1,3},{3,5},{5,7},{7,1},{8,10},{10,12},{12... | collective-permute-start | bytes 98312 | tf_op jit(solution)/shard_map/ppermute | solution.py:246

commit v5 on v4

--- a/solution.py
+++ b/solution.py
@@ -56,12 +56,12 @@
     return found
 
 
-def route_rows(data, routes, gates, base, experts, capacity):
+def route_picks(routes, gates, base, experts, capacity):
     batches, top = len(routes), routes[0].shape[0]
     block = batches * capacity
     found = route_slots(routes, base, experts, block, capacity)
     joined = lambda rows: jnp.concatenate(rows, axis=1)
-    tokens = data.shape[0] // 2
+    tokens = batches * routes[0].shape[1]
     row = lax.broadcasted_iota(jnp.int32, (2 * experts * block, tokens), 0)
     slot = lax.broadcasted_iota(jnp.int32, (experts * block, tokens), 0)
     in_x = row[:, :1] % (2 * block) < block
@@ -77,7 +77,7 @@
         pick_tok = pick_tok + jnp.where(slot == relative * block + within, 1.0, 0.0)
         gate = gate + jnp.sum(jnp.where(here, gates_k, 0.0), axis=1, keepdims=True)
     picks = joined([pick_x, pick_u]).astype(BF16)
-    return plain(picks, data) * gate, pick_tok
+    return picks, gate, pick_tok
 
 
 def forward_values(x_rows, weights):
@@ -216,17 +216,19 @@
         ]
         for copy in copies:
             copy.start()
-        for copy in copies:
+        for copy in copies[:2]:
             copy.wait()
-        sent, pick = route_rows(
-            data[...],
+        picks, gate, pick = route_picks(
             [routes_ref[m] for m in range(batches)],
             [gates_ref[m] for m in range(batches)],
             lax.axis_index("expert"), experts, capacity,
         )
+        pick_ref[...] = pick
+        for copy in copies[2:]:
+            copy.wait()
+        sent = plain(picks, data[...]) * gate
         for d in range(experts):
             outs[d][...] = sent[2 * d * block : 2 * (d + 1) * block].astype(BF16)
-        pick_ref[...] = pick
 
     *blocks, pick = call(
         dispatch_body,
@@ -247,8 +249,9 @@
             value, "expert", [(i, (i + by) % experts) for i in range(experts)]
         )
 
-    blocks[-1], far[0] = lax.optimization_barrier((blocks[-1], far[0]))
-    got = [blocks[0]] + [shift(blocks[d], d) for d in range(1, experts)]
+    blocks[1], far[0] = lax.optimization_barrier((blocks[1], far[0]))
+    got = [shift(blocks[d], d) for d in range(experts - 1, 0, -1)]
+    got = [blocks[0]] + got[::-1]
 
     turned_shapes = [
         kept((units, width), BF16), kept((units, width), BF16), kept((width, units), BF16)
@@ -356,9 +359,8 @@
     block = batches * capacity
     slots = experts * block
     units = own[0].shape[1]
-    sent, pick = route_rows(
-        jnp.concatenate([activations, upstream], axis=0), routes, gates, 0, experts, capacity
-    )
+    picks, gate, pick = route_picks(routes, gates, 0, experts, capacity)
+    sent = plain(picks, jnp.concatenate([activations, upstream], axis=0)) * gate
     weights = [(*w[:2], *(m.T for m in w)) for w in (own, [swap_half(w) for w in own])]
     sent = sent.astype(BF16).reshape(experts, 2 * block, width)
     got = lax.all_to_all(sent, "expert", split_axis=0, concat_axis=0, tiled=True)

time: 25.6 us -> 25.2 us (0.984)
  transfers between devices with their start and end apart: 10 -> 10, of which waited for: 4 -> 3; matrix products, arithmetic and copies ran while one was open for 0% -> 0% of each run, Pallas kernels for 26% -> 26%
where the time goes in v5:
time: 25.2 us; the launch traced here: 25 us
  starting transfers between devices  11 us (44%)
  Pallas kernels  9.4 us (37%)
  waiting for transfers between devices  3.83 us (15%)
  between operations  0.7 us (3%)
    ppermute x6, starting transfers between devices, shift(): lax.ppermute(value, 'expert', [(i, (i + by) % experts) for i in range(exp...  9.95 us
    pallas_call x4, Pallas kernels, call(): pl.pallas_call(body, out_shape=shapes, in_specs=specs or [IN_VMEM] * len(...  6.65 us
    ppermute x6, waiting for transfers between devices, shift(): lax.ppermute(value, 'expert', [(i, (i + by) % experts) for i in range(exp...  3.81 us
    pallas_call x1, Pallas kernels, small_program(): pl.pallas_call(core_body, out_shape=jax.ShapeDtypeStruct((units, width),...  2.75 us
    ppermute x4, starting transfers between devices, swap_half(): lax.ppermute(value, 'half', [(i, (i + 1) % halves) for i in range(halves)])  1.1 us
  transfers between devices with their start and end apart: 10, of which 3 were waited for; matrix products, arithmetic and copies ran while one was open for 0% of the time, Pallas kernels for 26%

profile of v5, /device:TPU:0, one launch (start us, length us, event | category | flops | bytes accessed | tf_op | source)
XLA Modules:
  0.0 25.0 jit_solution(11169997063249495336)
XLA Ops:
  0.6 0.5 %collective-permute-start = (bf16[2048,256]{1,0:T(8,128)(2,1)}, bf16[2048,256]{1,0:T(8,128)(2,1)S(1)}, u32[]{:S(2)}, u32[]{:S(2)}) collective-permute-start(bf16[2048,256]{1,0:T(8,128)(2,1)} %bitcast.10), channel_id=1, source_target_pairs={{0,1},{1,0},{2,3},{3,2},{4,5},{5,4},{6,7},{7,6},{8,9},{9,8},{10,11... | collective-permute-start | bytes 3145736 | tf_op jit(solution)/shard_map/ppermute | solution.py:196
  1.1 0.1 collective-permute-start.1
  1.2 0.4 %collective-permute-start.2 = (bf16[256,2048]{1,0:T(8,128)(2,1)}, bf16[256,2048]{1,0:T(8,128)(2,1)S(1)}, u32[]{:S(2)}, u32[]{:S(2)}) collective-permute-start(bf16[256,2048]{1,0:T(8,128)(2,1)} %bitcast.14), channel_id=1, source_target_pairs={{0,1},{1,0},{2,3},{3,2},{4,5},{5,4},{6,7},{7,6},{8,9},{9,8},{10,11... | collective-permute-start | bytes 3145736 | tf_op jit(solution)/shard_map/ppermute | solution.py:196
  1.7 1.2 %shard_map.86 = (bf16[16,2048]{1,0:T(8,128)(2,1)S(1)}, bf16[16,2048]{1,0:T(8,128)(2,1)S(1)}, bf16[16,2048]{1,0:T(8,128)(2,1)S(1)}, bf16[16,2048]{1,0:T(8,128)(2,1)S(1)}, f32[32,16]{1,0:T(8,128)S(1)}) custom-call(bf16[16,2048]{1,0:T(8,128)(2,1)} %bitcast.17, bf16[16,2048]{1,0:T(8,128)(2,1)} %bitcast.18, s32[2,2,8]{2,1,0:T(2,128)} %bitcast.19, f32[2,2,8]{2,1,0:T(2,128)} %bitcast.20), custom_call_target="tpu_custom_call" | custom-call | flops 10000000 | tf_op jit(solution)/shard_map/pallas_call | solution.py:171
  2.9 3.7 %collective-permute-start.4 = (bf16[16,2048]{1,0:T(8,128)(2,1)S(1)}, bf16[16,2048]{1,0:T(8,128)(2,1)S(1)}, u32[]{:S(2)}, u32[]{:S(2)}) collective-permute-start(bf16[16,2048]{1,0:T(8,128)(2,1)S(1)} %get-tuple-element.35), channel_id=1, source_target_pairs={{0,4},{2,6},{4,0},{6,2},{1,5},{3,7},{5,1},{7,3},{8,12},{10,14},{12... | collective-permute-start | bytes 196616 | tf_op jit(solution)/shard_map/ppermute | solution.py:248
  6.6 1.4 %collective-permute-start.5 = (bf16[16,2048]{1,0:T(8,128)(2,1)S(1)}, bf16[16,2048]{1,0:T(8,128)(2,1)S(1)}, u32[]{:S(2)}, u32[]{:S(2)}) collective-permute-start(bf16[16,2048]{1,0:T(8,128)(2,1)S(1)} %get-tuple-element.36), channel_id=1, source_target_pairs={{0,6},{2,0},{4,2},{6,4},{1,7},{3,1},{5,3},{7,5},{8,14},{10,8},{12,... | collective-permute-start | bytes 196616 | tf_op jit(solution)/shard_map/ppermute | solution.py:248
  8.0 0.0 collective-permute-done.refs_3_.refs_9_
  8.0 0.7 %collective-permute-start.3 = (bf16[16,2048]{1,0:T(8,128)(2,1)S(1)}, bf16[16,2048]{1,0:T(8,128)(2,1)S(1)}, u32[]{:S(2)}, u32[]{:S(2)}) collective-permute-start(bf16[16,2048]{1,0:T(8,128)(2,1)S(1)} %get-tuple-element.34), channel_id=1, source_target_pairs={{0,2},{2,4},{4,6},{6,0},{1,3},{3,5},{5,7},{7,1},{8,10},{10,12},{12... | collective-permute-start | bytes 196616 | tf_op jit(solution)/shard_map/ppermute | solution.py:248
  8.7 0.0 collective-permute-done.1.refs_4_.refs_10_
  8.7 0.0 collective-permute-done.2.refs_5_
  8.7 2.6 %shard_map.87 = (bf16[2048,256]{1,0:T(8,128)(2,1)S(1)}, bf16[2048,256]{1,0:T(8,128)(2,1)S(1)}, bf16[256,2048]{1,0:T(8,128)(2,1)S(1)}, bf16[256,2048]{1,0:T(8,128...) custom-call(f32[32,16]{1,0:T(8,128)S(1)} %get-tuple-element.29.pick_, ...), custom_call_target="tpu_custom_call" | custom-call | flops 1000000000 | tf_op jit(solution)/shard_map/pallas_call | solution.py:171
  11.2 0.0 collective-permute-done.4.refs_2_
  11.2 0.0 collective-permute-done.5.refs_3_
  11.3 2.8 %collective-permute-done.3.refs_1_ = bf16[16,2048]{1,0:T(8,128)(2,1)S(1)} collective-permute-done((bf16[16,2048]{1,0:T(8,128)(2,1)S(1)}, bf16[16,2048]{1,0:T(8,128)(2,1)S(1)}, u32[]{:S(2)}, u32[]{:S(2)}) %collective-permute-start.3) | collective-permute-done | bytes 65568 | tf_op jit(solution)/shard_map/ppermute | solution.py:248
  14.1 2.1 %shard_map.88 = (bf16[32,2560]{1,0:T(8,128)(2,1)S(1)}, bf16[32,2560]{1,0:T(8,128)(2,1)S(1)}, bf16[8,2048]{1,0:T(8,128)(2,1)S(1)}, bf16[8,2048]{1,0:T(8,128)(2,1)...) custom-call(bf16[16,2048]{1,0:T(8,128)(2,1)S(1)} %get-tuple-element.33.refs_0_, ...), custom_call_target="tpu_custom_call" | custom-call | flops 335544320 | tf_op jit(solution)/shard_map/pallas_call | solution.py:171
  16.1 0.1 collective-permute-start.6
  16.2 2.1 %collective-permute-start.7 = (bf16[8,2048]{1,0:T(8,128)(2,1)S(1)}, bf16[8,2048]{1,0:T(8,128)(2,1)S(1)}, u32[]{:S(2)}, u32[]{:S(2)}) collective-permute-start(bf16[8,2048]{1,0:T(8,128)(2,1)S(1)} %get-tuple-element.48), channel_id=1, source_target_pairs={{0,6},{2,0},{4,2},{6,4},{1,7},{3,1},{5,3},{7,5},{8,14},{10,8},{12,... | collective-permute-start | bytes 98312 | tf_op jit(solution)/shard_map/ppermute | solution.py:248
  18.3 0.2 collective-permute-start.8
  18.5 1.9 %collective-permute-start.9 = (bf16[8,2048]{1,0:T(8,128)(2,1)S(1)}, bf16[8,2048]{1,0:T(8,128)(2,1)S(1)}, u32[]{:S(2)}, u32[]{:S(2)}) collective-permute-start(bf16[8,2048]{1,0:T(8,128)(2,1)S(1)} %get-tuple-element.50), channel_id=1, source_target_pairs={{0,2},{2,4},{4,6},{6,0},{1,3},{3,5},{5,7},{7,1},{8,10},{10,12},{12... | collective-permute-start | bytes 98312 | tf_op jit(solution)/shard_map/ppermute | solution.py:248
  20.4 0.0 collective-permute-done.6.theirs_ref
  20.4 2.8 %shard_map.89 = bf16[256,2048]{1,0:T(8,128)(2,1)} custom-call(bf16[32,2560]{1,0:T(8,128)(2,1)S(1)} %get-tuple-element.45.mine_ref, bf16[32,2560]{1,0:T(8,128)(2,1)S(1)} %collective-permute-done.6.theirs_ref), custom_call_target="tpu_custom_call" | custom-call | flops 268435456 | tf_op jit(solution)/shard_map/pallas_call | solution.py:330
  23.2 0.0 collective-permute-done.7.refs_1_
  23.2 0.2 collective-permute-done.8.refs_2_
  23.4 0.8 %collective-permute-done.9.refs_3_ = bf16[8,2048]{1,0:T(8,128)(2,1)S(1)} collective-permute-done((bf16[8,2048]{1,0:T(8,128)(2,1)S(1)}, bf16[8,2048]{1,0:T(8,128)(2,1)S(1)}, u32[]{:S(2)}, u32[]{:S(2)}) %collective-permute-start.9) | collective-permute-done | bytes 32800 | tf_op jit(solution)/shard_map/ppermute | solution.py:248
  24.2 0.8 %shard_map.90 = bf16[16,2048]{1,0:T(8,128)(2,1)} custom-call(bf16[16,32]{1,0:T(8,128)(2,1)S(1)} %get-tuple-element.32.pick_ref, bf16[8,2048]{1,0:T(8,128)(2,1)S(1)} %get-tuple-element.51.refs_0_, bf16[8,2048]{1,0:T(8,128)(2,1)S(1)} %collective-permute-done.7.refs_1_, bf16[8,2048]{1,0:T(8,128)(2,1)S(1)} %collective-permute-done.8.refs_2_, ...), custom_call_target="tpu_custom_call" | custom-call | flops 1000000 | tf_op jit(solution)/shard_map/pallas_call | solution.py:171
Async XLA Ops:
  0.6 7.4 %collective-permute-start = (bf16[2048,256]{1,0:T(8,128)(2,1)}, bf16[2048,256]{1,0:T(8,128)(2,1)S(1)}, u32[]{:S(2)}, u32[]{:S(2)}) collective-permute-start(bf16[2048,256]{1,0:T(8,128)(2,1)} %bitcast.10), channel_id=1, source_target_pairs={{0,1},{1,0},{2,3},{3,2},{4,5},{5,4},{6,7},{7,6},{8,9},{9,8},{10,11... | collective-permute-start | bytes 3145736 | tf_op jit(solution)/shard_map/ppermute | solution.py:196
  1.1 7.5 %collective-permute-start.1 = (bf16[2048,256]{1,0:T(8,128)(2,1)}, bf16[2048,256]{1,0:T(8,128)(2,1)S(1)}, u32[]{:S(2)}, u32[]{:S(2)}) collective-permute-start(bf16[2048,256]{1,0:T(8,128)(2,1)} %bitcast.12), channel_id=1, source_target_pairs={{0,1},{1,0},{2,3},{3,2},{4,5},{5,4},{6,7},{7,6},{8,9},{9,8},{10,11... | collective-permute-start | bytes 3145736 | tf_op jit(solution)/shard_map/ppermute | solution.py:196
  1.2 7.4 %collective-permute-start.2 = (bf16[256,2048]{1,0:T(8,128)(2,1)}, bf16[256,2048]{1,0:T(8,128)(2,1)S(1)}, u32[]{:S(2)}, u32[]{:S(2)}) collective-permute-start(bf16[256,2048]{1,0:T(8,128)(2,1)} %bitcast.14), channel_id=1, source_target_pairs={{0,1},{1,0},{2,3},{3,2},{4,5},{5,4},{6,7},{7,6},{8,9},{9,8},{10,11... | collective-permute-start | bytes 3145736 | tf_op jit(solution)/shard_map/ppermute | solution.py:196
  2.9 8.3 %collective-permute-start.4 = (bf16[16,2048]{1,0:T(8,128)(2,1)S(1)}, bf16[16,2048]{1,0:T(8,128)(2,1)S(1)}, u32[]{:S(2)}, u32[]{:S(2)}) collective-permute-start(bf16[16,2048]{1,0:T(8,128)(2,1)S(1)} %get-tuple-element.35), channel_id=1, source_target_pairs={{0,4},{2,6},{4,0},{6,2},{1,5},{3,7},{5,1},{7,3},{8,12},{10,14},{12... | collective-permute-start | bytes 196616 | tf_op jit(solution)/shard_map/ppermute | solution.py:248
  6.6 4.6 %collective-permute-start.5 = (bf16[16,2048]{1,0:T(8,128)(2,1)S(1)}, bf16[16,2048]{1,0:T(8,128)(2,1)S(1)}, u32[]{:S(2)}, u32[]{:S(2)}) collective-permute-start(bf16[16,2048]{1,0:T(8,128)(2,1)S(1)} %get-tuple-element.36), channel_id=1, source_target_pairs={{0,6},{2,0},{4,2},{6,4},{1,7},{3,1},{5,3},{7,5},{8,14},{10,8},{12,... | collective-permute-start | bytes 196616 | tf_op jit(solution)/shard_map/ppermute | solution.py:248
  8.0 6.1 %collective-permute-start.3 = (bf16[16,2048]{1,0:T(8,128)(2,1)S(1)}, bf16[16,2048]{1,0:T(8,128)(2,1)S(1)}, u32[]{:S(2)}, u32[]{:S(2)}) collective-permute-start(bf16[16,2048]{1,0:T(8,128)(2,1)S(1)} %get-tuple-element.34), channel_id=1, source_target_pairs={{0,2},{2,4},{4,6},{6,0},{1,3},{3,5},{5,7},{7,1},{8,10},{10,12},{12... | collective-permute-start | bytes 196616 | tf_op jit(solution)/shard_map/ppermute | solution.py:248
  16.1 4.3 %collective-permute-start.6 = (bf16[32,2560]{1,0:T(8,128)(2,1)S(1)}, bf16[32,2560]{1,0:T(8,128)(2,1)S(1)}, u32[]{:S(2)}, u32[]{:S(2)}) collective-permute-start(bf16[32,2560]{1,0:T(8,128)(2,1)S(1)} %get-tuple-element.46), channel_id=1, source_target_pairs={{0,1},{1,0},{2,3},{3,2},{4,5},{5,4},{6,7},{7,6},{8,9},{9,8},{10,11... | collective-permute-start | bytes 491528 | tf_op jit(solution)/shard_map/ppermute | solution.py:196
  16.2 7.0 %collective-permute-start.7 = (bf16[8,2048]{1,0:T(8,128)(2,1)S(1)}, bf16[8,2048]{1,0:T(8,128)(2,1)S(1)}, u32[]{:S(2)}, u32[]{:S(2)}) collective-permute-start(bf16[8,2048]{1,0:T(8,128)(2,1)S(1)} %get-tuple-element.48), channel_id=1, source_target_pairs={{0,6},{2,0},{4,2},{6,4},{1,7},{3,1},{5,3},{7,5},{8,14},{10,8},{12,... | collective-permute-start | bytes 98312 | tf_op jit(solution)/shard_map/ppermute | solution.py:248
  18.3 5.2 %collective-permute-start.8 = (bf16[8,2048]{1,0:T(8,128)(2,1)S(1)}, bf16[8,2048]{1,0:T(8,128)(2,1)S(1)}, u32[]{:S(2)}, u32[]{:S(2)}) collective-permute-start(bf16[8,2048]{1,0:T(8,128)(2,1)S(1)} %get-tuple-element.49), channel_id=1, source_target_pairs={{0,4},{2,6},{4,0},{6,2},{1,5},{3,7},{5,1},{7,3},{8,12},{10,14},{12... | collective-permute-start | bytes 98312 | tf_op jit(solution)/shard_map/ppermute | solution.py:248
  18.5 5.7 %collective-permute-start.9 = (bf16[8,2048]{1,0:T(8,128)(2,1)S(1)}, bf16[8,2048]{1,0:T(8,128)(2,1)S(1)}, u32[]{:S(2)}, u32[]{:S(2)}) collective-permute-start(bf16[8,2048]{1,0:T(8,128)(2,1)S(1)} %get-tuple-element.50), channel_id=1, source_target_pairs={{0,2},{2,4},{4,6},{6,0},{1,3},{3,5},{5,7},{7,1},{8,10},{10,12},{12... | collective-permute-start | bytes 98312 | tf_op jit(solution)/shard_map/ppermute | solution.py:248

commit v6 on v5

--- a/solution.py
+++ b/solution.py
@@ -245,9 +245,13 @@
     )
 
     def shift(value, by):
-        return lax.ppermute(
-            value, "expert", [(i, (i + by) % experts) for i in range(experts)]
-        )
+        halves = lax.axis_size("half")
+        pairs = [
+            (i * halves + h, (i + by) % experts * halves + halves - 1 - h)
+            for i in range(experts)
+            for h in range(halves)
+        ]
+        return lax.ppermute(value, ("expert", "half"), pairs)
 
     blocks[1], far[0] = lax.optimization_barrier((blocks[1], far[0]))
     got = [shift(blocks[d], d) for d in range(experts - 1, 0, -1)]

time: 25.2 us -> 24.5 us (0.972)
  waiting for transfers between devices: 3.83 us -> 2.98 us
    ppermute x6, waiting for transfers between devices: 3.81 us -> 2.97 us  [shift(): return lax.ppermute(value, ('expert', 'half'), pairs)]
    ppermute x4, starting transfers between devices: 1.1 us -> 1.47 us  [swap_half(): lax.ppermute(value, 'half', [(i, (i + 1) % halves) for i in range(halves)])]
  transfers between devices with their start and end apart: 10 -> 10, of which waited for: 3 -> 3; matrix products, arithmetic and copies ran while one was open for 0% -> 0% of each run, Pallas kernels for 26% -> 27%
where the time goes in v6:
time: 24.5 us; the launch traced here: 24.3 us
  starting transfers between devices  11.2 us (46%)
  Pallas kernels  9.4 us (38%)
  waiting for transfers between devices  2.98 us (12%)
  between operations  0.69 us (3%)
    ppermute x6, starting transfers between devices, shift(): return lax.ppermute(value, ('expert', 'half'), pairs)  9.77 us
    pallas_call x4, Pallas kernels, call(): pl.pallas_call(body, out_shape=shapes, in_specs=specs or [IN_VMEM] * len(...  6.65 us
    ppermute x6, waiting for transfers between devices, shift(): return lax.ppermute(value, ('expert', 'half'), pairs)  2.97 us
    pallas_call x1, Pallas kernels, small_program(): pl.pallas_call(core_body, out_shape=jax.ShapeDtypeStruct((units, width),...  2.75 us
    ppermute x4, starting transfers between devices, swap_half(): lax.ppermute(value, 'half', [(i, (i + 1) % halves) for i in range(halves)])  1.47 us
  transfers between devices with their start and end apart: 10, of which 3 were waited for; matrix products, arithmetic and copies ran while one was open for 0% of the time, Pallas kernels for 27%

profile of v6, /device:TPU:0, one launch (start us, length us, event | category | flops | bytes accessed | tf_op | source)
XLA Modules:
  0.0 24.3 jit_solution(2773534558148710288)
XLA Ops:
  0.6 0.5 %collective-permute-start = (bf16[2048,256]{1,0:T(8,128)(2,1)}, bf16[2048,256]{1,0:T(8,128)(2,1)S(1)}, u32[]{:S(2)}, u32[]{:S(2)}) collective-permute-start(bf16[2048,256]{1,0:T(8,128)(2,1)} %bitcast.10), channel_id=1, source_target_pairs={{0,1},{1,0},{2,3},{3,2},{4,5},{5,4},{6,7},{7,6},{8,9},{9,8},{10,11... | collective-permute-start | bytes 3145736 | tf_op jit(solution)/shard_map/ppermute | solution.py:196
  1.1 0.1 collective-permute-start.1
  1.2 0.4 %collective-permute-start.2 = (bf16[256,2048]{1,0:T(8,128)(2,1)}, bf16[256,2048]{1,0:T(8,128)(2,1)S(1)}, u32[]{:S(2)}, u32[]{:S(2)}) collective-permute-start(bf16[256,2048]{1,0:T(8,128)(2,1)} %bitcast.14), channel_id=1, source_target_pairs={{0,1},{1,0},{2,3},{3,2},{4,5},{5,4},{6,7},{7,6},{8,9},{9,8},{10,11... | collective-permute-start | bytes 3145736 | tf_op jit(solution)/shard_map/ppermute | solution.py:196
  1.7 1.2 %shard_map.86 = (bf16[16,2048]{1,0:T(8,128)(2,1)S(1)}, bf16[16,2048]{1,0:T(8,128)(2,1)S(1)}, bf16[16,2048]{1,0:T(8,128)(2,1)S(1)}, bf16[16,2048]{1,0:T(8,128)(2,1)S(1)}, f32[32,16]{1,0:T(8,128)S(1)}) custom-call(bf16[16,2048]{1,0:T(8,128)(2,1)} %bitcast.17, bf16[16,2048]{1,0:T(8,128)(2,1)} %bitcast.18, s32[2,2,8]{2,1,0:T(2,128)} %bitcast.19, f32[2,2,8]{2,1,0:T(2,128)} %bitcast.20), custom_call_target="tpu_custom_call" | custom-call | flops 10000000 | tf_op jit(solution)/shard_map/pallas_call | solution.py:171
  2.9 3.8 %collective-permute-start.4 = (bf16[16,2048]{1,0:T(8,128)(2,1)S(1)}, bf16[16,2048]{1,0:T(8,128)(2,1)S(1)}, u32[]{:S(2)}, u32[]{:S(2)}) collective-permute-start(bf16[16,2048]{1,0:T(8,128)(2,1)S(1)} %get-tuple-element.35), channel_id=1, source_target_pairs={{0,5},{1,4},{2,7},{3,6},{4,1},{5,0},{6,3},{7,2},{8,13},{9,12},{10,... | collective-permute-start | bytes 196616 | tf_op jit(solution)/shard_map/ppermute | solution.py:254
  6.7 1.1 %collective-permute-start.5 = (bf16[16,2048]{1,0:T(8,128)(2,1)S(1)}, bf16[16,2048]{1,0:T(8,128)(2,1)S(1)}, u32[]{:S(2)}, u32[]{:S(2)}) collective-permute-start(bf16[16,2048]{1,0:T(8,128)(2,1)S(1)} %get-tuple-element.36), channel_id=1, source_target_pairs={{0,7},{1,6},{2,1},{3,0},{4,3},{5,2},{6,5},{7,4},{8,15},{9,14},{10,... | collective-permute-start | bytes 196616 | tf_op jit(solution)/shard_map/ppermute | solution.py:254
  7.8 0.0 collective-permute-done.refs_3_.refs_9_
  7.8 0.7 %collective-permute-start.3 = (bf16[16,2048]{1,0:T(8,128)(2,1)S(1)}, bf16[16,2048]{1,0:T(8,128)(2,1)S(1)}, u32[]{:S(2)}, u32[]{:S(2)}) collective-permute-start(bf16[16,2048]{1,0:T(8,128)(2,1)S(1)} %get-tuple-element.34), channel_id=1, source_target_pairs={{0,3},{1,2},{2,5},{3,4},{4,7},{5,6},{6,1},{7,0},{8,11},{9,10},{10,... | collective-permute-start | bytes 196616 | tf_op jit(solution)/shard_map/ppermute | solution.py:254
  8.4 0.0 collective-permute-done.1.refs_4_.refs_10_
  8.4 0.0 collective-permute-done.2.refs_5_
  8.4 2.6 %shard_map.87 = (bf16[2048,256]{1,0:T(8,128)(2,1)S(1)}, bf16[2048,256]{1,0:T(8,128)(2,1)S(1)}, bf16[256,2048]{1,0:T(8,128)(2,1)S(1)}, bf16[256,2048]{1,0:T(8,128...) custom-call(f32[32,16]{1,0:T(8,128)S(1)} %get-tuple-element.29.pick_, ...), custom_call_target="tpu_custom_call" | custom-call | flops 1000000000 | tf_op jit(solution)/shard_map/pallas_call | solution.py:171
  11.0 0.0 collective-permute-done.4.refs_2_
  11.0 0.1 collective-permute-done.5.refs_3_
  11.1 2.3 %collective-permute-done.3.refs_1_ = bf16[16,2048]{1,0:T(8,128)(2,1)S(1)} collective-permute-done((bf16[16,2048]{1,0:T(8,128)(2,1)S(1)}, bf16[16,2048]{1,0:T(8,128)(2,1)S(1)}, u32[]{:S(2)}, u32[]{:S(2)}) %collective-permute-start.3) | collective-permute-done | bytes 65568 | tf_op jit(solution)/shard_map/ppermute | solution.py:254
  13.4 2.1 %shard_map.88 = (bf16[32,2560]{1,0:T(8,128)(2,1)S(1)}, bf16[32,2560]{1,0:T(8,128)(2,1)S(1)}, bf16[8,2048]{1,0:T(8,128)(2,1)S(1)}, bf16[8,2048]{1,0:T(8,128)(2,1)...) custom-call(bf16[16,2048]{1,0:T(8,128)(2,1)S(1)} %get-tuple-element.33.refs_0_, ...), custom_call_target="tpu_custom_call" | custom-call | flops 335544320 | tf_op jit(solution)/shard_map/pallas_call | solution.py:171
  15.5 0.4 %collective-permute-start.6 = (bf16[32,2560]{1,0:T(8,128)(2,1)S(1)}, bf16[32,2560]{1,0:T(8,128)(2,1)S(1)}, u32[]{:S(2)}, u32[]{:S(2)}) collective-permute-start(bf16[32,2560]{1,0:T(8,128)(2,1)S(1)} %get-tuple-element.46), channel_id=1, source_target_pairs={{0,1},{1,0},{2,3},{3,2},{4,5},{5,4},{6,7},{7,6},{8,9},{9,8},{10,11... | collective-permute-start | bytes 491528 | tf_op jit(solution)/shard_map/ppermute | solution.py:196
  15.9 2.4 %collective-permute-start.7 = (bf16[8,2048]{1,0:T(8,128)(2,1)S(1)}, bf16[8,2048]{1,0:T(8,128)(2,1)S(1)}, u32[]{:S(2)}, u32[]{:S(2)}) collective-permute-start(bf16[8,2048]{1,0:T(8,128)(2,1)S(1)} %get-tuple-element.48), channel_id=1, source_target_pairs={{0,7},{1,6},{2,1},{3,0},{4,3},{5,2},{6,5},{7,4},{8,15},{9,14},{10,... | collective-permute-start | bytes 98312 | tf_op jit(solution)/shard_map/ppermute | solution.py:254
  18.3 0.1 collective-permute-start.8
  18.4 1.8 %collective-permute-start.9 = (bf16[8,2048]{1,0:T(8,128)(2,1)S(1)}, bf16[8,2048]{1,0:T(8,128)(2,1)S(1)}, u32[]{:S(2)}, u32[]{:S(2)}) collective-permute-start(bf16[8,2048]{1,0:T(8,128)(2,1)S(1)} %get-tuple-element.50), channel_id=1, source_target_pairs={{0,3},{1,2},{2,5},{3,4},{4,7},{5,6},{6,1},{7,0},{8,11},{9,10},{10,... | collective-permute-start | bytes 98312 | tf_op jit(solution)/shard_map/ppermute | solution.py:254
  20.2 0.0 collective-permute-done.6.theirs_ref
  20.2 2.8 %shard_map.89 = bf16[256,2048]{1,0:T(8,128)(2,1)} custom-call(bf16[32,2560]{1,0:T(8,128)(2,1)S(1)} %get-tuple-element.45.mine_ref, bf16[32,2560]{1,0:T(8,128)(2,1)S(1)} %collective-permute-done.6.theirs_ref), custom_call_target="tpu_custom_call" | custom-call | flops 268435456 | tf_op jit(solution)/shard_map/pallas_call | solution.py:334
  22.9 0.0 collective-permute-done.7.refs_1_
  22.9 0.0 collective-permute-done.8.refs_2_
  23.0 0.6 %collective-permute-done.9.refs_3_ = bf16[8,2048]{1,0:T(8,128)(2,1)S(1)} collective-permute-done((bf16[8,2048]{1,0:T(8,128)(2,1)S(1)}, bf16[8,2048]{1,0:T(8,128)(2,1)S(1)}, u32[]{:S(2)}, u32[]{:S(2)}) %collective-permute-start.9) | collective-permute-done | bytes 32800 | tf_op jit(solution)/shard_map/ppermute | solution.py:254
  23.5 0.8 %shard_map.90 = bf16[16,2048]{1,0:T(8,128)(2,1)} custom-call(bf16[16,32]{1,0:T(8,128)(2,1)S(1)} %get-tuple-element.32.pick_ref, bf16[8,2048]{1,0:T(8,128)(2,1)S(1)} %get-tuple-element.51.refs_0_, bf16[8,2048]{1,0:T(8,128)(2,1)S(1)} %collective-permute-done.7.refs_1_, bf16[8,2048]{1,0:T(8,128)(2,1)S(1)} %collective-permute-done.8.refs_2_, ...), custom_call_target="tpu_custom_call" | custom-call | flops 1000000 | tf_op jit(solution)/shard_map/pallas_call | solution.py:171
Async XLA Ops:
  0.6 7.1 %collective-permute-start = (bf16[2048,256]{1,0:T(8,128)(2,1)}, bf16[2048,256]{1,0:T(8,128)(2,1)S(1)}, u32[]{:S(2)}, u32[]{:S(2)}) collective-permute-start(bf16[2048,256]{1,0:T(8,128)(2,1)} %bitcast.10), channel_id=1, source_target_pairs={{0,1},{1,0},{2,3},{3,2},{4,5},{5,4},{6,7},{7,6},{8,9},{9,8},{10,11... | collective-permute-start | bytes 3145736 | tf_op jit(solution)/shard_map/ppermute | solution.py:196
  1.1 7.3 %collective-permute-start.1 = (bf16[2048,256]{1,0:T(8,128)(2,1)}, bf16[2048,256]{1,0:T(8,128)(2,1)S(1)}, u32[]{:S(2)}, u32[]{:S(2)}) collective-permute-start(bf16[2048,256]{1,0:T(8,128)(2,1)} %bitcast.12), channel_id=1, source_target_pairs={{0,1},{1,0},{2,3},{3,2},{4,5},{5,4},{6,7},{7,6},{8,9},{9,8},{10,11... | collective-permute-start | bytes 3145736 | tf_op jit(solution)/shard_map/ppermute | solution.py:196
  1.2 7.2 %collective-permute-start.2 = (bf16[256,2048]{1,0:T(8,128)(2,1)}, bf16[256,2048]{1,0:T(8,128)(2,1)S(1)}, u32[]{:S(2)}, u32[]{:S(2)}) collective-permute-start(bf16[256,2048]{1,0:T(8,128)(2,1)} %bitcast.14), channel_id=1, source_target_pairs={{0,1},{1,0},{2,3},{3,2},{4,5},{5,4},{6,7},{7,6},{8,9},{9,8},{10,11... | collective-permute-start | bytes 3145736 | tf_op jit(solution)/shard_map/ppermute | solution.py:196
  2.9 8.1 %collective-permute-start.4 = (bf16[16,2048]{1,0:T(8,128)(2,1)S(1)}, bf16[16,2048]{1,0:T(8,128)(2,1)S(1)}, u32[]{:S(2)}, u32[]{:S(2)}) collective-permute-start(bf16[16,2048]{1,0:T(8,128)(2,1)S(1)} %get-tuple-element.35), channel_id=1, source_target_pairs={{0,5},{1,4},{2,7},{3,6},{4,1},{5,0},{6,3},{7,2},{8,13},{9,12},{10,... | collective-permute-start | bytes 196616 | tf_op jit(solution)/shard_map/ppermute | solution.py:254
  6.7 4.4 %collective-permute-start.5 = (bf16[16,2048]{1,0:T(8,128)(2,1)S(1)}, bf16[16,2048]{1,0:T(8,128)(2,1)S(1)}, u32[]{:S(2)}, u32[]{:S(2)}) collective-permute-start(bf16[16,2048]{1,0:T(8,128)(2,1)S(1)} %get-tuple-element.36), channel_id=1, source_target_pairs={{0,7},{1,6},{2,1},{3,0},{4,3},{5,2},{6,5},{7,4},{8,15},{9,14},{10,... | collective-permute-start | bytes 196616 | tf_op jit(solution)/shard_map/ppermute | solution.py:254
  7.8 5.6 %collective-permute-start.3 = (bf16[16,2048]{1,0:T(8,128)(2,1)S(1)}, bf16[16,2048]{1,0:T(8,128)(2,1)S(1)}, u32[]{:S(2)}, u32[]{:S(2)}) collective-permute-start(bf16[16,2048]{1,0:T(8,128)(2,1)S(1)} %get-tuple-element.34), channel_id=1, source_target_pairs={{0,3},{1,2},{2,5},{3,4},{4,7},{5,6},{6,1},{7,0},{8,11},{9,10},{10,... | collective-permute-start | bytes 196616 | tf_op jit(solution)/shard_map/ppermute | solution.py:254
  15.5 4.7 %collective-permute-start.6 = (bf16[32,2560]{1,0:T(8,128)(2,1)S(1)}, bf16[32,2560]{1,0:T(8,128)(2,1)S(1)}, u32[]{:S(2)}, u32[]{:S(2)}) collective-permute-start(bf16[32,2560]{1,0:T(8,128)(2,1)S(1)} %get-tuple-element.46), channel_id=1, source_target_pairs={{0,1},{1,0},{2,3},{3,2},{4,5},{5,4},{6,7},{7,6},{8,9},{9,8},{10,11... | collective-permute-start | bytes 491528 | tf_op jit(solution)/shard_map/ppermute | solution.py:196
  15.9 7.0 %collective-permute-start.7 = (bf16[8,2048]{1,0:T(8,128)(2,1)S(1)}, bf16[8,2048]{1,0:T(8,128)(2,1)S(1)}, u32[]{:S(2)}, u32[]{:S(2)}) collective-permute-start(bf16[8,2048]{1,0:T(8,128)(2,1)S(1)} %get-tuple-element.48), channel_id=1, source_target_pairs={{0,7},{1,6},{2,1},{3,0},{4,3},{5,2},{6,5},{7,4},{8,15},{9,14},{10,... | collective-permute-start | bytes 98312 | tf_op jit(solution)/shard_map/ppermute | solution.py:254
  18.3 4.6 %collective-permute-start.8 = (bf16[8,2048]{1,0:T(8,128)(2,1)S(1)}, bf16[8,2048]{1,0:T(8,128)(2,1)S(1)}, u32[]{:S(2)}, u32[]{:S(2)}) collective-permute-start(bf16[8,2048]{1,0:T(8,128)(2,1)S(1)} %get-tuple-element.49), channel_id=1, source_target_pairs={{0,5},{1,4},{2,7},{3,6},{4,1},{5,0},{6,3},{7,2},{8,13},{9,12},{10,... | collective-permute-start | bytes 98312 | tf_op jit(solution)/shard_map/ppermute | solution.py:254
  18.4 5.1 %collective-permute-start.9 = (bf16[8,2048]{1,0:T(8,128)(2,1)S(1)}, bf16[8,2048]{1,0:T(8,128)(2,1)S(1)}, u32[]{:S(2)}, u32[]{:S(2)}) collective-permute-start(bf16[8,2048]{1,0:T(8,128)(2,1)S(1)} %get-tuple-element.50), channel_id=1, source_target_pairs={{0,3},{1,2},{2,5},{3,4},{4,7},{5,6},{6,1},{7,0},{8,11},{9,10},{10,... | collective-permute-start | bytes 98312 | tf_op jit(solution)/shard_map/ppermute | solution.py:254

commit v7 on v6

--- a/solution.py
+++ b/solution.py
@@ -54,6 +54,15 @@
             slots.append((relative, batch * capacity + position))
         found.append(slots)
     return found
+
+
+def ring_place(expert, experts):
+    back = jnp.where(expert == 0, 0, experts - expert // 2)
+    return jnp.where(expert % 2 == 1, (expert + 1) // 2, back)
+
+
+def ring_order(experts):
+    return [0, *range(1, experts, 2), *reversed(range(2, experts, 2))]
 
 
 def route_picks(routes, gates, base, experts, capacity):
@@ -219,9 +228,9 @@
         for copy in copies[:2]:
             copy.wait()
         picks, gate, pick = route_picks(
-            [routes_ref[m] for m in range(batches)],
+            [ring_place(routes_ref[m], experts) for m in range(batches)],
             [gates_ref[m] for m in range(batches)],
-            lax.axis_index("expert"), experts, capacity,
+            ring_place(lax.axis_index("expert"), experts), experts, capacity,
         )
         pick_ref[...] = pick
         for copy in copies[2:]:
@@ -246,16 +255,22 @@
 
     def shift(value, by):
         halves = lax.axis_size("half")
+        ring = ring_order(experts)
         pairs = [
-            (i * halves + h, (i + by) % experts * halves + halves - 1 - h)
+            (ring[i] * halves + h, ring[(i + by) % experts] * halves + halves - 1 - h)
             for i in range(experts)
             for h in range(halves)
         ]
         return lax.ppermute(value, ("expert", "half"), pairs)
 
-    blocks[1], far[0] = lax.optimization_barrier((blocks[1], far[0]))
-    got = [shift(blocks[d], d) for d in range(experts - 1, 0, -1)]
-    got = [blocks[0]] + got[::-1]
+    middle = experts // 2
+    order = [*range(max(1, middle), experts), *range(middle - 1, 0, -1)]
+    if order:
+        last = order[-1]
+        blocks[last], far[0] = lax.optimization_barrier((blocks[last], far[0]))
+    got = list(blocks)
+    for d in order:
+        got[d] = shift(blocks[d], d)
 
     turned_shapes = [
         kept((units, width), BF16), kept((units, width), BF16), kept((width, units), BF16)
@@ -308,7 +323,9 @@
         [vmem(v) for v in (*got, *near, *far)],
         2 * slots * width * units * 10,
     )
-    back = [grads[0]] + [shift(grads[d], experts - d) for d in range(1, experts)]
+    back = list(grads)
+    for d in order:
+        back[d] = shift(grads[d], experts - d)
     theirs = swap_half(to_other)
 
     chunk = width // CHUNKS

time: 24.5 us -> 24.1 us (0.984)
  waiting for transfers between devices: 2.98 us -> 2.16 us
  starting transfers between devices: 11.2 us -> 11.7 us
    ppermute x6, waiting for transfers between devices: 2.97 us -> 2.15 us  [shift(): return lax.ppermute(value, ('expert', 'half'), pairs)]
    ppermute x6, starting transfers between devices: 9.77 us -> 10.5 us  [shift(): return lax.ppermute(value, ('expert', 'half'), pairs)]
    ppermute x4, starting transfers between devices: 1.47 us -> 1.21 us  [swap_half(): lax.ppermute(value, 'half', [(i, (i + 1) % halves) for i in range(halves)])]
  transfers between devices with their start and end apart: 10 -> 10, of which waited for: 3 -> 2; matrix products, arithmetic and copies ran while one was open for 0% -> 0% of each run, Pallas kernels for 27% -> 27%
where the time goes in v7:
time: 24.1 us; the launch traced here: 23.9 us
  starting transfers between devices  11.7 us (49%)
  Pallas kernels  9.41 us (39%)
  waiting for transfers between devices  2.16 us (9%)
  between operations  0.7 us (3%)
    ppermute x6, starting transfers between devices, shift(): return lax.ppermute(value, ('expert', 'half'), pairs)  10.5 us
    pallas_call x4, Pallas kernels, call(): pl.pallas_call(body, out_shape=shapes, in_specs=specs or [IN_VMEM] * len(...  6.66 us
    pallas_call x1, Pallas kernels, small_program(): pl.pallas_call(core_body, out_shape=jax.ShapeDtypeStruct((units, width),...  2.75 us
    ppermute x6, waiting for transfers between devices, shift(): return lax.ppermute(value, ('expert', 'half'), pairs)  2.15 us
    ppermute x4, starting transfers between devices, swap_half(): lax.ppermute(value, 'half', [(i, (i + 1) % halves) for i in range(halves)])  1.21 us
  transfers between devices with their start and end apart: 10, of which 2 were waited for; matrix products, arithmetic and copies ran while one was open for 0% of the time, Pallas kernels for 27%

profile of v7, /device:TPU:0, one launch (start us, length us, event | category | flops | bytes accessed | tf_op | source)
XLA Modules:
  0.0 23.9 jit_solution(12384110150163913736)
XLA Ops:
  0.6 0.5 %collective-permute-start = (bf16[2048,256]{1,0:T(8,128)(2,1)}, bf16[2048,256]{1,0:T(8,128)(2,1)S(1)}, u32[]{:S(2)}, u32[]{:S(2)}) collective-permute-start(bf16[2048,256]{1,0:T(8,128)(2,1)} %bitcast.10), channel_id=1, source_target_pairs={{0,1},{1,0},{2,3},{3,2},{4,5},{5,4},{6,7},{7,6},{8,9},{9,8},{10,11... | collective-permute-start | bytes 3145736 | tf_op jit(solution)/shard_map/ppermute | solution.py:205
  1.1 0.1 collective-permute-start.1
  1.2 0.4 %collective-permute-start.2 = (bf16[256,2048]{1,0:T(8,128)(2,1)}, bf16[256,2048]{1,0:T(8,128)(2,1)S(1)}, u32[]{:S(2)}, u32[]{:S(2)}) collective-permute-start(bf16[256,2048]{1,0:T(8,128)(2,1)} %bitcast.14), channel_id=1, source_target_pairs={{0,1},{1,0},{2,3},{3,2},{4,5},{5,4},{6,7},{7,6},{8,9},{9,8},{10,11... | collective-permute-start | bytes 3145736 | tf_op jit(solution)/shard_map/ppermute | solution.py:205
  1.7 1.3 %shard_map.86 = (bf16[16,2048]{1,0:T(8,128)(2,1)S(1)}, bf16[16,2048]{1,0:T(8,128)(2,1)S(1)}, bf16[16,2048]{1,0:T(8,128)(2,1)S(1)}, bf16[16,2048]{1,0:T(8,128)(2,1)S(1)}, f32[32,16]{1,0:T(8,128)S(1)}) custom-call(bf16[16,2048]{1,0:T(8,128)(2,1)} %bitcast.17, bf16[16,2048]{1,0:T(8,128)(2,1)} %bitcast.18, s32[2,2,8]{2,1,0:T(2,128)} %bitcast.19, f32[2,2,8]{2,1,0:T(2,128)} %bitcast.20), custom_call_target="tpu_custom_call" | custom-call | flops 10000000 | tf_op jit(solution)/shard_map/pallas_call | solution.py:180
  2.9 4.8 %collective-permute-start.4 = (bf16[16,2048]{1,0:T(8,128)(2,1)S(1)}, bf16[16,2048]{1,0:T(8,128)(2,1)S(1)}, u32[]{:S(2)}, u32[]{:S(2)}) collective-permute-start(bf16[16,2048]{1,0:T(8,128)(2,1)S(1)} %get-tuple-element.35), channel_id=1, source_target_pairs={{0,7},{1,6},{2,5},{3,4},{6,1},{7,0},{4,3},{5,2},{8,15},{9,14},{10,... | collective-permute-start | bytes 196616 | tf_op jit(solution)/shard_map/ppermute | solution.py:264
  7.7 0.0 collective-permute-start.5
  7.7 0.0 collective-permute-done.refs_3_.refs_9_
  7.7 1.7 %collective-permute-start.3 = (bf16[16,2048]{1,0:T(8,128)(2,1)S(1)}, bf16[16,2048]{1,0:T(8,128)(2,1)S(1)}, u32[]{:S(2)}, u32[]{:S(2)}) collective-permute-start(bf16[16,2048]{1,0:T(8,128)(2,1)S(1)} %get-tuple-element.34), channel_id=1, source_target_pairs={{0,3},{1,2},{2,7},{3,6},{6,5},{7,4},{4,1},{5,0},{8,11},{9,10},{10,... | collective-permute-start | bytes 196616 | tf_op jit(solution)/shard_map/ppermute | solution.py:264
  9.4 0.0 collective-permute-done.1.refs_4_.refs_10_
  9.5 0.0 collective-permute-done.2.refs_5_
  9.5 2.6 %shard_map.87 = (bf16[2048,256]{1,0:T(8,128)(2,1)S(1)}, bf16[2048,256]{1,0:T(8,128)(2,1)S(1)}, bf16[256,2048]{1,0:T(8,128)(2,1)S(1)}, bf16[256,2048]{1,0:T(8,128...) custom-call(f32[32,16]{1,0:T(8,128)S(1)} %get-tuple-element.29.pick_, ...), custom_call_target="tpu_custom_call" | custom-call | flops 1000000000 | tf_op jit(solution)/shard_map/pallas_call | solution.py:180
  12.0 0.0 collective-permute-done.4.refs_2_
  12.0 0.0 collective-permute-done.5.refs_3_
  12.0 1.5 %collective-permute-done.3.refs_1_ = bf16[16,2048]{1,0:T(8,128)(2,1)S(1)} collective-permute-done((bf16[16,2048]{1,0:T(8,128)(2,1)S(1)}, bf16[16,2048]{1,0:T(8,128)(2,1)S(1)}, u32[]{:S(2)}, u32[]{:S(2)}) %collective-permute-start.3) | collective-permute-done | bytes 65568 | tf_op jit(solution)/shard_map/ppermute | solution.py:264
  13.5 2.1 %shard_map.88 = (bf16[32,2560]{1,0:T(8,128)(2,1)S(1)}, bf16[32,2560]{1,0:T(8,128)(2,1)S(1)}, bf16[8,2048]{1,0:T(8,128)(2,1)S(1)}, bf16[8,2048]{1,0:T(8,128)(2,1)...) custom-call(bf16[16,2048]{1,0:T(8,128)(2,1)S(1)} %get-tuple-element.33.refs_0_, ...), custom_call_target="tpu_custom_call" | custom-call | flops 335544320 | tf_op jit(solution)/shard_map/pallas_call | solution.py:180
  15.6 0.2 collective-permute-start.6
  15.8 0.8 %collective-permute-start.7 = (bf16[8,2048]{1,0:T(8,128)(2,1)S(1)}, bf16[8,2048]{1,0:T(8,128)(2,1)S(1)}, u32[]{:S(2)}, u32[]{:S(2)}) collective-permute-start(bf16[8,2048]{1,0:T(8,128)(2,1)S(1)} %get-tuple-element.48), channel_id=1, source_target_pairs={{0,5},{1,4},{2,1},{3,0},{6,3},{7,2},{4,7},{5,6},{8,13},{9,12},{10,... | collective-permute-start | bytes 98312 | tf_op jit(solution)/shard_map/ppermute | solution.py:264
  16.6 2.4 %collective-permute-start.8 = (bf16[8,2048]{1,0:T(8,128)(2,1)S(1)}, bf16[8,2048]{1,0:T(8,128)(2,1)S(1)}, u32[]{:S(2)}, u32[]{:S(2)}) collective-permute-start(bf16[8,2048]{1,0:T(8,128)(2,1)S(1)} %get-tuple-element.49), channel_id=1, source_target_pairs={{0,7},{1,6},{2,5},{3,4},{6,1},{7,0},{4,3},{5,2},{8,15},{9,14},{10,... | collective-permute-start | bytes 98312 | tf_op jit(solution)/shard_map/ppermute | solution.py:264
  18.9 0.8 %collective-permute-start.9 = (bf16[8,2048]{1,0:T(8,128)(2,1)S(1)}, bf16[8,2048]{1,0:T(8,128)(2,1)S(1)}, u32[]{:S(2)}, u32[]{:S(2)}) collective-permute-start(bf16[8,2048]{1,0:T(8,128)(2,1)S(1)} %get-tuple-element.50), channel_id=1, source_target_pairs={{0,3},{1,2},{2,7},{3,6},{6,5},{7,4},{4,1},{5,0},{8,11},{9,10},{10,... | collective-permute-start | bytes 98312 | tf_op jit(solution)/shard_map/ppermute | solution.py:264
  19.7 0.0 collective-permute-done.6.theirs_ref
  19.7 2.8 %shard_map.89 = bf16[256,2048]{1,0:T(8,128)(2,1)} custom-call(bf16[32,2560]{1,0:T(8,128)(2,1)S(1)} %get-tuple-element.45.mine_ref, bf16[32,2560]{1,0:T(8,128)(2,1)S(1)} %collective-permute-done.6.theirs_ref), custom_call_target="tpu_custom_call" | custom-call | flops 268435456 | tf_op jit(solution)/shard_map/pallas_call | solution.py:351
  22.5 0.0 collective-permute-done.7.refs_1_
  22.5 0.0 collective-permute-done.8.refs_2_
  22.5 0.7 %collective-permute-done.9.refs_3_ = bf16[8,2048]{1,0:T(8,128)(2,1)S(1)} collective-permute-done((bf16[8,2048]{1,0:T(8,128)(2,1)S(1)}, bf16[8,2048]{1,0:T(8,128)(2,1)S(1)}, u32[]{:S(2)}, u32[]{:S(2)}) %collective-permute-start.9) | collective-permute-done | bytes 32800 | tf_op jit(solution)/shard_map/ppermute | solution.py:264
  23.2 0.8 %shard_map.90 = bf16[16,2048]{1,0:T(8,128)(2,1)} custom-call(bf16[16,32]{1,0:T(8,128)(2,1)S(1)} %get-tuple-element.32.pick_ref, bf16[8,2048]{1,0:T(8,128)(2,1)S(1)} %get-tuple-element.51.refs_0_, bf16[8,2048]{1,0:T(8,128)(2,1)S(1)} %collective-permute-done.7.refs_1_, bf16[8,2048]{1,0:T(8,128)(2,1)S(1)} %collective-permute-done.8.refs_2_, ...), custom_call_target="tpu_custom_call" | custom-call | flops 1000000 | tf_op jit(solution)/shard_map/pallas_call | solution.py:180
Async XLA Ops:
  0.6 7.1 %collective-permute-start = (bf16[2048,256]{1,0:T(8,128)(2,1)}, bf16[2048,256]{1,0:T(8,128)(2,1)S(1)}, u32[]{:S(2)}, u32[]{:S(2)}) collective-permute-start(bf16[2048,256]{1,0:T(8,128)(2,1)} %bitcast.10), channel_id=1, source_target_pairs={{0,1},{1,0},{2,3},{3,2},{4,5},{5,4},{6,7},{7,6},{8,9},{9,8},{10,11... | collective-permute-start | bytes 3145736 | tf_op jit(solution)/shard_map/ppermute | solution.py:205
  1.1 8.3 %collective-permute-start.1 = (bf16[2048,256]{1,0:T(8,128)(2,1)}, bf16[2048,256]{1,0:T(8,128)(2,1)S(1)}, u32[]{:S(2)}, u32[]{:S(2)}) collective-permute-start(bf16[2048,256]{1,0:T(8,128)(2,1)} %bitcast.12), channel_id=1, source_target_pairs={{0,1},{1,0},{2,3},{3,2},{4,5},{5,4},{6,7},{7,6},{8,9},{9,8},{10,11... | collective-permute-start | bytes 3145736 | tf_op jit(solution)/shard_map/ppermute | solution.py:205
  1.2 8.2 %collective-permute-start.2 = (bf16[256,2048]{1,0:T(8,128)(2,1)}, bf16[256,2048]{1,0:T(8,128)(2,1)S(1)}, u32[]{:S(2)}, u32[]{:S(2)}) collective-permute-start(bf16[256,2048]{1,0:T(8,128)(2,1)} %bitcast.14), channel_id=1, source_target_pairs={{0,1},{1,0},{2,3},{3,2},{4,5},{5,4},{6,7},{7,6},{8,9},{9,8},{10,11... | collective-permute-start | bytes 3145736 | tf_op jit(solution)/shard_map/ppermute | solution.py:205
  2.9 9.1 %collective-permute-start.4 = (bf16[16,2048]{1,0:T(8,128)(2,1)S(1)}, bf16[16,2048]{1,0:T(8,128)(2,1)S(1)}, u32[]{:S(2)}, u32[]{:S(2)}) collective-permute-start(bf16[16,2048]{1,0:T(8,128)(2,1)S(1)} %get-tuple-element.35), channel_id=1, source_target_pairs={{0,7},{1,6},{2,5},{3,4},{6,1},{7,0},{4,3},{5,2},{8,15},{9,14},{10,... | collective-permute-start | bytes 196616 | tf_op jit(solution)/shard_map/ppermute | solution.py:264
  7.7 4.3 %collective-permute-start.5 = (bf16[16,2048]{1,0:T(8,128)(2,1)S(1)}, bf16[16,2048]{1,0:T(8,128)(2,1)S(1)}, u32[]{:S(2)}, u32[]{:S(2)}) collective-permute-start(bf16[16,2048]{1,0:T(8,128)(2,1)S(1)} %get-tuple-element.36), channel_id=1, source_target_pairs={{0,5},{1,4},{2,1},{3,0},{6,3},{7,2},{4,7},{5,6},{8,13},{9,12},{10,... | collective-permute-start | bytes 196616 | tf_op jit(solution)/shard_map/ppermute | solution.py:264
  7.7 5.8 %collective-permute-start.3 = (bf16[16,2048]{1,0:T(8,128)(2,1)S(1)}, bf16[16,2048]{1,0:T(8,128)(2,1)S(1)}, u32[]{:S(2)}, u32[]{:S(2)}) collective-permute-start(bf16[16,2048]{1,0:T(8,128)(2,1)S(1)} %get-tuple-element.34), channel_id=1, source_target_pairs={{0,3},{1,2},{2,7},{3,6},{6,5},{7,4},{4,1},{5,0},{8,11},{9,10},{10,... | collective-permute-start | bytes 196616 | tf_op jit(solution)/shard_map/ppermute | solution.py:264
  15.6 4.1 %collective-permute-start.6 = (bf16[32,2560]{1,0:T(8,128)(2,1)S(1)}, bf16[32,2560]{1,0:T(8,128)(2,1)S(1)}, u32[]{:S(2)}, u32[]{:S(2)}) collective-permute-start(bf16[32,2560]{1,0:T(8,128)(2,1)S(1)} %get-tuple-element.46), channel_id=1, source_target_pairs={{0,1},{1,0},{2,3},{3,2},{4,5},{5,4},{6,7},{7,6},{8,9},{9,8},{10,11... | collective-permute-start | bytes 491528 | tf_op jit(solution)/shard_map/ppermute | solution.py:205
  15.8 6.7 %collective-permute-start.7 = (bf16[8,2048]{1,0:T(8,128)(2,1)S(1)}, bf16[8,2048]{1,0:T(8,128)(2,1)S(1)}, u32[]{:S(2)}, u32[]{:S(2)}) collective-permute-start(bf16[8,2048]{1,0:T(8,128)(2,1)S(1)} %get-tuple-element.48), channel_id=1, source_target_pairs={{0,5},{1,4},{2,1},{3,0},{6,3},{7,2},{4,7},{5,6},{8,13},{9,12},{10,... | collective-permute-start | bytes 98312 | tf_op jit(solution)/shard_map/ppermute | solution.py:264
  16.6 5.9 %collective-permute-start.8 = (bf16[8,2048]{1,0:T(8,128)(2,1)S(1)}, bf16[8,2048]{1,0:T(8,128)(2,1)S(1)}, u32[]{:S(2)}, u32[]{:S(2)}) collective-permute-start(bf16[8,2048]{1,0:T(8,128)(2,1)S(1)} %get-tuple-element.49), channel_id=1, source_target_pairs={{0,7},{1,6},{2,5},{3,4},{6,1},{7,0},{4,3},{5,2},{8,15},{9,14},{10,... | collective-permute-start | bytes 98312 | tf_op jit(solution)/shard_map/ppermute | solution.py:264
  18.9 4.3 %collective-permute-start.9 = (bf16[8,2048]{1,0:T(8,128)(2,1)S(1)}, bf16[8,2048]{1,0:T(8,128)(2,1)S(1)}, u32[]{:S(2)}, u32[]{:S(2)}) collective-permute-start(bf16[8,2048]{1,0:T(8,128)(2,1)S(1)} %get-tuple-element.50), channel_id=1, source_target_pairs={{0,3},{1,2},{2,7},{3,6},{6,5},{7,4},{4,1},{5,0},{8,11},{9,10},{10,... | collective-permute-start | bytes 98312 | tf_op jit(solution)/shard_map/ppermute | solution.py:264

commit v8 on v7

--- a/solution.py
+++ b/solution.py
@@ -213,7 +213,7 @@
     slots = experts * block
     units = own[0].shape[1]
 
-    far = [swap_half(w) for w in own]
+    far = [swap_half(own[0])]
 
     def dispatch_body(x_hbm, u_hbm, routes_hbm, gates_hbm, *refs):
         *outs, pick_ref, data, routes_ref, gates_ref, sems = refs
@@ -263,6 +263,8 @@
         ]
         return lax.ppermute(value, ("expert", "half"), pairs)
 
+    later, pick = lax.optimization_barrier((list(own[1:]), pick))
+    far += [swap_half(w) for w in later]
     middle = experts // 2
     order = [*range(max(1, middle), experts), *range(middle - 1, 0, -1)]
     if order:

time: 24.1 us -> 24.1 us (level)
  no operation moved by 1% of the time
where the time goes in v8:
time: 24.1 us; the launch traced here: 23.9 us
  starting transfers between devices  11.7 us (49%)
  Pallas kernels  9.4 us (39%)
  waiting for transfers between devices  2.15 us (9%)
  between operations  0.7 us (3%)
    ppermute x6, starting transfers between devices, shift(): return lax.ppermute(value, ('expert', 'half'), pairs)  10.4 us
    pallas_call x4, Pallas kernels, call(): pl.pallas_call(body, out_shape=shapes, in_specs=specs or [IN_VMEM] * len(...  6.64 us
    pallas_call x1, Pallas kernels, small_program(): pl.pallas_call(core_body, out_shape=jax.ShapeDtypeStruct((units, width),...  2.75 us
    ppermute x6, waiting for transfers between devices, shift(): return lax.ppermute(value, ('expert', 'half'), pairs)  2.14 us
    ppermute x4, starting transfers between devices, swap_half(): lax.ppermute(value, 'half', [(i, (i + 1) % halves) for i in range(halves)])  1.28 us
  transfers between devices with their start and end apart: 10, of which 2 were waited for; matrix products, arithmetic and copies ran while one was open for 0% of the time, Pallas kernels for 27%

profile of v8, /device:TPU:0, one launch (start us, length us, event | category | flops | bytes accessed | tf_op | source)
XLA Modules:
  0.0 23.9 jit_solution(2933626992758578852)
XLA Ops:
  0.6 0.5 %collective-permute-start = (bf16[2048,256]{1,0:T(8,128)(2,1)}, bf16[2048,256]{1,0:T(8,128)(2,1)S(1)}, u32[]{:S(2)}, u32[]{:S(2)}) collective-permute-start(bf16[2048,256]{1,0:T(8,128)(2,1)} %bitcast.10), channel_id=1, source_target_pairs={{0,1},{1,0},{2,3},{3,2},{4,5},{5,4},{6,7},{7,6},{8,9},{9,8},{10,11... | collective-permute-start | bytes 3145736 | tf_op jit(solution)/shard_map/ppermute | solution.py:205
  1.1 1.2 %shard_map.86 = (bf16[16,2048]{1,0:T(8,128)(2,1)S(1)}, bf16[16,2048]{1,0:T(8,128)(2,1)S(1)}, bf16[16,2048]{1,0:T(8,128)(2,1)S(1)}, bf16[16,2048]{1,0:T(8,128)(2,1)S(1)}, f32[32,16]{1,0:T(8,128)S(1)}) custom-call(bf16[16,2048]{1,0:T(8,128)(2,1)} %bitcast.17, bf16[16,2048]{1,0:T(8,128)(2,1)} %bitcast.18, s32[2,2,8]{2,1,0:T(2,128)} %bitcast.19, f32[2,2,8]{2,1,0:T(2,128)} %bitcast.20), custom_call_target="tpu_custom_call" | custom-call | flops 10000000 | tf_op jit(solution)/shard_map/pallas_call | solution.py:180
  2.4 0.1 collective-permute-start.1
  2.5 0.4 %collective-permute-start.2 = (bf16[256,2048]{1,0:T(8,128)(2,1)}, bf16[256,2048]{1,0:T(8,128)(2,1)S(1)}, u32[]{:S(2)}, u32[]{:S(2)}) collective-permute-start(bf16[256,2048]{1,0:T(8,128)(2,1)} %bitcast.14), channel_id=1, source_target_pairs={{0,1},{1,0},{2,3},{3,2},{4,5},{5,4},{6,7},{7,6},{8,9},{9,8},{10,11... | collective-permute-start | bytes 3145736 | tf_op jit(solution)/shard_map/ppermute | solution.py:205
  3.0 4.7 %collective-permute-start.4 = (bf16[16,2048]{1,0:T(8,128)(2,1)S(1)}, bf16[16,2048]{1,0:T(8,128)(2,1)S(1)}, u32[]{:S(2)}, u32[]{:S(2)}) collective-permute-start(bf16[16,2048]{1,0:T(8,128)(2,1)S(1)} %get-tuple-element.41), channel_id=1, source_target_pairs={{0,7},{1,6},{2,5},{3,4},{6,1},{7,0},{4,3},{5,2},{8,15},{9,14},{10,... | collective-permute-start | bytes 196616 | tf_op jit(solution)/shard_map/ppermute | solution.py:264
  7.7 0.0 collective-permute-start.5
  7.7 0.0 collective-permute-done.refs_3_.refs_9_
  7.7 1.7 %collective-permute-start.3 = (bf16[16,2048]{1,0:T(8,128)(2,1)S(1)}, bf16[16,2048]{1,0:T(8,128)(2,1)S(1)}, u32[]{:S(2)}, u32[]{:S(2)}) collective-permute-start(bf16[16,2048]{1,0:T(8,128)(2,1)S(1)} %get-tuple-element.40), channel_id=1, source_target_pairs={{0,3},{1,2},{2,7},{3,6},{6,5},{7,4},{4,1},{5,0},{8,11},{9,10},{10,... | collective-permute-start | bytes 196616 | tf_op jit(solution)/shard_map/ppermute | solution.py:264
  9.5 0.0 collective-permute-done.1.refs_4_.refs_10_
  9.5 0.0 collective-permute-done.2.refs_5_
  9.5 2.6 %shard_map.87 = (bf16[2048,256]{1,0:T(8,128)(2,1)S(1)}, bf16[2048,256]{1,0:T(8,128)(2,1)S(1)}, bf16[256,2048]{1,0:T(8,128)(2,1)S(1)}, bf16[256,2048]{1,0:T(8,128...) custom-call(f32[32,16]{1,0:T(8,128)S(1)} %get-tuple-element.33.pick_, ...), custom_call_target="tpu_custom_call" | custom-call | flops 1000000000 | tf_op jit(solution)/shard_map/pallas_call | solution.py:180
  12.0 0.0 collective-permute-done.4.refs_2_
  12.0 0.0 collective-permute-done.5.refs_3_
  12.0 1.5 %collective-permute-done.3.refs_1_ = bf16[16,2048]{1,0:T(8,128)(2,1)S(1)} collective-permute-done((bf16[16,2048]{1,0:T(8,128)(2,1)S(1)}, bf16[16,2048]{1,0:T(8,128)(2,1)S(1)}, u32[]{:S(2)}, u32[]{:S(2)}) %collective-permute-start.3) | collective-permute-done | bytes 65568 | tf_op jit(solution)/shard_map/ppermute | solution.py:264
  13.5 2.1 %shard_map.88 = (bf16[32,2560]{1,0:T(8,128)(2,1)S(1)}, bf16[32,2560]{1,0:T(8,128)(2,1)S(1)}, bf16[8,2048]{1,0:T(8,128)(2,1)S(1)}, bf16[8,2048]{1,0:T(8,128)(2,1)...) custom-call(bf16[16,2048]{1,0:T(8,128)(2,1)S(1)} %get-tuple-element.39.refs_0_, ...), custom_call_target="tpu_custom_call" | custom-call | flops 335544320 | tf_op jit(solution)/shard_map/pallas_call | solution.py:180
  15.6 0.2 collective-permute-start.6
  15.8 0.8 %collective-permute-start.7 = (bf16[8,2048]{1,0:T(8,128)(2,1)S(1)}, bf16[8,2048]{1,0:T(8,128)(2,1)S(1)}, u32[]{:S(2)}, u32[]{:S(2)}) collective-permute-start(bf16[8,2048]{1,0:T(8,128)(2,1)S(1)} %get-tuple-element.54), channel_id=1, source_target_pairs={{0,5},{1,4},{2,1},{3,0},{6,3},{7,2},{4,7},{5,6},{8,13},{9,12},{10,... | collective-permute-start | bytes 98312 | tf_op jit(solution)/shard_map/ppermute | solution.py:264
  16.6 2.3 %collective-permute-start.8 = (bf16[8,2048]{1,0:T(8,128)(2,1)S(1)}, bf16[8,2048]{1,0:T(8,128)(2,1)S(1)}, u32[]{:S(2)}, u32[]{:S(2)}) collective-permute-start(bf16[8,2048]{1,0:T(8,128)(2,1)S(1)} %get-tuple-element.55), channel_id=1, source_target_pairs={{0,7},{1,6},{2,5},{3,4},{6,1},{7,0},{4,3},{5,2},{8,15},{9,14},{10,... | collective-permute-start | bytes 98312 | tf_op jit(solution)/shard_map/ppermute | solution.py:264
  18.9 0.8 %collective-permute-start.9 = (bf16[8,2048]{1,0:T(8,128)(2,1)S(1)}, bf16[8,2048]{1,0:T(8,128)(2,1)S(1)}, u32[]{:S(2)}, u32[]{:S(2)}) collective-permute-start(bf16[8,2048]{1,0:T(8,128)(2,1)S(1)} %get-tuple-element.56), channel_id=1, source_target_pairs={{0,3},{1,2},{2,7},{3,6},{6,5},{7,4},{4,1},{5,0},{8,11},{9,10},{10,... | collective-permute-start | bytes 98312 | tf_op jit(solution)/shard_map/ppermute | solution.py:264
  19.7 0.0 collective-permute-done.6.theirs_ref
  19.7 2.8 %shard_map.89 = bf16[256,2048]{1,0:T(8,128)(2,1)} custom-call(bf16[32,2560]{1,0:T(8,128)(2,1)S(1)} %get-tuple-element.51.mine_ref, bf16[32,2560]{1,0:T(8,128)(2,1)S(1)} %collective-permute-done.6.theirs_ref), custom_call_target="tpu_custom_call" | custom-call | flops 268435456 | tf_op jit(solution)/shard_map/pallas_call | solution.py:353
  22.5 0.0 collective-permute-done.7.refs_1_
  22.5 0.0 collective-permute-done.8.refs_2_
  22.5 0.7 %collective-permute-done.9.refs_3_ = bf16[8,2048]{1,0:T(8,128)(2,1)S(1)} collective-permute-done((bf16[8,2048]{1,0:T(8,128)(2,1)S(1)}, bf16[8,2048]{1,0:T(8,128)(2,1)S(1)}, u32[]{:S(2)}, u32[]{:S(2)}) %collective-permute-start.9) | collective-permute-done | bytes 32800 | tf_op jit(solution)/shard_map/ppermute | solution.py:264
  23.2 0.8 %shard_map.90 = bf16[16,2048]{1,0:T(8,128)(2,1)} custom-call(bf16[16,32]{1,0:T(8,128)(2,1)S(1)} %get-tuple-element.38.pick_ref, bf16[8,2048]{1,0:T(8,128)(2,1)S(1)} %get-tuple-element.57.refs_0_, bf16[8,2048]{1,0:T(8,128)(2,1)S(1)} %collective-permute-done.7.refs_1_, bf16[8,2048]{1,0:T(8,128)(2,1)S(1)} %collective-permute-done.8.refs_2_, ...), custom_call_target="tpu_custom_call" | custom-call | flops 1000000 | tf_op jit(solution)/shard_map/pallas_call | solution.py:180
Async XLA Ops:
  0.6 7.1 %collective-permute-start = (bf16[2048,256]{1,0:T(8,128)(2,1)}, bf16[2048,256]{1,0:T(8,128)(2,1)S(1)}, u32[]{:S(2)}, u32[]{:S(2)}) collective-permute-start(bf16[2048,256]{1,0:T(8,128)(2,1)} %bitcast.10), channel_id=1, source_target_pairs={{0,1},{1,0},{2,3},{3,2},{4,5},{5,4},{6,7},{7,6},{8,9},{9,8},{10,11... | collective-permute-start | bytes 3145736 | tf_op jit(solution)/shard_map/ppermute | solution.py:205
  2.4 7.1 %collective-permute-start.1 = (bf16[2048,256]{1,0:T(8,128)(2,1)}, bf16[2048,256]{1,0:T(8,128)(2,1)S(1)}, u32[]{:S(2)}, u32[]{:S(2)}) collective-permute-start(bf16[2048,256]{1,0:T(8,128)(2,1)} %bitcast.12), channel_id=1, source_target_pairs={{0,1},{1,0},{2,3},{3,2},{4,5},{5,4},{6,7},{7,6},{8,9},{9,8},{10,11... | collective-permute-start | bytes 3145736 | tf_op jit(solution)/shard_map/ppermute | solution.py:205
  2.5 6.9 %collective-permute-start.2 = (bf16[256,2048]{1,0:T(8,128)(2,1)}, bf16[256,2048]{1,0:T(8,128)(2,1)S(1)}, u32[]{:S(2)}, u32[]{:S(2)}) collective-permute-start(bf16[256,2048]{1,0:T(8,128)(2,1)} %bitcast.14), channel_id=1, source_target_pairs={{0,1},{1,0},{2,3},{3,2},{4,5},{5,4},{6,7},{7,6},{8,9},{9,8},{10,11... | collective-permute-start | bytes 3145736 | tf_op jit(solution)/shard_map/ppermute | solution.py:205
  3.0 9.1 %collective-permute-start.4 = (bf16[16,2048]{1,0:T(8,128)(2,1)S(1)}, bf16[16,2048]{1,0:T(8,128)(2,1)S(1)}, u32[]{:S(2)}, u32[]{:S(2)}) collective-permute-start(bf16[16,2048]{1,0:T(8,128)(2,1)S(1)} %get-tuple-element.41), channel_id=1, source_target_pairs={{0,7},{1,6},{2,5},{3,4},{6,1},{7,0},{4,3},{5,2},{8,15},{9,14},{10,... | collective-permute-start | bytes 196616 | tf_op jit(solution)/shard_map/ppermute | solution.py:264
  7.7 4.3 %collective-permute-start.5 = (bf16[16,2048]{1,0:T(8,128)(2,1)S(1)}, bf16[16,2048]{1,0:T(8,128)(2,1)S(1)}, u32[]{:S(2)}, u32[]{:S(2)}) collective-permute-start(bf16[16,2048]{1,0:T(8,128)(2,1)S(1)} %get-tuple-element.42), channel_id=1, source_target_pairs={{0,5},{1,4},{2,1},{3,0},{6,3},{7,2},{4,7},{5,6},{8,13},{9,12},{10,... | collective-permute-start | bytes 196616 | tf_op jit(solution)/shard_map/ppermute | solution.py:264
  7.7 5.8 %collective-permute-start.3 = (bf16[16,2048]{1,0:T(8,128)(2,1)S(1)}, bf16[16,2048]{1,0:T(8,128)(2,1)S(1)}, u32[]{:S(2)}, u32[]{:S(2)}) collective-permute-start(bf16[16,2048]{1,0:T(8,128)(2,1)S(1)} %get-tuple-element.40), channel_id=1, source_target_pairs={{0,3},{1,2},{2,7},{3,6},{6,5},{7,4},{4,1},{5,0},{8,11},{9,10},{10,... | collective-permute-start | bytes 196616 | tf_op jit(solution)/shard_map/ppermute | solution.py:264
  15.6 4.1 %collective-permute-start.6 = (bf16[32,2560]{1,0:T(8,128)(2,1)S(1)}, bf16[32,2560]{1,0:T(8,128)(2,1)S(1)}, u32[]{:S(2)}, u32[]{:S(2)}) collective-permute-start(bf16[32,2560]{1,0:T(8,128)(2,1)S(1)} %get-tuple-element.52), channel_id=1, source_target_pairs={{0,1},{1,0},{2,3},{3,2},{4,5},{5,4},{6,7},{7,6},{8,9},{9,8},{10,11... | collective-permute-start | bytes 491528 | tf_op jit(solution)/shard_map/ppermute | solution.py:205
  15.8 6.7 %collective-permute-start.7 = (bf16[8,2048]{1,0:T(8,128)(2,1)S(1)}, bf16[8,2048]{1,0:T(8,128)(2,1)S(1)}, u32[]{:S(2)}, u32[]{:S(2)}) collective-permute-start(bf16[8,2048]{1,0:T(8,128)(2,1)S(1)} %get-tuple-element.54), channel_id=1, source_target_pairs={{0,5},{1,4},{2,1},{3,0},{6,3},{7,2},{4,7},{5,6},{8,13},{9,12},{10,... | collective-permute-start | bytes 98312 | tf_op jit(solution)/shard_map/ppermute | solution.py:264
  16.6 5.9 %collective-permute-start.8 = (bf16[8,2048]{1,0:T(8,128)(2,1)S(1)}, bf16[8,2048]{1,0:T(8,128)(2,1)S(1)}, u32[]{:S(2)}, u32[]{:S(2)}) collective-permute-start(bf16[8,2048]{1,0:T(8,128)(2,1)S(1)} %get-tuple-element.55), channel_id=1, source_target_pairs={{0,7},{1,6},{2,5},{3,4},{6,1},{7,0},{4,3},{5,2},{8,15},{9,14},{10,... | collective-permute-start | bytes 98312 | tf_op jit(solution)/shard_map/ppermute | solution.py:264
  18.9 4.3 %collective-permute-start.9 = (bf16[8,2048]{1,0:T(8,128)(2,1)S(1)}, bf16[8,2048]{1,0:T(8,128)(2,1)S(1)}, u32[]{:S(2)}, u32[]{:S(2)}) collective-permute-start(bf16[8,2048]{1,0:T(8,128)(2,1)S(1)} %get-tuple-element.56), channel_id=1, source_target_pairs={{0,3},{1,2},{2,7},{3,6},{6,5},{7,4},{4,1},{5,0},{8,11},{9,10},{10,... | collective-permute-start | bytes 98312 | tf_op jit(solution)/shard_map/ppermute | solution.py:264
